TPU v7x, 512 devices: a whole 4x4x16 slice. The times are simulated.
512 devices in a mesh: fsdp: 32 (over z, core), tensor: 16 (over y, x).
Axes of the slice: x: 4, y: 4, z: 16, core: 2. Of those that a mesh axis runs over, the one named last changes fastest.
Arguments:
- gradient: bfloat16 [4, 1024, 8192], P(None, 'tensor', 'fsdp'), may hold values from -6 to 6
- block_owner: int32 [4, 8], replicated, may hold values from 0 to 31, as said below
- left_stats: float32 [96, 1024, 1024], P('fsdp', 'tensor'), may hold values from -6 to 6
- right_stats: float32 [96, 1024, 1024], P('fsdp', 'tensor'), may hold values from -6 to 6
- left_root: bfloat16 [96, 1024, 1024], P('fsdp', 'tensor'), may hold values from -120 to 120, as said below
- right_root: bfloat16 [96, 1024, 1024], P('fsdp', 'tensor'), may hold values from -120 to 120, as said below
Outputs:
- left_updated: float32 [96, 1024, 1024], P('fsdp', 'tensor')
- right_updated: float32 [96, 1024, 1024], P('fsdp', 'tensor')
- update: bfloat16 [4, 1024, 8192], P(None, 'tensor', 'fsdp')
Inputs may be any that keep to these rules, and one draw needn't show every extreme that they name: `block_owner`: each owner holds at most 3 blocks and never two with the same row block k; some owner holds exactly 3. `left_root`: each matrix is symmetric. `right_root`: each matrix is symmetric.
All inputs are finite; a program needn't handle non-finite values.
Results may differ from a plain program's by a relative error of at most 0.0049.
Values may be sent and summed in bfloat16 or wider, within the bound.
No kernel may reach another device: no remote copies, remote signals or barrier semaphores. Data moves between devices by JAX's collectives and lax.ppermute only.
A program may use at most 64 MiB of HBM per device.

v0:
```python
import jax
import jax.numpy as jnp
from jax import lax
from jax.sharding import PartitionSpec as P

BETA = 0.999
STEP = 0.5
EPS = 1e-06


def slot_numbers(owners_flat):
    total = owners_flat.shape[0]
    same = owners_flat[:, None] == owners_flat[None, :]
    earlier = jnp.arange(total)[None, :] < jnp.arange(total)[:, None]
    return jnp.sum(jnp.where(same & earlier, 1, 0), axis=1).astype(jnp.int32)


def gram_fold(local_rows, left_factor, tensor_index, local_height):

    def fold(carry, piece, start):
        own_columns = lax.dynamic_slice_in_dim(piece, tensor_index * local_height, local_height, 2)
        right_term = jnp.einsum(
            "sji,sjk->sik", own_columns, piece, preferred_element_type=jnp.float32
        )
        across = jnp.einsum("sjk,snk->sjn", local_rows, piece, preferred_element_type=jnp.float32)
        left_mixed = jnp.einsum(
            "sjn,snk->sjk", left_factor, piece, preferred_element_type=jnp.float32
        )
        grad_power = jnp.einsum("sjk,sjk->s", piece, piece, preferred_element_type=jnp.float32)
        return (across, right_term, left_mixed, grad_power)

    return fold


def root_fold(mixed, piece):
    return jnp.einsum("sjn,snk->sjk", mixed, piece, preferred_element_type=jnp.float32)


def per_device(gradient, block_owner, left_stats, right_stats, left_root, right_root):
    tensor_index = lax.axis_index("tensor")
    fsdp_index = lax.axis_index("fsdp")
    fsdp_count = lax.axis_size("fsdp")
    col_blocks, local_height, row_depth = gradient.shape
    row_blocks = block_owner.shape[1]
    capacity, _, block_side = left_stats.shape
    row_parts = block_side // row_depth
    band_index = fsdp_index // row_parts
    band_mask = jnp.arange(row_blocks) == band_index
    band_owner = jnp.sum(jnp.where(band_mask[None, :], block_owner, 0), axis=1)
    targets = (band_owner[:, None] == jnp.arange(fsdp_count)[None, :]).astype(jnp.bfloat16)
    owners_flat = block_owner.reshape(-1)
    slot_of = slot_numbers(owners_flat)
    held_slots = (
        (owners_flat[:, None] == fsdp_index) & (slot_of[:, None] == jnp.arange(capacity)[None, :])
    ).astype(jnp.float32)
    block_band = jnp.arange(owners_flat.shape[0]) % row_blocks
    sources = block_band[:, None] * row_parts + jnp.arange(row_parts)[None, :]
    from_source = (sources[:, :, None] == jnp.arange(fsdp_count)[None, None, :]).astype(jnp.float32)
    selector = jnp.einsum("bs,brf->srf", held_slots, from_source).astype(jnp.bfloat16)
    block_column = jnp.arange(owners_flat.shape[0]) // row_blocks
    slot_band = jnp.einsum("bs,b->s", held_slots, block_band.astype(jnp.float32)).astype(jnp.int32)
    column_hits = (block_column[:, None] == jnp.arange(col_blocks)[None, :]).astype(jnp.float32)
    picks = jnp.einsum("bs,bc->sc", held_slots, column_hits).astype(jnp.bfloat16)
    chosen = jnp.einsum(
        "sc,cjn->sjn",
        picks,
        lax.all_gather(gradient, "fsdp", axis=2, tiled=True),
        preferred_element_type=jnp.float32,
    ).astype(jnp.bfloat16)
    local_rows = jnp.stack(
        [
            lax.dynamic_slice_in_dim(chosen[number], slot_band[number] * block_side, block_side, 1)
            for number in range(capacity)
        ],
        axis=0,
    )
    results = []
    for slot_number in range(capacity):
        slot_rows = local_rows[slot_number : slot_number + 1]
        blank = jnp.zeros((1, local_height, block_side), jnp.float32)
        fold = gram_fold(
            slot_rows, left_root[slot_number : slot_number + 1], tensor_index, local_height
        )
        results.append(
            fold(
                (blank, blank, blank, jnp.zeros((1,), jnp.float32)),
                lax.all_gather(slot_rows, "tensor", axis=1, tiled=True),
                jnp.int32(0),
            )
        )
    left_term = jnp.concatenate([item[0] for item in results], axis=0)
    right_term = jnp.concatenate([item[1] for item in results], axis=0)
    left_mixed = jnp.concatenate([item[2] for item in results], axis=0)
    grad_power = jnp.concatenate([item[3] for item in results], axis=0)
    mixed = left_mixed.astype(jnp.bfloat16)
    product = root_fold(mixed, lax.all_gather(right_root, "tensor", axis=1, tiled=True))
    local_power = jnp.sum(product * product, axis=(1, 2))
    power = lax.psum(local_power, "tensor")
    graft_scale = -STEP * jnp.sqrt(grad_power) * lax.rsqrt(power + EPS)
    step_rows = (graft_scale[:, None, None] * product).astype(jnp.bfloat16)
    left_updated = BETA * left_stats + (1.0 - BETA) * left_term
    right_updated = BETA * right_stats + (1.0 - BETA) * right_term
    leaving = jnp.einsum(
        "srf,sjri->fji",
        selector,
        step_rows.reshape(capacity, local_height, row_parts, row_depth),
        preferred_element_type=jnp.float32,
    ).astype(jnp.bfloat16)
    returned = lax.all_to_all(leaving, "fsdp", split_axis=0, concat_axis=0, tiled=True)
    update = jnp.einsum(
        "cg,gji->cji", targets, returned, preferred_element_type=jnp.float32
    ).astype(jnp.bfloat16)
    return (left_updated, right_updated, update)


def solution(mesh):
    placed = (
        P(None, "tensor", "fsdp"),
        P(),
        P("fsdp", "tensor", None),
        P("fsdp", "tensor", None),
        P("fsdp", "tensor", None),
        P("fsdp", "tensor", None),
    )
    return jax.shard_map(
        per_device,
        mesh=mesh,
        in_specs=placed,
        out_specs=(P("fsdp", "tensor", None), P("fsdp", "tensor", None), P(None, "tensor", "fsdp")),
        check_vma=False,
    )
```

profile of v0, /device:TPU:1, one launch (start us, length us, event | category | flops | bytes accessed | tf_op | source)
XLA Modules:
  0.0 509.7 jit_solution(7079396397033412903)
XLA Ops:
  7.2 0.0 all-gather.6.cloned.1.call-start
  7.2 1.7 copy.28
  8.9 0.0 all-gather.6.cloned.1.call-update
  8.9 0.0 all-gather.10.cloned.1.call-start
  9.0 0.8 broadcast_in_dim_reshape.2
  9.7 0.2 select_reduce_fusion
  9.9 0.1 fusion.59
  10.0 0.6 fusion.110
  11.3 85.1 %all-gather.6.cloned.1.call-done = bf16[4,64,8192]{2,0,1:T(4,128)(2,1)} async-done(((bf16[4,64,256]{2,0,1:T(4,128)(2,1)}), bf16[4,64,8192]{2,0,1:T(4,128)(2,1)}) %all-gather.6.cloned.1.call-update) | async-done | bytes 4194320 | tf_op jit(solution)/shard_map/all_gather | solution.py:67
  96.4 6.7 %convolution_convert_fusion = bf16[3,64,8192]{2,0,1:T(4,128)(2,1)} fusion(bf16[4,64,8192]{2,0,1:T(4,128)(2,1)} %all-gather.6.cloned.1.call-done, s32[32]{0:T(128)S(1)} %and_select_fusion.1, s32[32]{0:T(128)S(1)} %select_reduce_fusion, pred[32]{0:T(512)(128)(4,1)S(1)} %broadcast_compare_fusion), kind=kOutput, calls=%fused_computation | convolution fusion | flops 14156876 | bytes 7340320 | tf_op jit(solution)/shard_map/sc,cjn->sjn/dot_general | solution.py:64
  103.1 11.4 %fusion.109 = (bf16[1,64,8192]{2,0,1:T(2,128)(2,1)}, bf16[1,64,8192]{2,0,1:T(2,128)(2,1)S(1)}, bf16[1,64,8192]{2,0,1:T(2,128)(2,1)S(1)}) fusion(bf16[3,64,8192]{2,0,1:T(4,128)(2,1)} %convolution_convert_fusion), kind=kLoop, calls=%fused_computation.110 | loop fusion | bytes 6291456 | tf_op jit(solution)/shard_map/slice | solution.py:72
  114.5 0.3 constant_dynamic-slice_fusion.1
  114.8 0.7 copy.53
  115.5 0.0 all-gather.10.cloned.1.call-update
  115.5 0.0 all-gather.8.cloned.1.call-start
  116.2 1.2 constant_dynamic-slice_fusion.2
  117.4 0.7 copy.52
  118.1 0.0 all-gather.8.cloned.1.call-update
  118.2 0.0 all-gather.12.cloned.1.call-start
  118.8 0.3 constant_dynamic-slice_fusion
  119.0 0.7 copy.54
  119.7 0.0 all-gather.12.cloned.1.call-update
  119.8 0.0 all-gather.14.cloned.1.call-start
  119.8 0.5 all-gather.14.cloned.1.call-update
  120.4 50.7 %all-gather.10.cloned.1.call-done = bf16[1,1024,1024]{2,1,0:T(8,128)(2,1)} async-done(((bf16[1,64,1024]{2,1,0:T(8,128)(2,1)}), bf16[1,1024,1024]{2,1,0:T(8,128)(2,1)}) %all-gather.10.cloned.1.call-update) | async-done | bytes 2097168 | tf_op jit(solution)/shard_map/all_gather | solution.py:87
  171.1 0.0 copy-done.9
  171.1 2.1 fusion.51
  173.2 60.7 %all-gather.8.cloned.1.call-done = bf16[1,1024,1024]{2,1,0:T(8,128)(2,1)} async-done(((bf16[1,64,1024]{2,1,0:T(8,128)(2,1)}), bf16[1,1024,1024]{2,1,0:T(8,128)(2,1)}) %all-gather.8.cloned.1.call-update) | async-done | bytes 2097168 | tf_op jit(solution)/shard_map/all_gather | solution.py:87
  233.9 2.1 fusion.54
  236.0 61.1 %all-gather.12.cloned.1.call-done = bf16[1,1024,1024]{2,1,0:T(8,128)(2,1)} async-done(((bf16[1,64,1024]{2,1,0:T(8,128)(2,1)}), bf16[1,1024,1024]{2,1,0:T(8,128)(2,1)}) %all-gather.12.cloned.1.call-update) | async-done | bytes 2097168 | tf_op jit(solution)/shard_map/all_gather | solution.py:87
  297.1 2.1 fusion.48
  299.1 77.8 %all-gather.14.cloned.1.call-done = bf16[3,1024,1024]{2,1,0:T(8,128)(2,1)} async-done(((bf16[3,64,1024]{2,1,0:T(8,128)(2,1)}), bf16[3,1024,1024]{2,1,0:T(8,128)(2,1)}) %all-gather.14.cloned.1.call-update) | async-done | bytes 6291472 | tf_op jit(solution)/shard_map/all_gather | solution.py:96
  376.9 4.1 multiply_reduce_fusion
  381.0 31.3 %psum.7 = f32[3]{0:T(128)S(1)} all-reduce(f32[3]{0:T(128)S(1)} %get-tuple-element.21), channel_id=1, replica_groups=mesh['fsdp'=32,'tensor'=16] {'tensor'}, use_global_device_ids=true, to_apply=%region_3.4 | all-reduce | flops 3 | bytes 24 | tf_op jit(solution)/shard_map/psum | solution.py:98
  412.3 3.5 fusion.2
  415.8 0.0 copy-done
  415.8 1.7 fusion.1
  417.5 0.0 copy-done.2
  417.5 1.7 fusion
  419.2 1.9 fusion.100
  421.1 0.1 multiply_convert_fusion
  421.2 1.0 reshape.156
  422.3 1.9 bitcast_convert_fusion
  424.1 0.0 copy-start.10
  424.1 1.6 copy.36
  425.8 20.2 %all-to-all-start = ((bf16[32,64,256]{2,1,0:T(8,128)(2,1)}), bf16[32,64,256]{2,1,0:T(8,128)(2,1)S(1)}, u32[]{:S(2)}, u32[]{:S(2)}) async-start(bf16[32,64,256]{2,1,0:T(8,128)(2,1)} %copy.36), calls=%async_computation | async-start | bytes 2097152 | tf_op jit(solution)/shard_map/all_to_all | solution.py:109
  446.1 0.0 copy-done.10
  446.1 0.1 select_reduce_fusion.1
  446.2 2.5 fusion.21
  448.7 0.6 fusion.24
  449.3 0.0 copy-start.4
  449.4 0.6 fusion.27
  450.0 0.3 copy-done.1
  450.3 0.8 fusion.30
  451.0 0.0 copy-start.7
  451.0 0.0 copy-start.8
  451.1 0.8 fusion.33
  451.8 0.8 fusion.36
  452.6 0.0 copy-done.7
  452.6 0.0 copy-done.8
  452.6 1.5 fusion.61
  454.1 47.7 %all-to-all-done = bf16[32,64,256]{2,1,0:T(8,128)(2,1)S(1)} async-done(((bf16[32,64,256]{2,1,0:T(8,128)(2,1)}), bf16[32,64,256]{2,1,0:T(8,128)(2,1)S(1)}, u32[]{:S(2)}, u32[]{:S(2)}) %all-to-all-start) | async-done | bytes 1048608 | tf_op jit(solution)/shard_map/all_to_all | solution.py:109
  501.8 0.7 convolution_convert_fusion.1
  502.4 0.7 copy.38
  (16 shorter events, 0.0 us)
Async XLA Ops:
  7.2 89.3 %all-gather.6.cloned.1.call-start = ((), (), s32[]{:S(2)}) async-start(), calls=%async_computation.1 | async-start | bytes 4325376 | tf_op jit(solution)/shard_map/all_gather | solution.py:67
  8.9 162.2 %all-gather.10.cloned.1.call-start = ((), (), s32[]{:S(2)}) async-start(), calls=%async_computation.3 | async-start | bytes 2228224 | tf_op jit(solution)/shard_map/all_gather | solution.py:87
  114.5 56.6 %copy-start.9 = (bf16[3,64,1024]{2,1,0:T(8,128)(2,1)S(1)}, bf16[3,64,1024]{2,1,0:T(8,128)(2,1)}, u32[]{:S(2)}) copy-start(bf16[3,64,1024]{2,1,0:T(8,128)(2,1)} %param.10) | copy-start | bytes 1179652
  115.5 118.4 %all-gather.8.cloned.1.call-start = ((), (), s32[]{:S(2)}) async-start(), calls=%async_computation.2 | async-start | bytes 2228224 | tf_op jit(solution)/shard_map/all_gather | solution.py:87
  118.2 178.9 %all-gather.12.cloned.1.call-start = ((), (), s32[]{:S(2)}) async-start(), calls=%async_computation.4 | async-start | bytes 2228224 | tf_op jit(solution)/shard_map/all_gather | solution.py:87
  119.8 257.2 %all-gather.14.cloned.1.call-start = ((), (), s32[]{:S(2)}) async-start(), calls=%async_computation.5 | async-start | bytes 6684672 | tf_op jit(solution)/shard_map/all_gather | solution.py:96
  381.0 34.8 %copy-start = (bf16[1,1024,1024]{2,1,0:T(8,128)(2,1)S(1)}, bf16[1,1024,1024]{2,1,0:T(8,128)(2,1)}, u32[]{:S(2)}) copy-start(bf16[1,1024,1024]{2,1,0:T(8,128)(2,1)} %all-gather.10.cloned.1.call-done) | copy-start | bytes 6291460
  412.3 5.2 %copy-start.2 = (bf16[1,1024,1024]{2,1,0:T(8,128)(2,1)S(1)}, bf16[1,1024,1024]{2,1,0:T(8,128)(2,1)}, u32[]{:S(2)}) copy-start(bf16[1,1024,1024]{2,1,0:T(8,128)(2,1)} %all-gather.12.cloned.1.call-done) | copy-start | bytes 6291460
  424.1 21.9 %copy-start.10 = (s32[4,8]{1,0:T(4,128)S(1)}, s32[4,8]{1,0:T(4,128)}, u32[]{:S(2)}) copy-start(s32[4,8]{1,0:T(4,128)} %param.7) | copy-start | bytes 388
  425.8 76.0 %all-to-all-start = ((bf16[32,64,256]{2,1,0:T(8,128)(2,1)}), bf16[32,64,256]{2,1,0:T(8,128)(2,1)S(1)}, u32[]{:S(2)}, u32[]{:S(2)}) async-start(bf16[32,64,256]{2,1,0:T(8,128)(2,1)} %copy.36), calls=%async_computation | async-start | bytes 2097152 | tf_op jit(solution)/shard_map/all_to_all | solution.py:109
  446.2 3.1 copy-start.3
  448.7 1.6 copy-start.1
  448.7 1.6 copy-start.5
  449.3 1.7 copy-start.4
  450.3 1.6 copy-start.6
  451.0 1.6 copy-start.7
  451.0 1.5 copy-start.8
Sparse Core Ops, SparseCore 0:
  10.6 85.7 all-gather.5
  115.6 55.4 all-gather.9
  174.1 59.6 all-gather.7
  237.3 59.6 all-gather.11
  299.9 76.9 all-gather.13
where the time goes:
time: 510 us
  waiting for transfers between devices  384 us (75%)
  blocking collectives  31.3 us (6%)
  matrix products  25.6 us (5%)
  local copies, waits for them, and re-layouts  22 us (4%)
  starting transfers between devices  20.5 us (4%)
  between operations  15.9 us (3%)
  other arithmetic  10.7 us (2%)
    all_gather x3, waiting for transfers between devices, per_device(): lax.all_gather(slot_rows, 'tensor', axis=1, tiled=True)  173 us
    all_gather x1, waiting for transfers between devices, per_device(): lax.all_gather(gradient, 'fsdp', axis=2, tiled=True)  85.1 us
    all_gather x1, waiting for transfers between devices, per_device(): lax.all_gather(right_root, 'tensor', axis=1, tiled=True)  77.8 us
    all_to_all x1, waiting for transfers between devices, per_device(): lax.all_to_all(leaving, 'fsdp', split_axis=0, concat_axis=0, tiled=True)  47.7 us
    psum x1, blocking collectives, per_device(): power = lax.psum(local_power, 'tensor')  31.3 us
    all_to_all x1, starting transfers between devices, per_device(): lax.all_to_all(leaving, 'fsdp', split_axis=0, concat_axis=0, tiled=True)  20.2 us
    slice x1, local copies, waits for them, and re-layouts, per_device(): chosen[number]  11.4 us
  transfers between devices with their start and end apart: 6, of which 6 were waited for; matrix products, arithmetic and copies ran while one was open for 4% of the time, Pallas kernels for 0%

commit v1 on v0

v1 whole, which is shorter than its diff:
```python
import functools
import jax
import jax.numpy as jnp
from jax import lax
from jax.experimental import pallas as pl
from jax.experimental.pallas import tpu as pltpu
from jax.sharding import PartitionSpec as P

BETA = 0.999
STEP = 0.5
EPS = 1e-06
TAIL = 16
VMEM = pl.BlockSpec(memory_space=pltpu.VMEM)
SMEM = pl.BlockSpec(memory_space=pltpu.SMEM)
LIMIT = pltpu.CompilerParams(vmem_limit_bytes=24 * 2**20)


def cost(flops, moved):
    return pl.CostEstimate(flops=flops, bytes_accessed=moved, transcendentals=0)


def slot_numbers(owners_flat):
    total = owners_flat.shape[0]
    same = owners_flat[:, None] == owners_flat[None, :]
    earlier = jnp.arange(total)[None, :] < jnp.arange(total)[:, None]
    return jnp.sum(jnp.where(same & earlier, 1, 0), axis=1).astype(jnp.int32)


def exchange(pieces):
    return lax.all_to_all(pieces, "tensor", split_axis=0, concat_axis=0, tiled=True)


def outgoing_kernel(owner_ref, gradient_ref, out_ref):
    out_ref[...] = jnp.zeros(out_ref.shape, out_ref.dtype)
    for column in range(gradient_ref.shape[0]):
        out_ref[owner_ref[column]] = gradient_ref[column]


def held_rows_kernel(band_ref, used_ref, pieces_ref, sent_ref, rows_ref, sems):
    capacity, _, block_side = rows_ref.shape
    width = pieces_ref.shape[2]
    parts = block_side // width
    copies = []
    for slot in range(capacity + 1):
        if slot < capacity:
            keep = used_ref[slot] > 0
            for part in range(parts):
                piece = pieces_ref[band_ref[slot] * parts + part]
                rows_ref[slot, :, pl.ds(part * width, width)] = jnp.where(
                    keep, piece, jnp.zeros_like(piece)
                )
        for member in range(parts):
            place = slot * parts + member
            if place < sent_ref.shape[0]:
                source = rows_ref.at[min(slot, capacity - 1)]
                copies.append(pltpu.make_async_copy(source, sent_ref.at[place], sems.at[place]))
                copies[-1].start()
    for copy in copies:
        copy.wait()


def held_rows(band_of, used, pieces, capacity, block_side, places):
    height = pieces.shape[1]
    return pl.pallas_call(
        held_rows_kernel,
        out_shape=jax.ShapeDtypeStruct((places, height, block_side), pieces.dtype),
        in_specs=[SMEM, SMEM, VMEM],
        out_specs=pl.BlockSpec(memory_space=pl.ANY),
        scratch_shapes=[
            pltpu.VMEM((capacity, height, block_side), pieces.dtype),
            pltpu.SemaphoreType.DMA((places,)),
        ],
        compiler_params=LIMIT,
        cost_estimate=cost(0, 4 * 2**20),
    )(band_of, used, pieces)


def three_parts(value):
    high = value.astype(jnp.bfloat16)
    rest = value - high.astype(jnp.float32)
    middle = rest.astype(jnp.bfloat16)
    return [high, middle, (rest - middle.astype(jnp.float32)).astype(jnp.bfloat16)]


def around(place, step, count):
    return lax.rem(place + count - step, count)


def precondition_kernel(side, place_ref, *refs):
    left_refs, (right_ref, block_ref, out_ref) = refs[:side], refs[side:]
    y, x = place_ref[0], place_ref[1]
    places, height, block_side = block_ref.shape
    width = out_ref.shape[2]
    block = block_ref[...].reshape(block_side, block_side)
    right = jnp.concatenate([right_ref[around(y, at, side)] for at in range(side)], axis=0)
    power = jnp.zeros((1, width), jnp.float32)
    for step in range(side):
        left = left_refs[step][...].reshape(side * height, block_side)
        mixed = jnp.dot(left, block, preferred_element_type=jnp.float32).astype(jnp.bfloat16)
        product = lax.dot_general(
            mixed, right, (((1,), (1,)), ((), ())), preferred_element_type=jnp.float32
        )
        power += jnp.sum(product * product, axis=0, keepdims=True)
        product = product.astype(jnp.bfloat16)
        for at in range(side):
            place = around(y, at, side) * side + around(x, step, side)
            out_ref[place, pl.ds(0, height), :] = product[at * height : (at + 1) * height]
    share = places // side
    own = block_ref[pl.ds(x * share, share)].astype(jnp.float32).reshape(width, block_side)
    own = jnp.sum(own * own, axis=0, keepdims=True)
    grad = sum(own[:, at * width : (at + 1) * width] for at in range(side))
    number = lax.broadcasted_iota(jnp.int32, (TAIL, width), 0)
    tail = jnp.zeros((TAIL, width), jnp.float32)
    for at, line in enumerate(three_parts(power) + three_parts(grad)):
        tail = jnp.where(number == at, line.astype(jnp.float32), tail)
    tail = tail.astype(jnp.bfloat16)
    for place in range(places):
        out_ref[place, pl.ds(height, TAIL), :] = tail


def precondition(place, lefts, right, block):
    places, height, block_side = block.shape
    width = block_side // len(lefts)
    return pl.pallas_call(
        functools.partial(precondition_kernel, len(lefts)),
        out_shape=jax.ShapeDtypeStruct((places, height + TAIL, width), jnp.bfloat16),
        in_specs=[SMEM] + [VMEM] * (len(lefts) + 2),
        out_specs=VMEM,
        compiler_params=pltpu.CompilerParams(vmem_limit_bytes=32 * 2**20),
        cost_estimate=cost(2 * block_side * block_side * (block_side + width), 6 * 2**20),
    )(place, *lefts, right, block)


def steps_kernel(side, band_ref, used_ref, back_ref, out_ref):
    height, width = out_ref.shape[1:]
    piece = width // side
    out_ref[...] = jnp.zeros(out_ref.shape, out_ref.dtype)
    for slot in range(band_ref.shape[0]):
        sums = sum(
            back_ref[slot * side + member, pl.ds(height, TAIL), :].astype(jnp.float32)
            for member in range(side)
        )
        sums = jnp.sum(sums, axis=1, keepdims=True)
        power = jnp.sum(sums[0:3], axis=0, keepdims=True)
        grad = jnp.sum(sums[3:6], axis=0, keepdims=True)
        scale = -STEP * jnp.sqrt(grad) * lax.rsqrt(power + EPS)

        @pl.when(used_ref[slot] > 0)
        def _():
            parts = [
                (
                    scale * back_ref[slot * side + member, pl.ds(0, height), :].astype(jnp.float32)
                ).astype(jnp.bfloat16)
                for member in range(side)
            ]
            for part in range(side):
                out_ref[band_ref[slot] * side + part] = jnp.concatenate(
                    [rows[:, part * piece : (part + 1) * piece] for rows in parts], axis=1
                )


def update_kernel(owner_ref, returned_ref, out_ref):
    for column in range(out_ref.shape[0]):
        out_ref[column] = returned_ref[owner_ref[column]]


def statistics_kernel(side, place_ref, left_ref, right_ref, *refs):
    term_refs, outs = refs[:side], refs[side:]
    y, x = place_ref[0], place_ref[1]
    width = left_ref.shape[2] // side
    for step in range(side):
        columns = pl.ds(pl.multiple_of(around(x, step, side) * width, width), width)
        for slot in range(left_ref.shape[0]):
            for kind, (old, new) in enumerate(zip((left_ref, right_ref), outs)):
                term = term_refs[step][around(y, slot, side), kind].astype(jnp.float32)
                new[slot, :, columns] = BETA * old[slot, :, columns] + (1.0 - BETA) * term


def per_device(gradient, block_owner, left_stats, right_stats, left_root, right_root):
    tensor_index = lax.axis_index("tensor")
    fsdp_index = lax.axis_index("fsdp")
    fsdp_count = lax.axis_size("fsdp")
    tensor_count = lax.axis_size("tensor")
    col_blocks, local_height, row_depth = gradient.shape
    row_blocks = block_owner.shape[1]
    capacity, _, block_side = left_stats.shape
    side = block_side // row_depth
    y, x = tensor_index // side, tensor_index % side
    place = jnp.stack([y, x]).astype(jnp.int32)

    def along_y(value, step, sources, targets):
        pairs = [
            (a * side + b, (a + step) % side * side + b)
            for a in range(side)
            for b in range(side)
            if a < sources and (a + step) % side < targets
        ]
        return lax.ppermute(value, "tensor", pairs)

    def along_x(value, step, rows):
        pairs = [
            (a * side + b, a * side + (b + step) % side) for a in range(rows) for b in range(side)
        ]
        return lax.ppermute(value, "tensor", pairs)

    with jax.named_scope("gradient_to_owners"):
        band_mask = jnp.arange(row_blocks) == fsdp_index // side
        band_owner = jnp.sum(jnp.where(band_mask[None, :], block_owner, 0), axis=1)
        band_owner = band_owner.astype(jnp.int32)
        outgoing = pl.pallas_call(
            outgoing_kernel,
            out_shape=jax.ShapeDtypeStruct((fsdp_count, local_height, row_depth), gradient.dtype),
            in_specs=[SMEM, VMEM],
            out_specs=VMEM,
            compiler_params=LIMIT,
            cost_estimate=cost(0, 2**20),
        )(band_owner, gradient)
        outgoing, left_root, right_root = lax.optimization_barrier(
            (outgoing, left_root, right_root)
        )
        pieces = lax.all_to_all(outgoing, "fsdp", split_axis=0, concat_axis=0, tiled=True)

    with jax.named_scope("roots_to_slot_groups"):
        roots = jnp.stack([left_root, right_root], axis=1)
        taken = []
        for step in range(side):
            slot = jnp.minimum((y + step) % side, capacity - 1)
            own = lax.dynamic_index_in_dim(roots, slot, 0, keepdims=False)
            taken.append(along_y(own, step, side, capacity) if step else own)
        left_rows = jnp.stack([piece[0] for piece in taken])
        right_rows = jnp.stack([piece[1] for piece in taken])
        lefts = [left_rows] + [along_x(left_rows, step, capacity) for step in range(1, side)]
        pieces, right_rows, *lefts = lax.optimization_barrier((pieces, right_rows, *lefts))

    with jax.named_scope("held_blocks"):
        owners_flat = block_owner.reshape(-1)
        numbers = jnp.arange(owners_flat.shape[0])
        held = (owners_flat == fsdp_index)[:, None] & (
            slot_numbers(owners_flat)[:, None] == jnp.arange(capacity)[None, :]
        )
        used = jnp.any(held, axis=0).astype(jnp.int32)
        band_of = jnp.sum(jnp.where(held, (numbers % row_blocks)[:, None], 0), axis=0)
        band_of = band_of.astype(jnp.int32)

    with jax.named_scope("rows_of_held_blocks"):
        block = exchange(held_rows(band_of, used, pieces, capacity, block_side, tensor_count))

    with jax.named_scope("precondition"):
        leaving = precondition(place, lefts, right_rows, block)

    with jax.named_scope("step_to_gradient_rows"):
        back = exchange(leaving)
        steps = pl.pallas_call(
            functools.partial(steps_kernel, side),
            out_shape=jax.ShapeDtypeStruct((fsdp_count, local_height, row_depth), jnp.bfloat16),
            in_specs=[SMEM, SMEM, VMEM],
            out_specs=VMEM,
            compiler_params=LIMIT,
            cost_estimate=cost(0, 2 * 2**20),
        )(band_of, used, back)
        returned = lax.all_to_all(steps, "fsdp", split_axis=0, concat_axis=0, tiled=True)

    with jax.named_scope("statistics"):
        block, steps = lax.optimization_barrier((block, steps))
        block = block.reshape(block_side, block_side)
        chunk_rows = lax.dynamic_slice_in_dim(block, x * row_depth, row_depth, 0)
        chunk_columns = lax.dynamic_slice_in_dim(block, x * row_depth, row_depth, 1)
        left_term = jnp.einsum("jk,ck->jc", block, chunk_rows, preferred_element_type=jnp.float32)
        right_term = jnp.einsum(
            "jk,jc->kc", block, chunk_columns, preferred_element_type=jnp.float32
        )
        terms = jnp.stack([left_term.astype(jnp.bfloat16), right_term.astype(jnp.bfloat16)])
        terms = terms.reshape(2, side, block_side // side, row_depth)
        gathered = []
        for step in range(side):
            own = lax.dynamic_index_in_dim(terms, (y + step) % side, 1, keepdims=False)
            gathered.append(along_y(own, step, capacity, side) if step else own)
        gathered = jnp.stack(gathered).reshape(side, 2, side, local_height, row_depth)
        arrived = []
        for step in range(side):
            own = lax.dynamic_index_in_dim(gathered, (x + step) % side, 2, keepdims=False)
            arrived.append(along_x(own, step, side) if step else own)
        left_updated, right_updated = pl.pallas_call(
            functools.partial(statistics_kernel, side),
            out_shape=(
                jax.ShapeDtypeStruct(left_stats.shape, left_stats.dtype),
                jax.ShapeDtypeStruct(right_stats.shape, right_stats.dtype),
            ),
            in_specs=[SMEM] + [VMEM] * (2 + side),
            out_specs=(VMEM, VMEM),
            compiler_params=LIMIT,
            cost_estimate=cost(0, 4 * 2**20),
        )(place, left_stats, right_stats, *arrived)
        returned, left_updated, right_updated = lax.optimization_barrier(
            (returned, left_updated, right_updated)
        )

    with jax.named_scope("update"):
        update = pl.pallas_call(
            update_kernel,
            out_shape=jax.ShapeDtypeStruct(gradient.shape, gradient.dtype),
            in_specs=[SMEM, VMEM],
            out_specs=VMEM,
            compiler_params=LIMIT,
            cost_estimate=cost(0, 2**20),
        )(band_owner, returned)
    return (left_updated, right_updated, update)


def solution(mesh):
    placed = (
        P(None, "tensor", "fsdp"),
        P(),
        P("fsdp", "tensor", None),
        P("fsdp", "tensor", None),
        P("fsdp", "tensor", None),
        P("fsdp", "tensor", None),
    )
    return jax.shard_map(
        per_device,
        mesh=mesh,
        in_specs=placed,
        out_specs=(P("fsdp", "tensor", None), P("fsdp", "tensor", None), P(None, "tensor", "fsdp")),
        check_vma=False,
    )
```

time: 510 us -> 206 us (0.40)
  waiting for transfers between devices: 384 us -> 101 us
  starting transfers between devices: 20.5 us -> 67.4 us
  matrix products: 25.6 us -> 1.55 us
  local copies, waits for them, and re-layouts: 22 us -> 4.31 us
  blocking collectives: 31.3 us -> 14.8 us
  between operations: 15.9 us -> 1.19 us
  Pallas kernels: 0 us -> 12.2 us
  other arithmetic: 10.7 us -> 2.6 us
    all_gather x5 -> x0, waiting for transfers between devices: 335 us -> none  [the longest x3 173 us: per_device(): lax.all_gather(slot_rows, 'tensor', axis=1, tiled=True)]
    ppermute x0 -> x12, waiting for transfers between devices: none -> 46.1 us  [the longest x6 26.6 us: along_x(): return lax.ppermute(value, 'tensor', pairs)]
    ppermute x0 -> x12, starting transfers between devices: none -> 35.4 us  [the longest x6 19.7 us: along_x(): return lax.ppermute(value, 'tensor', pairs)]
    psum x1 -> x0, blocking collectives: 31.3 us -> none  [per_device(): power = lax.psum(local_power, 'tensor')]
    dot_general x14 -> x2, matrix products: 25.6 us -> 1.55 us  [the longest x1 0.79 us: per_device(): jnp.einsum('jk,jc->kc', block, chunk_columns, preferred_element_type=jnp....]
    all_to_all x0 -> x1, blocking collectives: none -> 14.8 us  [exchange(): lax.all_to_all(pieces, 'tensor', split_axis=0, concat_axis=0, tiled=True)]
    pallas_call x0 -> x6, Pallas kernels: none -> 12.2 us  [the longest x1 3.6 us: precondition(): pl.pallas_call(functools.partial(precondition_kernel, len(lefts)), out_sh...]
    slice x2 -> x4, local copies, waits for them, and re-layouts: 12 us -> 0.07 us  [per_device(): left_rows = jnp.stack([piece[0] for piece in taken])]
  transfers between devices with their start and end apart: 6 -> 15, of which waited for: 6 -> 15; matrix products, arithmetic and copies ran while one was open for 4% -> 2% of each run, Pallas kernels for 0% -> 1%
where the time goes in v1:
time: 206 us; the launch traced here: 205 us
  waiting for transfers between devices  101 us (49%)
  starting transfers between devices  67.4 us (33%)
  blocking collectives  14.8 us (7%)
  Pallas kernels  12.2 us (6%)
  local copies, waits for them, and re-layouts  4.31 us (2%)
  other arithmetic  2.6 us (1%)
    all_to_all x1, waiting for transfers between devices, exchange(): lax.all_to_all(pieces, 'tensor', split_axis=0, concat_axis=0, tiled=True)  31.3 us
    ppermute x6, waiting for transfers between devices, along_x(): return lax.ppermute(value, 'tensor', pairs)  26.6 us
    ppermute x6, starting transfers between devices, along_x(): return lax.ppermute(value, 'tensor', pairs)  19.7 us
    ppermute x6, waiting for transfers between devices, along_y(): return lax.ppermute(value, 'tensor', pairs)  19.5 us
    all_to_all x1, waiting for transfers between devices, per_device(): lax.all_to_all(steps, 'fsdp', split_axis=0, concat_axis=0, tiled=True)  17.5 us
    all_to_all x1, starting transfers between devices, per_device(): lax.all_to_all(outgoing, 'fsdp', split_axis=0, concat_axis=0, tiled=True)  16.9 us
    ppermute x6, starting transfers between devices, along_y(): return lax.ppermute(value, 'tensor', pairs)  15.7 us
    all_to_all x1, blocking collectives, exchange(): lax.all_to_all(pieces, 'tensor', split_axis=0, concat_axis=0, tiled=True)  14.8 us
  transfers between devices with their start and end apart: 15, of which 15 were waited for; matrix products, arithmetic and copies ran while one was open for 2% of the time, Pallas kernels for 1%

profile of v1, /device:TPU:1, one launch (start us, length us, event | category | flops | bytes accessed | tf_op | source)
XLA Modules:
  0.0 205.5 jit_solution(567817942293912348)
XLA Ops:
  0.7 0.8 select_reduce_fusion.1.owner_ref
  1.5 0.9 copy-done.5
  2.4 1.6 gradient_to_owners.1
  4.0 16.9 %all-to-all-start = ((bf16[32,64,256]{2,1,0:T(8,128)(2,1)}), bf16[32,64,256]{2,1,0:T(8,128)(2,1)S(1)}, u32[]{:S(2)}, u32[]{:S(2)}) async-start(bf16[32,64,256]{2,1,0:T(8,128)(2,1)} %gradient_to_owners.1), calls=%async_computation | async-start | bytes 2097152 | tf_op jit(solution)/shard_map/gradient_to_owners/all_to_all | solution.py:221
  21.0 0.0 copy-done.12
  21.0 0.0 copy-done.13
  21.0 0.1 fusion.4
  21.1 1.3 collective-permute-start.2
  22.4 5.6 %collective-permute-start.1 = (bf16[2,64,1024]{2,1,0:T(8,128)(2,1)S(1)}, bf16[2,64,1024]{2,1,0:T(8,128)(2,1)S(1)}, u32[]{:S(2)}, u32[]{:S(2)}) collective-permute-start(bf16[2,64,1024]{2,1,0:T(8,128)(2,1)S(1)} %get-tuple-element.43), channel_id=1, source_target_pairs={{0,8},{1,9},{2,10},{3,11},{8,0},{9,1},{10,2},{11,3},{12,4},{13,5},... | collective-permute-start | bytes 786440 | tf_op jit(solution)/shard_map/roots_to_slot_groups/ppermute | solution.py:198
  28.0 1.9 collective-permute-start
  30.0 0.0 copy-done.14
  30.0 0.1 reshape.52
  30.1 0.6 collective-permute-done.2
  30.7 3.5 %collective-permute-done.1 = bf16[2,64,1024]{2,1,0:T(8,128)(2,1)S(1)} collective-permute-done((bf16[2,64,1024]{2,1,0:T(8,128)(2,1)S(1)}, bf16[2,64,1024]{2,1,0:T(8,128)(2,1)S(1)}, u32[]{:S(2)}, u32[]{:S(2)}) %collective-permute-start.1) | collective-permute-done | bytes 262176 | tf_op jit(solution)/shard_map/roots_to_slot_groups/ppermute | solution.py:198
  34.2 6.0 %collective-permute-done = bf16[2,64,1024]{2,1,0:T(8,128)(2,1)S(1)} collective-permute-done((bf16[2,64,1024]{2,1,0:T(8,128)(2,1)S(1)}, bf16[2,64,1024]{2,1,0:T(8,128)(2,1)S(1)}, u32[]{:S(2)}, u32[]{:S(2)}) %collective-permute-start) | collective-permute-done | bytes 262176 | tf_op jit(solution)/shard_map/roots_to_slot_groups/ppermute | solution.py:198
  40.3 0.1 pad_maximum_fusion.2.refs_0_
  40.4 0.0 copy-start.2
  40.4 3.1 %collective-permute-start.3 = (bf16[4,64,1024]{2,1,0:T(8,128)(2,1)S(1)}, bf16[4,64,1024]{2,1,0:T(8,128)(2,1)S(1)}, u32[]{:S(2)}, u32[]{:S(2)}) collective-permute-start(bf16[4,64,1024]{2,1,0:T(8,128)(2,1)S(1)} %pad_maximum_fusion.2.refs_0_), channel_id=1, source_target_pairs={{0,1},{1,2},{2,3},{3,0},{4,5},{5,6},{6,7},{7,4},{8,9},{9,10},{10,1... | collective-permute-start | bytes 1572872 | tf_op jit(solution)/shard_map/roots_to_slot_groups/ppermute | solution.py:204
  43.5 4.4 %collective-permute-start.4 = (bf16[4,64,1024]{2,1,0:T(8,128)(2,1)S(1)}, bf16[4,64,1024]{2,1,0:T(8,128)(2,1)S(1)}, u32[]{:S(2)}, u32[]{:S(2)}) collective-permute-start(bf16[4,64,1024]{2,1,0:T(8,128)(2,1)S(1)} %pad_maximum_fusion.2.refs_0_), channel_id=1, source_target_pairs={{0,2},{1,3},{2,0},{3,1},{4,6},{5,7},{6,4},{7,5},{8,10},{9,11},{10,... | collective-permute-start | bytes 1572872 | tf_op jit(solution)/shard_map/roots_to_slot_groups/ppermute | solution.py:204
  47.9 3.1 %collective-permute-start.5 = (bf16[4,64,1024]{2,1,0:T(8,128)(2,1)S(1)}, bf16[4,64,1024]{2,1,0:T(8,128)(2,1)S(1)}, u32[]{:S(2)}, u32[]{:S(2)}) collective-permute-start(bf16[4,64,1024]{2,1,0:T(8,128)(2,1)S(1)} %pad_maximum_fusion.2.refs_0_), channel_id=1, source_target_pairs={{0,3},{1,0},{2,1},{3,2},{4,7},{5,4},{6,5},{7,6},{8,11},{9,8},{10,9... | collective-permute-start | bytes 1572872 | tf_op jit(solution)/shard_map/roots_to_slot_groups/ppermute | solution.py:204
  50.9 0.2 select_reduce_fusion
  51.1 0.1 fusion.20
  51.3 0.1 select_reduce_fusion.2.band_ref
  51.4 0.9 pad_maximum_fusion.1.refs_4_
  52.3 4.1 %collective-permute-done.3.refs_1_ = bf16[4,64,1024]{2,1,0:T(8,128)(2,1)S(1)} collective-permute-done((bf16[4,64,1024]{2,1,0:T(8,128)(2,1)S(1)}, bf16[4,64,1024]{2,1,0:T(8,128)(2,1)S(1)}, u32[]{:S(2)}, u32[]{:S(2)}) %collective-permute-start.3) | collective-permute-done | bytes 524320 | tf_op jit(solution)/shard_map/roots_to_slot_groups/ppermute | solution.py:204
  56.3 12.2 %collective-permute-done.4.refs_2_ = bf16[4,64,1024]{2,1,0:T(8,128)(2,1)S(1)} collective-permute-done((bf16[4,64,1024]{2,1,0:T(8,128)(2,1)S(1)}, bf16[4,64,1024]{2,1,0:T(8,128)(2,1)S(1)}, u32[]{:S(2)}, u32[]{:S(2)}) %collective-permute-start.4) | collective-permute-done | bytes 524320 | tf_op jit(solution)/shard_map/roots_to_slot_groups/ppermute | solution.py:204
  68.6 0.0 copy-done.2
  68.6 1.5 collective-permute-done.5.refs_3_
  70.0 6.5 %all-to-all-done.pieces_ref = bf16[32,64,256]{2,1,0:T(8,128)(2,1)S(1)} async-done(((bf16[32,64,256]{2,1,0:T(8,128)(2,1)}), bf16[32,64,256]{2,1,0:T(8,128)(2,1)S(1)}, u32[]{:S(2)}, u32[]{:S(2)}) %all-to-all-start) | async-done | bytes 1048608 | tf_op jit(solution)/shard_map/gradient_to_owners/all_to_all | solution.py:221
  76.6 2.0 rows_of_held_blocks.1
  78.6 0.0 copy-start.3
  78.6 0.0 copy-start.4
  78.7 6.9 %all-to-all-start.1 = ((bf16[16,64,1024]{2,1,0:T(8,128)(2,1)}), bf16[16,64,1024]{2,1,0:T(8,128)(2,1)S(1)}, u32[]{:S(2)}, u32[]{:S(2)}) async-start(bf16[16,64,1024]{2,1,0:T(8,128)(2,1)} %rows_of_held_blocks.1), calls=%async_computation.1 | async-start | bytes 4194304 | tf_op jit(solution)/shard_map/rows_of_held_blocks/all_to_all | solution.py:30
  85.6 0.1 pad_add_fusion.place_ref
  85.7 31.3 %all-to-all-done.1.refs_5_ = bf16[16,64,1024]{2,1,0:T(8,128)(2,1)S(1)} async-done(((bf16[16,64,1024]{2,1,0:T(8,128)(2,1)}), bf16[16,64,1024]{2,1,0:T(8,128)(2,1)S(1)}, u32[]{:S(2)}, u32[]{:S(2)}) %all-to-all-start.1) | async-done | bytes 2097184 | tf_op jit(solution)/shard_map/rows_of_held_blocks/all_to_all | solution.py:30
  116.9 0.0 copy-done.4
  116.9 1.0 copy-done.7
  118.0 1.0 copy-done.9
  119.0 1.0 copy-done.11
  120.1 3.6 %precondition.1 = bf16[16,80,256]{2,1,0:T(8,128)(2,1)S(1)} custom-call(s32[2]{0:T(128)S(1)} %pad_add_fusion.place_ref, bf16[4,64,1024]{2,1,0:T(8,128)(2,1)S(1)} %copy-done.3, bf16[4,64,1024]{2,1,0:T(8,128)(2,1)S(1)} %copy-done.7, bf16[4,64,1024]{2,1,0:T(8,128)(2,1)S(1)} %copy-done.9, bf16[4,64,1024]{2,1,0:T(8,128)(2,1)S(1)} %copy-done.11, ...), custom_call_target="tpu_custom_call" | custom-call | flops 2684354560 | bytes 6291456 | tf_op jit(solution)/shard_map/precondition/pallas_call | solution.py:124
  123.7 14.8 %all_to_all.20.back_ref = bf16[16,80,256]{2,1,0:T(8,128)(2,1)S(1)} all-to-all(bf16[16,80,256]{2,1,0:T(8,128)(2,1)S(1)} %precondition.1), channel_id=1, replica_groups=mesh['fsdp'=32,'tensor'=16] {'tensor'}, dimensions={0} | all-to-all | bytes 1310720 | tf_op jit(solution)/shard_map/step_to_gradient_rows/all_to_all | solution.py:30
  138.5 1.8 step_to_gradient_rows.1
  140.3 8.2 %all-to-all-start.3 = ((bf16[32,64,256]{2,1,0:T(8,128)(2,1)}), bf16[32,64,256]{2,1,0:T(8,128)(2,1)S(1)}, u32[]{:S(2)}, u32[]{:S(2)}) async-start(bf16[32,64,256]{2,1,0:T(8,128)(2,1)} %step_to_gradient_rows.1), calls=%async_computation.3 | async-start | bytes 2097152 | tf_op jit(solution)/shard_map/step_to_gradient_rows/all_to_all | solution.py:261
  148.6 0.8 convolution_convert_fusion.1
  149.4 0.8 convolution_convert_fusion
  150.2 0.1 fusion.11
  150.3 2.5 %collective-permute-start.8 = (bf16[2,256,256]{2,1,0:T(8,128)(2,1)S(1)}, bf16[2,256,256]{2,1,0:T(8,128)(2,1)S(1)}, u32[]{:S(2)}, u32[]{:S(2)}) collective-permute-start(bf16[2,256,256]{2,1,0:T(8,128)(2,1)S(1)} %get-tuple-element.40), channel_id=1, source_target_pairs={{0,12},{1,13},{2,14},{3,15},{4,0},{5,1},{6,2},{7,3},{8,4},{9,5},{1... | collective-permute-start | bytes 786440 | tf_op jit(solution)/shard_map/statistics/ppermute | solution.py:198
  152.8 3.1 %collective-permute-start.7 = (bf16[2,256,256]{2,1,0:T(8,128)(2,1)S(1)}, bf16[2,256,256]{2,1,0:T(8,128)(2,1)S(1)}, u32[]{:S(2)}, u32[]{:S(2)}) collective-permute-start(bf16[2,256,256]{2,1,0:T(8,128)(2,1)S(1)} %get-tuple-element.39), channel_id=1, source_target_pairs={{0,8},{1,9},{2,10},{3,11},{4,12},{5,13},{6,14},{7,15},{8,0},{9,1},... | collective-permute-start | bytes 786440 | tf_op jit(solution)/shard_map/statistics/ppermute | solution.py:198
  155.9 1.3 collective-permute-start.6
  157.3 2.6 %collective-permute-done.8 = bf16[2,256,256]{2,1,0:T(8,128)(2,1)S(1)} collective-permute-done((bf16[2,256,256]{2,1,0:T(8,128)(2,1)S(1)}, bf16[2,256,256]{2,1,0:T(8,128)(2,1)S(1)}, u32[]{:S(2)}, u32[]{:S(2)}) %collective-permute-start.8) | collective-permute-done | bytes 262176 | tf_op jit(solution)/shard_map/statistics/ppermute | solution.py:198
  159.8 3.7 %collective-permute-done.7 = bf16[2,256,256]{2,1,0:T(8,128)(2,1)S(1)} collective-permute-done((bf16[2,256,256]{2,1,0:T(8,128)(2,1)S(1)}, bf16[2,256,256]{2,1,0:T(8,128)(2,1)S(1)}, u32[]{:S(2)}, u32[]{:S(2)}) %collective-permute-start.7) | collective-permute-done | bytes 262176 | tf_op jit(solution)/shard_map/statistics/ppermute | solution.py:198
  163.5 3.1 %collective-permute-done.6 = bf16[2,256,256]{2,1,0:T(8,128)(2,1)S(1)} collective-permute-done((bf16[2,256,256]{2,1,0:T(8,128)(2,1)S(1)}, bf16[2,256,256]{2,1,0:T(8,128)(2,1)S(1)}, u32[]{:S(2)}, u32[]{:S(2)}) %collective-permute-start.6) | collective-permute-done | bytes 262176 | tf_op jit(solution)/shard_map/statistics/ppermute | solution.py:198
  166.7 0.1 pad_maximum_fusion
  166.8 0.1 dynamic-slice_bitcast_fusion
  166.9 2.3 %collective-permute-start.9 = (bf16[4,2,64,256]{3,2,1,0:T(8,128)(2,1)S(1)}, bf16[4,2,64,256]{3,2,1,0:T(8,128)(2,1)S(1)}, u32[]{:S(2)}, u32[]{:S(2)}) collective-permute-start(bf16[4,2,64,256]{3,2,1,0:T(8,128)(2,1)S(1)} %get-tuple-element.35), channel_id=1, source_target_pairs={{0,1},{1,2},{2,3},{3,0},{4,5},{5,6},{6,7},{7,4},{8,9},{9,10},{10,1... | collective-permute-start | bytes 786440 | tf_op jit(solution)/shard_map/statistics/ppermute | solution.py:204
  169.2 3.8 %collective-permute-start.10 = (bf16[4,2,64,256]{3,2,1,0:T(8,128)(2,1)S(1)}, bf16[4,2,64,256]{3,2,1,0:T(8,128)(2,1)S(1)}, u32[]{:S(2)}, u32[]{:S(2)}) collective-permute-start(bf16[4,2,64,256]{3,2,1,0:T(8,128)(2,1)S(1)} %get-tuple-element.34), channel_id=1, source_target_pairs={{0,2},{1,3},{2,0},{3,1},{4,6},{5,7},{6,4},{7,5},{8,10},{9,11},{10,... | collective-permute-start | bytes 786440 | tf_op jit(solution)/shard_map/statistics/ppermute | solution.py:204
  173.0 3.0 %collective-permute-start.11 = (bf16[4,2,64,256]{3,2,1,0:T(8,128)(2,1)S(1)}, bf16[4,2,64,256]{3,2,1,0:T(8,128)(2,1)S(1)}, u32[]{:S(2)}, u32[]{:S(2)}) collective-permute-start(bf16[4,2,64,256]{3,2,1,0:T(8,128)(2,1)S(1)} %get-tuple-element.33), channel_id=1, source_target_pairs={{0,3},{1,0},{2,1},{3,2},{4,7},{5,4},{6,5},{7,6},{8,11},{9,8},{10,9... | collective-permute-start | bytes 786440 | tf_op jit(solution)/shard_map/statistics/ppermute | solution.py:204
  176.1 1.0 collective-permute-done.9.refs_1_
  177.1 4.6 %collective-permute-done.10.refs_2_ = bf16[4,2,64,256]{3,2,1,0:T(8,128)(2,1)S(1)} collective-permute-done((bf16[4,2,64,256]{3,2,1,0:T(8,128)(2,1)S(1)}, bf16[4,2,64,256]{3,2,1,0:T(8,128)(2,1)S(1)}, u32[]{:S(2)}, u32[]{:S(2)}) %collective-permute-start.10) | collective-permute-done | bytes 262176 | tf_op jit(solution)/shard_map/statistics/ppermute | solution.py:204
  181.7 3.2 %collective-permute-done.11.refs_3_ = bf16[4,2,64,256]{3,2,1,0:T(8,128)(2,1)S(1)} collective-permute-done((bf16[4,2,64,256]{3,2,1,0:T(8,128)(2,1)S(1)}, bf16[4,2,64,256]{3,2,1,0:T(8,128)(2,1)S(1)}, u32[]{:S(2)}, u32[]{:S(2)}) %collective-permute-start.11) | collective-permute-done | bytes 262176 | tf_op jit(solution)/shard_map/statistics/ppermute | solution.py:204
  184.9 0.0 copy-done
  184.9 1.9 statistics.1
  186.8 17.5 %all-to-all-done.3.returned_ref = bf16[32,64,256]{2,1,0:T(8,128)(2,1)S(1)} async-done(((bf16[32,64,256]{2,1,0:T(8,128)(2,1)}), bf16[32,64,256]{2,1,0:T(8,128)(2,1)S(1)}, u32[]{:S(2)}, u32[]{:S(2)}) %all-to-all-start.3) | async-done | bytes 1048608 | tf_op jit(solution)/shard_map/step_to_gradient_rows/all_to_all | solution.py:261
  204.3 1.2 update.1
  (25 shorter events, 0.1 us)
Async XLA Ops:
  1.5 0.9 copy-start.5
  2.4 18.6 %copy-start.12 = (bf16[3,64,1024]{2,1,0:T(8,128)(2,1)S(1)}, bf16[3,64,1024]{2,1,0:T(8,128)(2,1)}, u32[]{:S(2)}) copy-start(bf16[3,64,1024]{2,1,0:T(8,128)(2,1)} %param.10) | copy-start | bytes 1179652
  2.4 18.6 %copy-start.13 = (bf16[3,64,1024]{2,1,0:T(8,128)(2,1)S(1)}, bf16[3,64,1024]{2,1,0:T(8,128)(2,1)}, u32[]{:S(2)}) copy-start(bf16[3,64,1024]{2,1,0:T(8,128)(2,1)} %param.11) | copy-start | bytes 1179652
  4.0 26.0 %copy-start.14 = (s32[4,8]{1,0:T(4,128)S(1)}, s32[4,8]{1,0:T(4,128)}, u32[]{:S(2)}) copy-start(s32[4,8]{1,0:T(4,128)} %param.7) | copy-start | bytes 388
  4.0 72.6 %all-to-all-start = ((bf16[32,64,256]{2,1,0:T(8,128)(2,1)}), bf16[32,64,256]{2,1,0:T(8,128)(2,1)S(1)}, u32[]{:S(2)}, u32[]{:S(2)}) async-start(bf16[32,64,256]{2,1,0:T(8,128)(2,1)} %gradient_to_owners.1), calls=%async_computation | async-start | bytes 2097152 | tf_op jit(solution)/shard_map/gradient_to_owners/all_to_all | solution.py:221
  21.1 9.6 %collective-permute-start.2 = (bf16[2,64,1024]{2,1,0:T(8,128)(2,1)S(1)}, bf16[2,64,1024]{2,1,0:T(8,128)(2,1)S(1)}, u32[]{:S(2)}, u32[]{:S(2)}) collective-permute-start(bf16[2,64,1024]{2,1,0:T(8,128)(2,1)S(1)} %get-tuple-element.44), channel_id=1, source_target_pairs={{4,0},{5,1},{6,2},{7,3},{8,4},{9,5},{10,6},{11,7},{12,8},{13,9},{1... | collective-permute-start | bytes 786440 | tf_op jit(solution)/shard_map/roots_to_slot_groups/ppermute | solution.py:198
  22.4 11.8 %collective-permute-start.1 = (bf16[2,64,1024]{2,1,0:T(8,128)(2,1)S(1)}, bf16[2,64,1024]{2,1,0:T(8,128)(2,1)S(1)}, u32[]{:S(2)}, u32[]{:S(2)}) collective-permute-start(bf16[2,64,1024]{2,1,0:T(8,128)(2,1)S(1)} %get-tuple-element.43), channel_id=1, source_target_pairs={{0,8},{1,9},{2,10},{3,11},{8,0},{9,1},{10,2},{11,3},{12,4},{13,5},... | collective-permute-start | bytes 786440 | tf_op jit(solution)/shard_map/roots_to_slot_groups/ppermute | solution.py:198
  28.0 12.2 %collective-permute-start = (bf16[2,64,1024]{2,1,0:T(8,128)(2,1)S(1)}, bf16[2,64,1024]{2,1,0:T(8,128)(2,1)S(1)}, u32[]{:S(2)}, u32[]{:S(2)}) collective-permute-start(bf16[2,64,1024]{2,1,0:T(8,128)(2,1)S(1)} %get-tuple-element.42), channel_id=1, source_target_pairs={{0,4},{1,5},{2,6},{3,7},{4,8},{5,9},{6,10},{7,11},{12,0},{13,1},{1... | collective-permute-start | bytes 786440 | tf_op jit(solution)/shard_map/roots_to_slot_groups/ppermute | solution.py:198
  40.4 28.2 %copy-start.2 = (bf16[4,64,1024]{2,1,0:T(8,128)(2,1)}, bf16[4,64,1024]{2,1,0:T(8,128)(2,1)S(1)}, u32[]{:S(2)}) copy-start(bf16[4,64,1024]{2,1,0:T(8,128)(2,1)S(1)} %pad_maximum_fusion.2.refs_0_) | copy-start | bytes 1572868
  40.4 16.0 %collective-permute-start.3 = (bf16[4,64,1024]{2,1,0:T(8,128)(2,1)S(1)}, bf16[4,64,1024]{2,1,0:T(8,128)(2,1)S(1)}, u32[]{:S(2)}, u32[]{:S(2)}) collective-permute-start(bf16[4,64,1024]{2,1,0:T(8,128)(2,1)S(1)} %pad_maximum_fusion.2.refs_0_), channel_id=1, source_target_pairs={{0,1},{1,2},{2,3},{3,0},{4,5},{5,6},{6,7},{7,4},{8,9},{9,10},{10,1... | collective-permute-start | bytes 1572872 | tf_op jit(solution)/shard_map/roots_to_slot_groups/ppermute | solution.py:204
  43.5 25.1 %collective-permute-start.4 = (bf16[4,64,1024]{2,1,0:T(8,128)(2,1)S(1)}, bf16[4,64,1024]{2,1,0:T(8,128)(2,1)S(1)}, u32[]{:S(2)}, u32[]{:S(2)}) collective-permute-start(bf16[4,64,1024]{2,1,0:T(8,128)(2,1)S(1)} %pad_maximum_fusion.2.refs_0_), channel_id=1, source_target_pairs={{0,2},{1,3},{2,0},{3,1},{4,6},{5,7},{6,4},{7,5},{8,10},{9,11},{10,... | collective-permute-start | bytes 1572872 | tf_op jit(solution)/shard_map/roots_to_slot_groups/ppermute | solution.py:204
  47.9 22.2 %collective-permute-start.5 = (bf16[4,64,1024]{2,1,0:T(8,128)(2,1)S(1)}, bf16[4,64,1024]{2,1,0:T(8,128)(2,1)S(1)}, u32[]{:S(2)}, u32[]{:S(2)}) collective-permute-start(bf16[4,64,1024]{2,1,0:T(8,128)(2,1)S(1)} %pad_maximum_fusion.2.refs_0_), channel_id=1, source_target_pairs={{0,3},{1,0},{2,1},{3,2},{4,7},{5,4},{6,5},{7,6},{8,11},{9,8},{10,9... | collective-permute-start | bytes 1572872 | tf_op jit(solution)/shard_map/roots_to_slot_groups/ppermute | solution.py:204
  56.3 22.3 %copy-start.6 = (bf16[4,64,1024]{2,1,0:T(8,128)(2,1)}, bf16[4,64,1024]{2,1,0:T(8,128)(2,1)S(1)}, u32[]{:S(2)}) copy-start(bf16[4,64,1024]{2,1,0:T(8,128)(2,1)S(1)} %collective-permute-done.3.refs_1_) | copy-start | bytes 1572868
  68.6 10.1 %copy-start.8 = (bf16[4,64,1024]{2,1,0:T(8,128)(2,1)}, bf16[4,64,1024]{2,1,0:T(8,128)(2,1)S(1)}, u32[]{:S(2)}) copy-start(bf16[4,64,1024]{2,1,0:T(8,128)(2,1)S(1)} %collective-permute-done.4.refs_2_) | copy-start | bytes 1572868
  70.0 8.6 %copy-start.10 = (bf16[4,64,1024]{2,1,0:T(8,128)(2,1)}, bf16[4,64,1024]{2,1,0:T(8,128)(2,1)S(1)}, u32[]{:S(2)}) copy-start(bf16[4,64,1024]{2,1,0:T(8,128)(2,1)S(1)} %collective-permute-done.5.refs_3_) | copy-start | bytes 1572868
  78.6 38.3 %copy-start.3 = (bf16[4,64,1024]{2,1,0:T(8,128)(2,1)S(1)}, bf16[4,64,1024]{2,1,0:T(8,128)(2,1)}, u32[]{:S(2)}) copy-start(bf16[4,64,1024]{2,1,0:T(8,128)(2,1)} %copy-done.2) | copy-start | bytes 1572868
  78.6 38.3 %copy-start.4 = (bf16[4,64,1024]{2,1,0:T(8,128)(2,1)S(1)}, bf16[4,64,1024]{2,1,0:T(8,128)(2,1)}, u32[]{:S(2)}) copy-start(bf16[4,64,1024]{2,1,0:T(8,128)(2,1)} %pad_maximum_fusion.1.refs_4_) | copy-start | bytes 1572868
  78.7 38.3 %all-to-all-start.1 = ((bf16[16,64,1024]{2,1,0:T(8,128)(2,1)}), bf16[16,64,1024]{2,1,0:T(8,128)(2,1)S(1)}, u32[]{:S(2)}, u32[]{:S(2)}) async-start(bf16[16,64,1024]{2,1,0:T(8,128)(2,1)} %rows_of_held_blocks.1), calls=%async_computation.1 | async-start | bytes 4194304 | tf_op jit(solution)/shard_map/rows_of_held_blocks/all_to_all | solution.py:30
  116.9 1.0 copy-start.7
  118.0 1.0 copy-start.9
  119.0 1.0 copy-start.11
  140.3 64.0 %all-to-all-start.3 = ((bf16[32,64,256]{2,1,0:T(8,128)(2,1)}), bf16[32,64,256]{2,1,0:T(8,128)(2,1)S(1)}, u32[]{:S(2)}, u32[]{:S(2)}) async-start(bf16[32,64,256]{2,1,0:T(8,128)(2,1)} %step_to_gradient_rows.1), calls=%async_computation.3 | async-start | bytes 2097152 | tf_op jit(solution)/shard_map/step_to_gradient_rows/all_to_all | solution.py:261
  150.3 9.6 %collective-permute-start.8 = (bf16[2,256,256]{2,1,0:T(8,128)(2,1)S(1)}, bf16[2,256,256]{2,1,0:T(8,128)(2,1)S(1)}, u32[]{:S(2)}, u32[]{:S(2)}) collective-permute-start(bf16[2,256,256]{2,1,0:T(8,128)(2,1)S(1)} %get-tuple-element.40), channel_id=1, source_target_pairs={{0,12},{1,13},{2,14},{3,15},{4,0},{5,1},{6,2},{7,3},{8,4},{9,5},{1... | collective-permute-start | bytes 786440 | tf_op jit(solution)/shard_map/statistics/ppermute | solution.py:198
  152.8 10.8 %collective-permute-start.7 = (bf16[2,256,256]{2,1,0:T(8,128)(2,1)S(1)}, bf16[2,256,256]{2,1,0:T(8,128)(2,1)S(1)}, u32[]{:S(2)}, u32[]{:S(2)}) collective-permute-start(bf16[2,256,256]{2,1,0:T(8,128)(2,1)S(1)} %get-tuple-element.39), channel_id=1, source_target_pairs={{0,8},{1,9},{2,10},{3,11},{4,12},{5,13},{6,14},{7,15},{8,0},{9,1},... | collective-permute-start | bytes 786440 | tf_op jit(solution)/shard_map/statistics/ppermute | solution.py:198
  155.9 10.8 %collective-permute-start.6 = (bf16[2,256,256]{2,1,0:T(8,128)(2,1)S(1)}, bf16[2,256,256]{2,1,0:T(8,128)(2,1)S(1)}, u32[]{:S(2)}, u32[]{:S(2)}) collective-permute-start(bf16[2,256,256]{2,1,0:T(8,128)(2,1)S(1)} %get-tuple-element.38), channel_id=1, source_target_pairs={{0,4},{1,5},{2,6},{3,7},{4,8},{5,9},{6,10},{7,11},{8,12},{9,13},{1... | collective-permute-start | bytes 786440 | tf_op jit(solution)/shard_map/statistics/ppermute | solution.py:198
  166.7 18.2 %copy-start = (f32[3,64,1024]{2,1,0:T(8,128)S(1)}, f32[3,64,1024]{2,1,0:T(8,128)}, u32[]{:S(2)}) copy-start(f32[3,64,1024]{2,1,0:T(8,128)} %left_ref.1) | copy-start | bytes 2359300
  166.7 18.2 %copy-start.1 = (f32[3,64,1024]{2,1,0:T(8,128)S(1)}, f32[3,64,1024]{2,1,0:T(8,128)}, u32[]{:S(2)}) copy-start(f32[3,64,1024]{2,1,0:T(8,128)} %right_ref.1) | copy-start | bytes 2359300
  166.9 10.2 %collective-permute-start.9 = (bf16[4,2,64,256]{3,2,1,0:T(8,128)(2,1)S(1)}, bf16[4,2,64,256]{3,2,1,0:T(8,128)(2,1)S(1)}, u32[]{:S(2)}, u32[]{:S(2)}) collective-permute-start(bf16[4,2,64,256]{3,2,1,0:T(8,128)(2,1)S(1)} %get-tuple-element.35), channel_id=1, source_target_pairs={{0,1},{1,2},{2,3},{3,0},{4,5},{5,6},{6,7},{7,4},{8,9},{9,10},{10,1... | collective-permute-start | bytes 786440 | tf_op jit(solution)/shard_map/statistics/ppermute | solution.py:204
  169.2 12.5 %collective-permute-start.10 = (bf16[4,2,64,256]{3,2,1,0:T(8,128)(2,1)S(1)}, bf16[4,2,64,256]{3,2,1,0:T(8,128)(2,1)S(1)}, u32[]{:S(2)}, u32[]{:S(2)}) collective-permute-start(bf16[4,2,64,256]{3,2,1,0:T(8,128)(2,1)S(1)} %get-tuple-element.34), channel_id=1, source_target_pairs={{0,2},{1,3},{2,0},{3,1},{4,6},{5,7},{6,4},{7,5},{8,10},{9,11},{10,... | collective-permute-start | bytes 786440 | tf_op jit(solution)/shard_map/statistics/ppermute | solution.py:204
  173.0 11.9 %collective-permute-start.11 = (bf16[4,2,64,256]{3,2,1,0:T(8,128)(2,1)S(1)}, bf16[4,2,64,256]{3,2,1,0:T(8,128)(2,1)S(1)}, u32[]{:S(2)}, u32[]{:S(2)}) collective-permute-start(bf16[4,2,64,256]{3,2,1,0:T(8,128)(2,1)S(1)} %get-tuple-element.33), channel_id=1, source_target_pairs={{0,3},{1,0},{2,1},{3,2},{4,7},{5,4},{6,5},{7,6},{8,11},{9,8},{10,9... | collective-permute-start | bytes 786440 | tf_op jit(solution)/shard_map/statistics/ppermute | solution.py:204

commit v2 on v1

v2 whole, which is shorter than its diff:
```python
import functools
import jax
import jax.numpy as jnp
from jax import lax
from jax.experimental import pallas as pl
from jax.experimental.pallas import tpu as pltpu
from jax.sharding import PartitionSpec as P

BETA = 0.999
STEP = 0.5
EPS = 1e-06
TAIL = 16
ROWS = 16
LANES = 128
VMEM = pl.BlockSpec(memory_space=pltpu.VMEM)
ANY = pl.BlockSpec(memory_space=pl.ANY)
SMEM = pl.BlockSpec(memory_space=pltpu.SMEM)
LIMIT = pltpu.CompilerParams(vmem_limit_bytes=24 * 2**20)


def cost(flops, moved):
    return pl.CostEstimate(flops=flops, bytes_accessed=moved, transcendentals=0)


def slot_numbers(owners_flat):
    total = owners_flat.shape[0]
    same = owners_flat[:, None] == owners_flat[None, :]
    earlier = jnp.arange(total)[None, :] < jnp.arange(total)[:, None]
    return jnp.sum(jnp.where(same & earlier, 1, 0), axis=1).astype(jnp.int32)


def exchange(pieces):
    return lax.all_to_all(pieces, "tensor", split_axis=0, concat_axis=0, tiled=True)


def tile_of(number):
    return pl.ds(number // 2 * ROWS, ROWS), pl.ds(number % 2 * LANES, LANES)


def spread_kernel(part_ref, gradient_ref, out_ref):
    count = gradient_ref.shape[0]
    tiles = out_ref.shape[0] // count
    for group in range(count):
        column = lax.rem(group + count - part_ref[0], count)
        for tile in range(tiles):
            rows, lanes = tile_of(tile)
            out_ref[group * tiles + tile] = gradient_ref[column, rows, lanes]


def pick_kernel(index_ref, tiles_ref, out_ref):
    for at in range(out_ref.shape[0]):
        out_ref[at] = tiles_ref[index_ref[at]]


def pick(index, tiles):
    shape = (index.shape[0],) + tiles.shape[1:]
    return pl.pallas_call(
        pick_kernel,
        out_shape=jax.ShapeDtypeStruct(shape, tiles.dtype),
        in_specs=[SMEM, VMEM],
        out_specs=VMEM,
        compiler_params=LIMIT,
        cost_estimate=cost(0, 2**20),
    )(index, tiles)


def held_rows_kernel(column_ref, used_ref, tiles_ref, sent_ref, rows_ref, sems):
    capacity, _, block_side = rows_ref.shape
    places = sent_ref.shape[0]
    parts = places // (capacity + 1)
    width = block_side // parts
    tiles = tiles_ref.shape[0] // parts
    copies = []
    for slot in range(capacity + 1):
        if slot < capacity:
            keep = used_ref[slot] > 0
            for part in range(parts):
                group = lax.rem(column_ref[slot] + part, parts)
                for tile in range(tiles):
                    rows, lanes = tile_of(tile)
                    lanes = pl.ds(part * width + lanes.start, LANES)
                    value = tiles_ref[group * tiles + tile, slot]
                    rows_ref[slot, rows, lanes] = jnp.where(keep, value, jnp.zeros_like(value))
        for member in range(parts):
            place = slot * parts + member
            source = rows_ref.at[min(slot, capacity - 1)]
            copies.append(pltpu.make_async_copy(source, sent_ref.at[place], sems.at[place]))
            copies[-1].start()
    for copy in copies:
        copy.wait()


def held_rows(column_of, used, tiles, height, block_side, places):
    capacity = tiles.shape[1]
    return pl.pallas_call(
        held_rows_kernel,
        out_shape=jax.ShapeDtypeStruct((places, height, block_side), tiles.dtype),
        in_specs=[SMEM, SMEM, VMEM],
        out_specs=ANY,
        scratch_shapes=[
            pltpu.VMEM((capacity, height, block_side), tiles.dtype),
            pltpu.SemaphoreType.DMA((places,)),
        ],
        compiler_params=LIMIT,
        cost_estimate=cost(0, 4 * 2**20),
    )(column_of, used, tiles)


def three_parts(value):
    high = value.astype(jnp.bfloat16)
    rest = value - high.astype(jnp.float32)
    middle = rest.astype(jnp.bfloat16)
    return [high, middle, (rest - middle.astype(jnp.float32)).astype(jnp.bfloat16)]


def around(place, step, count):
    return lax.rem(place + count - step, count)


def precondition_kernel(side, origins, place_ref, *refs):
    left_ref, right_ref, block_ref, out_ref = refs
    y, x = place_ref[0], place_ref[1]
    places, height, block_side = block_ref.shape
    width = out_ref.shape[2]
    block = block_ref[...].reshape(block_side, block_side)
    right = jnp.concatenate([right_ref[around(y, at, side)] for at in range(side)], axis=0)
    power = jnp.zeros((1, width), jnp.float32)
    for begin in range(0, places, side):
        left = left_ref[pl.ds(begin, side)].reshape(side * height, block_side)
        mixed = jnp.dot(left, block, preferred_element_type=jnp.float32).astype(jnp.bfloat16)
        product = lax.dot_general(
            mixed, right, (((1,), (1,)), ((), ())), preferred_element_type=jnp.float32
        )
        power += jnp.sum(product * product, axis=0, keepdims=True)
        product = product.astype(jnp.bfloat16)
        for at, (row, column) in enumerate(origins[begin : begin + side]):
            place = around(y, row, side) * side + around(x, column, side)
            out_ref[place, pl.ds(0, height), :] = product[at * height : (at + 1) * height]
    share = places // side
    own = block_ref[pl.ds(x * share, share)].astype(jnp.float32).reshape(width, block_side)
    own = jnp.sum(own * own, axis=0, keepdims=True)
    grad = sum(own[:, at * width : (at + 1) * width] for at in range(side))
    number = lax.broadcasted_iota(jnp.int32, (TAIL, width), 0)
    tail = jnp.zeros((TAIL, width), jnp.float32)
    for at, line in enumerate(three_parts(power) + three_parts(grad)):
        tail = jnp.where(number == at, line.astype(jnp.float32), tail)
    tail = tail.astype(jnp.bfloat16)
    for place in range(places):
        out_ref[place, pl.ds(height, TAIL), :] = tail


def precondition(place, left, origins, right, block):
    places, height, block_side = block.shape
    side = right.shape[0]
    width = block_side // side
    return pl.pallas_call(
        functools.partial(precondition_kernel, side, origins),
        out_shape=jax.ShapeDtypeStruct((places, height + TAIL, width), jnp.bfloat16),
        in_specs=[SMEM] + [VMEM] * 3,
        out_specs=VMEM,
        compiler_params=pltpu.CompilerParams(vmem_limit_bytes=32 * 2**20),
        cost_estimate=cost(2 * block_side * block_side * (block_side + width), 6 * 2**20),
    )(place, left, right, block)


def steps_kernel(side, column_ref, back_ref, out_ref):
    height = back_ref.shape[1] - TAIL
    piece = back_ref.shape[2] // side
    tiles = out_ref.shape[0] // side
    for slot in range(column_ref.shape[0]):
        sums = sum(
            back_ref[slot * side + member, pl.ds(height, TAIL), :].astype(jnp.float32)
            for member in range(side)
        )
        sums = jnp.sum(sums, axis=1, keepdims=True)
        power = jnp.sum(sums[0:3], axis=0, keepdims=True)
        grad = jnp.sum(sums[3:6], axis=0, keepdims=True)
        scale = -STEP * jnp.sqrt(grad) * lax.rsqrt(power + EPS)
        rows_of = [
            (
                scale * back_ref[slot * side + member, pl.ds(0, height), :].astype(jnp.float32)
            ).astype(jnp.bfloat16)
            for member in range(side)
        ]
        for part in range(side):
            group = lax.rem(column_ref[slot] + part, side)
            chunk = jnp.concatenate(
                [rows[:, part * piece : (part + 1) * piece] for rows in rows_of], axis=1
            )
            for tile in range(tiles):
                rows, lanes = tile_of(tile)
                out_ref[group * tiles + tile, slot] = chunk[
                    rows.start : rows.start + ROWS, lanes.start : lanes.start + LANES
                ]


def update_kernel(part_ref, tiles_ref, out_ref):
    count = out_ref.shape[0]
    tiles = tiles_ref.shape[0] // count
    for column in range(count):
        group = lax.rem(column + part_ref[0], count)
        for tile in range(tiles):
            rows, lanes = tile_of(tile)
            out_ref[column, rows, lanes] = tiles_ref[group * tiles + tile]


def statistics_kernel(side, place_ref, left_ref, right_ref, *refs):
    term_refs, outs = refs[:side], refs[side:]
    for step in range(side):
        slot = around(place_ref[0], step, side)

        @pl.when(slot < left_ref.shape[0])
        def _():
            for kind, (old, new) in enumerate(zip((left_ref, right_ref), outs)):
                term = term_refs[step][kind].astype(jnp.float32)
                new[slot] = BETA * old[slot] + (1.0 - BETA) * term


def per_device(gradient, block_owner, left_stats, right_stats, left_root, right_root):
    tensor_index = lax.axis_index("tensor")
    fsdp_index = lax.axis_index("fsdp")
    fsdp_count = lax.axis_size("fsdp")
    tensor_count = lax.axis_size("tensor")
    col_blocks, local_height, row_depth = gradient.shape
    row_blocks = block_owner.shape[1]
    capacity, _, block_side = left_stats.shape
    side = block_side // row_depth
    y, x = tensor_index // side, tensor_index % side
    place = jnp.stack([y, x]).astype(jnp.int32)

    def along_y(value, step, sources, targets):
        pairs = [
            (a * side + b, (a + step) % side * side + b)
            for a in range(side)
            for b in range(side)
            if a < sources and (a + step) % side < targets
        ]
        return lax.ppermute(value, "tensor", pairs)

    def along_x(value, step, rows):
        pairs = [
            (a * side + b, a * side + (b + step) % side) for a in range(rows) for b in range(side)
        ]
        return lax.ppermute(value, "tensor", pairs)

    def over_rows(value):
        return lax.all_to_all(value, "fsdp", split_axis=0, concat_axis=0, tiled=True)

    part = (fsdp_index % side).astype(jnp.int32).reshape(1)
    group = fsdp_index // (fsdp_count // col_blocks)

    with jax.named_scope("gradient_spread"):
        spread = pl.pallas_call(
            spread_kernel,
            out_shape=jax.ShapeDtypeStruct((fsdp_count, ROWS, LANES), gradient.dtype),
            in_specs=[SMEM, VMEM],
            out_specs=VMEM,
            compiler_params=LIMIT,
            cost_estimate=cost(0, 2**18),
        )(part, gradient)
        spread, left_root, right_root = lax.optimization_barrier((spread, left_root, right_root))
        spread = over_rows(spread)

    with jax.named_scope("where_blocks_go"):
        owners_flat = block_owner.reshape(-1)
        numbers = jnp.arange(owners_flat.shape[0])
        column_flat, band_flat = numbers // row_blocks, numbers % row_blocks
        entries = owners_flat * capacity + slot_numbers(owners_flat)
        held_at = entries[:, None] == jnp.arange(fsdp_count * capacity)[None, :]
        source = band_flat * side + (group - column_flat + side) % side
        forward = jnp.sum(jnp.where(held_at, source[:, None], 0), axis=0).astype(jnp.int32)
        mine = entries[:, None] == (fsdp_index * capacity + jnp.arange(capacity))[None, :]
        used = jnp.any(mine, axis=0).astype(jnp.int32)
        column_of = jnp.sum(jnp.where(mine, column_flat[:, None], 0), axis=0).astype(jnp.int32)
        homes = jnp.arange(fsdp_count)
        wanted = (group - homes % side + side) % side * row_blocks + homes // side
        backward = jnp.sum(
            jnp.where(wanted[:, None] == numbers[None, :], entries[None, :], 0), axis=1
        ).astype(jnp.int32)

    with jax.named_scope("gradient_to_owners"):
        sent = pick(forward, spread).reshape(fsdp_count, capacity, ROWS, LANES)
        tiles = over_rows(sent)

    with jax.named_scope("roots_to_slot_groups"):
        roots = jnp.stack([left_root, right_root], axis=1)
        taken = []
        for step in range(side):
            slot = jnp.minimum((y + step) % side, capacity - 1)
            own = lax.dynamic_index_in_dim(roots, slot, 0, keepdims=False)
            taken.append(along_y(own, step, side, capacity) if step else own)
        left_rows = jnp.stack([piece[0] for piece in taken])
        right_rows = jnp.stack([piece[1] for piece in taken])
        half = side // 2
        before = along_x(left_rows, 1, capacity)
        behind = along_x(left_rows, side - 1, capacity)
        lefts = [
            left_rows,
            before,
            behind,
            along_x(before[:half], 1, capacity),
            along_x(behind[half:], side - 1, capacity),
        ]
        origins = [
            (row, column) for column in (0, 1, side - 1, half) for row in range(side)
        ]
        tiles, right_rows, *lefts = lax.optimization_barrier((tiles, right_rows, *lefts))

    with jax.named_scope("rows_of_held_blocks"):
        sent = held_rows(column_of, used, tiles, local_height, block_side, tensor_count)
        sent, *lefts = lax.optimization_barrier((sent, *lefts))
        block = exchange(sent)
        left = jnp.concatenate(lefts)

    with jax.named_scope("precondition"):
        leaving = precondition(place, left, origins, right_rows, block)

    with jax.named_scope("step_to_gradient_rows"):
        back = exchange(leaving)
        steps = pl.pallas_call(
            functools.partial(steps_kernel, side),
            out_shape=jax.ShapeDtypeStruct((fsdp_count, capacity, ROWS, LANES), jnp.bfloat16),
            in_specs=[SMEM, VMEM],
            out_specs=VMEM,
            compiler_params=LIMIT,
            cost_estimate=cost(0, 2 * 2**20),
        )(column_of, back)
        passing = over_rows(steps).reshape(fsdp_count * capacity, ROWS, LANES)

    with jax.named_scope("statistics"):
        block, steps = lax.optimization_barrier((block, steps))
        block = block.reshape(block_side, block_side)
        own_rows = lax.dynamic_index_in_dim(
            block.reshape(side, side, local_height, block_side), x, 1, keepdims=False
        ).reshape(row_depth, block_side)
        own_columns = jnp.concatenate(
            [
                lax.dynamic_slice_in_dim(block, (at * side + x) * local_height, local_height, 1)
                for at in range(side)
            ],
            axis=1,
        )
        left_term = jnp.einsum("ak,jk->aj", own_rows, block, preferred_element_type=jnp.float32)
        right_term = jnp.einsum("ja,jk->ak", own_columns, block, preferred_element_type=jnp.float32)
        terms = jnp.stack([left_term.astype(jnp.bfloat16), right_term.astype(jnp.bfloat16)])
        terms = terms.reshape(2, side, local_height, block_side)
        arrived = []
        for step in range(side):
            own = lax.dynamic_index_in_dim(terms, (y + step) % side, 1, keepdims=False)
            arrived.append(along_y(own, step, capacity, side) if step else own)
        passing, *arrived = lax.optimization_barrier((passing, *arrived))
        returned = over_rows(pick(backward, passing))
        left_updated, right_updated = pl.pallas_call(
            functools.partial(statistics_kernel, side),
            out_shape=(
                jax.ShapeDtypeStruct(left_stats.shape, left_stats.dtype),
                jax.ShapeDtypeStruct(right_stats.shape, right_stats.dtype),
            ),
            in_specs=[SMEM] + [VMEM] * (2 + side),
            out_specs=(VMEM, VMEM),
            compiler_params=LIMIT,
            cost_estimate=cost(0, 4 * 2**20),
        )(place, left_stats, right_stats, *arrived)
        returned, left_updated, right_updated = lax.optimization_barrier(
            (returned, left_updated, right_updated)
        )

    with jax.named_scope("update"):
        update = pl.pallas_call(
            update_kernel,
            out_shape=jax.ShapeDtypeStruct(gradient.shape, gradient.dtype),
            in_specs=[SMEM, VMEM],
            out_specs=VMEM,
            compiler_params=LIMIT,
            cost_estimate=cost(0, 2**20),
        )(part, returned)
    return (left_updated, right_updated, update)


def solution(mesh):
    placed = (
        P(None, "tensor", "fsdp"),
        P(),
        P("fsdp", "tensor", None),
        P("fsdp", "tensor", None),
        P("fsdp", "tensor", None),
        P("fsdp", "tensor", None),
    )
    return jax.shard_map(
        per_device,
        mesh=mesh,
        in_specs=placed,
        out_specs=(P("fsdp", "tensor", None), P("fsdp", "tensor", None), P(None, "tensor", "fsdp")),
        check_vma=False,
    )
```

time: 206 us -> 195 us (0.947)
  waiting for transfers between devices: 101 us -> 79.2 us
  starting transfers between devices: 67.4 us -> 74.7 us
  local copies, waits for them, and re-layouts: 4.31 us -> 6.63 us
    all_to_all x2 -> x4, starting transfers between devices: 25.1 us -> 38.4 us  [over_rows(): lax.all_to_all(value, 'fsdp', split_axis=0, concat_axis=0, tiled=True)]
    ppermute x6 -> x4, waiting for transfers between devices: 26.6 us -> 13.6 us  [along_x(): return lax.ppermute(value, 'tensor', pairs)]
    ppermute x6, waiting for transfers between devices: 19.5 us -> 8.46 us  [along_y(): return lax.ppermute(value, 'tensor', pairs)]
    ppermute x6 -> x4, starting transfers between devices: 19.7 us -> 13 us  [along_x(): return lax.ppermute(value, 'tensor', pairs)]
    all_to_all x2 -> x4, waiting for transfers between devices: 24 us -> 29.3 us  [over_rows(): lax.all_to_all(value, 'fsdp', split_axis=0, concat_axis=0, tiled=True)]
    all_to_all x1, waiting for transfers between devices: 31.3 us -> 27.8 us  [exchange(): lax.all_to_all(pieces, 'tensor', split_axis=0, concat_axis=0, tiled=True)]
    pallas_call x2 -> x4, Pallas kernels: 5.21 us -> 6.85 us  [the longest x1 3.59 us: precondition(): pl.pallas_call(functools.partial(precondition_kernel, side, origins), out...]
    unnamed x30 -> x22, local copies, waits for them, and re-layouts: 4.07 us -> 5.02 us
  transfers between devices with their start and end apart: 15 -> 15, of which waited for: 15 -> 10; matrix products, arithmetic and copies ran while one was open for 2% -> 4% of each run, Pallas kernels for 1% -> 2%
where the time goes in v2:
time: 195 us; the launch traced here: 194 us
  waiting for transfers between devices  79.2 us (41%)
  starting transfers between devices  74.7 us (38%)
  blocking collectives  14.8 us (8%)
  Pallas kernels  13.1 us (7%)
  local copies, waits for them, and re-layouts  6.63 us (3%)
  other arithmetic  2.57 us (1%)
    all_to_all x4, starting transfers between devices, over_rows(): lax.all_to_all(value, 'fsdp', split_axis=0, concat_axis=0, tiled=True)  38.4 us
    all_to_all x4, waiting for transfers between devices, over_rows(): lax.all_to_all(value, 'fsdp', split_axis=0, concat_axis=0, tiled=True)  29.3 us
    all_to_all x1, waiting for transfers between devices, exchange(): lax.all_to_all(pieces, 'tensor', split_axis=0, concat_axis=0, tiled=True)  27.8 us
    ppermute x6, starting transfers between devices, along_y(): return lax.ppermute(value, 'tensor', pairs)  16.5 us
    all_to_all x1, blocking collectives, exchange(): lax.all_to_all(pieces, 'tensor', split_axis=0, concat_axis=0, tiled=True)  14.8 us
    ppermute x4, waiting for transfers between devices, along_x(): return lax.ppermute(value, 'tensor', pairs)  13.6 us
    ppermute x4, starting transfers between devices, along_x(): return lax.ppermute(value, 'tensor', pairs)  13 us
    ppermute x6, waiting for transfers between devices, along_y(): return lax.ppermute(value, 'tensor', pairs)  8.46 us
  transfers between devices with their start and end apart: 15, of which 10 were waited for; matrix products, arithmetic and copies ran while one was open for 4% of the time, Pallas kernels for 2%

profile of v2, /device:TPU:1, one launch (start us, length us, event | category | flops | bytes accessed | tf_op | source)
XLA Modules:
  0.0 193.8 jit_solution(3051700324365278518)
XLA Ops:
  0.6 0.0 copy-start.8
  0.7 0.9 copy-done.4
  1.6 0.7 gradient_spread.1
  2.2 16.7 %all-to-all-start = ((bf16[32,16,128]{2,1,0:T(8,128)(2,1)}), bf16[32,16,128]{2,1,0:T(8,128)(2,1)S(1)}, u32[]{:S(2)}, u32[]{:S(2)}) async-start(bf16[32,16,128]{2,1,0:T(8,128)(2,1)} %gradient_spread.1), calls=%async_computation | async-start | bytes 262144 | tf_op jit(solution)/shard_map/gradient_spread/all_to_all | solution.py:247
  19.1 1.4 fusion.9
  20.5 1.3 collective-permute-start.2
  21.8 5.6 %collective-permute-start.1 = (bf16[2,64,1024]{2,1,0:T(8,128)(2,1)S(1)}, bf16[2,64,1024]{2,1,0:T(8,128)(2,1)S(1)}, u32[]{:S(2)}, u32[]{:S(2)}) collective-permute-start(bf16[2,64,1024]{2,1,0:T(8,128)(2,1)S(1)} %get-tuple-element.67), channel_id=1, source_target_pairs={{0,8},{1,9},{2,10},{3,11},{8,0},{9,1},{10,2},{11,3},{12,4},{13,5},... | collective-permute-start | bytes 786440 | tf_op jit(solution)/shard_map/roots_to_slot_groups/ppermute | solution.py:238
  27.4 1.9 collective-permute-start
  29.3 0.1 reshape.133
  29.4 0.2 select_reduce_fusion.2
  29.7 0.1 select_reduce_fusion.index_ref
  29.8 5.1 %all-to-all-done.tiles_ref = bf16[32,16,128]{2,1,0:T(8,128)(2,1)S(1)} async-done(((bf16[32,16,128]{2,1,0:T(8,128)(2,1)}), bf16[32,16,128]{2,1,0:T(8,128)(2,1)S(1)}, u32[]{:S(2)}, u32[]{:S(2)}) %all-to-all-start) | async-done | bytes 131104 | tf_op jit(solution)/shard_map/gradient_spread/all_to_all | solution.py:247
  34.8 1.4 gradient_to_owners.1
  36.2 7.7 %all-to-all-start.1 = ((bf16[32,3,16,128]{3,2,1,0:T(8,128)(2,1)}), bf16[32,3,16,128]{3,2,1,0:T(8,128)(2,1)S(1)}, u32[]{:S(2)}, u32[]{:S(2)}) async-start(bf16[32,3,16,128]{3,2,1,0:T(8,128)(2,1)} %bitcast.3), calls=%async_computation.1 | async-start | bytes 786432 | tf_op jit(solution)/shard_map/gradient_to_owners/all_to_all | solution.py:247
  43.9 0.0 collective-permute-done.2
  43.9 0.0 collective-permute-done.1
  44.0 0.0 collective-permute-done
  44.0 0.1 pad_maximum_fusion.1
  44.1 3.1 %collective-permute-start.3 = (bf16[4,64,1024]{2,1,0:T(8,128)(2,1)S(1)}, bf16[4,64,1024]{2,1,0:T(8,128)(2,1)S(1)}, u32[]{:S(2)}, u32[]{:S(2)}) collective-permute-start(bf16[4,64,1024]{2,1,0:T(8,128)(2,1)S(1)} %pad_maximum_fusion.1), channel_id=1, source_target_pairs={{0,1},{1,2},{2,3},{3,0},{4,5},{5,6},{6,7},{7,4},{8,9},{9,10},{10,1... | collective-permute-start | bytes 1572872 | tf_op jit(solution)/shard_map/roots_to_slot_groups/ppermute | solution.py:244
  47.2 3.4 %collective-permute-start.4 = (bf16[4,64,1024]{2,1,0:T(8,128)(2,1)S(1)}, bf16[4,64,1024]{2,1,0:T(8,128)(2,1)S(1)}, u32[]{:S(2)}, u32[]{:S(2)}) collective-permute-start(bf16[4,64,1024]{2,1,0:T(8,128)(2,1)S(1)} %pad_maximum_fusion.1), channel_id=1, source_target_pairs={{0,3},{1,0},{2,1},{3,2},{4,7},{5,4},{6,5},{7,6},{8,11},{9,8},{10,9... | collective-permute-start | bytes 1572872 | tf_op jit(solution)/shard_map/roots_to_slot_groups/ppermute | solution.py:244
  50.6 0.2 compare_reduce_fusion
  50.8 9.7 %collective-permute-done.3 = bf16[4,64,1024]{2,1,0:T(8,128)(2,1)S(1)} collective-permute-done((bf16[4,64,1024]{2,1,0:T(8,128)(2,1)S(1)}, bf16[4,64,1024]{2,1,0:T(8,128)(2,1)S(1)}, u32[]{:S(2)}, u32[]{:S(2)}) %collective-permute-start.3) | collective-permute-done | bytes 524320 | tf_op jit(solution)/shard_map/roots_to_slot_groups/ppermute | solution.py:244
  60.5 1.9 collective-permute-start.5
  62.4 0.0 collective-permute-done.4
  62.4 0.0 copy-start.6
  62.5 4.6 %collective-permute-start.6 = (bf16[2,64,1024]{2,1,0:T(8,128)(2,1)S(1)}, bf16[2,64,1024]{2,1,0:T(8,128)(2,1)}, u32[]{:S(2)}, u32[]{:S(2)}) collective-permute-start(bf16[2,64,1024]{2,1,0:T(8,128)(2,1)S(1)} %slice.57), channel_id=1, source_target_pairs={{0,3},{1,0},{2,1},{3,2},{4,7},{5,4},{6,5},{7,6},{8,11},{9,8},{10,9... | collective-permute-start | bytes 786440 | tf_op jit(solution)/shard_map/roots_to_slot_groups/ppermute | solution.py:244
  67.1 0.2 fusion.23.column_ref
  67.3 0.1 pad_maximum_fusion.refs_1_
  67.3 3.0 %collective-permute-done.5 = bf16[2,64,1024]{2,1,0:T(8,128)(2,1)S(1)} collective-permute-done((bf16[2,64,1024]{2,1,0:T(8,128)(2,1)S(1)}, bf16[2,64,1024]{2,1,0:T(8,128)(2,1)S(1)}, u32[]{:S(2)}, u32[]{:S(2)}) %collective-permute-start.5) | collective-permute-done | bytes 262176 | tf_op jit(solution)/shard_map/roots_to_slot_groups/ppermute | solution.py:244
  70.3 1.0 collective-permute-done.6
  71.3 0.6 all-to-all-done.1.tiles_ref
  71.9 2.1 %rows_of_held_blocks.1 = bf16[16,64,1024]{2,1,0:T(8,128)(2,1)} custom-call(s32[3]{0:T(128)S(1)} %fusion.23.column_ref, s32[3]{0:T(128)S(1)} %convert_element_type.9.used_ref, bf16[32,3,16,128]{3,2,1,0:T(8,128)(2,1)S(1)} %all-to-all-done.1.tiles_ref), custom_call_target="tpu_custom_call" | custom-call | bytes 4194304 | tf_op jit(solution)/shard_map/rows_of_held_blocks/pallas_call | solution.py:95
  73.9 6.8 %all-to-all-start.2 = ((bf16[16,64,1024]{2,1,0:T(8,128)(2,1)}), bf16[16,64,1024]{2,1,0:T(8,128)(2,1)S(1)}, u32[]{:S(2)}, u32[]{:S(2)}) async-start(bf16[16,64,1024]{2,1,0:T(8,128)(2,1)} %rows_of_held_blocks.1), calls=%async_computation.2 | async-start | bytes 4194304 | tf_op jit(solution)/shard_map/rows_of_held_blocks/all_to_all | solution.py:33
  80.8 0.0 copy-start.7
  80.8 0.1 pad_add_fusion.place_ref
  80.9 1.1 constant_dynamic-update-slice_fusion.3
  82.0 0.0 copy-done.7
  82.1 1.0 constant_dynamic-update-slice_fusion.refs_0_
  83.1 1.3 copy-done.2
  84.4 27.8 %all-to-all-done.2.refs_2_ = bf16[16,64,1024]{2,1,0:T(8,128)(2,1)S(1)} async-done(((bf16[16,64,1024]{2,1,0:T(8,128)(2,1)}), bf16[16,64,1024]{2,1,0:T(8,128)(2,1)S(1)}, u32[]{:S(2)}, u32[]{:S(2)}) %all-to-all-start.2) | async-done | bytes 2097184 | tf_op jit(solution)/shard_map/rows_of_held_blocks/all_to_all | solution.py:33
  112.1 1.6 copy-done.3
  113.7 3.6 %precondition.1 = bf16[16,80,256]{2,1,0:T(8,128)(2,1)S(1)} custom-call(s32[2]{0:T(128)S(1)} %pad_add_fusion.place_ref, bf16[16,64,1024]{2,1,0:T(8,128)(2,1)S(1)} %copy-done.3, bf16[4,64,1024]{2,1,0:T(8,128)(2,1)S(1)} %pad_maximum_fusion.refs_1_, bf16[16,64,1024]{2,1,0:T(8,128)(2,1)S(1)} %all-to-all-done.2.refs_2_), custom_call_target="tpu_custom_call" | custom-call | flops 2684354560 | bytes 6291456 | tf_op jit(solution)/shard_map/precondition/pallas_call | solution.py:156
  117.3 14.8 %all_to_all.30.back_ref = bf16[16,80,256]{2,1,0:T(8,128)(2,1)S(1)} all-to-all(bf16[16,80,256]{2,1,0:T(8,128)(2,1)S(1)} %precondition.1), channel_id=1, replica_groups=mesh['fsdp'=32,'tensor'=16] {'tensor'}, dimensions={0} | all-to-all | bytes 1310720 | tf_op jit(solution)/shard_map/step_to_gradient_rows/all_to_all | solution.py:33
  132.1 1.6 step_to_gradient_rows.1
  133.7 10.0 %all-to-all-start.4 = ((bf16[32,3,16,128]{3,2,1,0:T(8,128)(2,1)}), bf16[32,3,16,128]{3,2,1,0:T(8,128)(2,1)S(1)}, u32[]{:S(2)}, u32[]{:S(2)}) async-start(bf16[32,3,16,128]{3,2,1,0:T(8,128)(2,1)} %step_to_gradient_rows.1), calls=%async_computation.4 | async-start | bytes 786432 | tf_op jit(solution)/shard_map/step_to_gradient_rows/all_to_all | solution.py:247
  143.8 0.4 constant_dynamic-slice_fusion.3
  144.2 0.8 convolution_convert_fusion
  145.0 0.7 convolution_convert_fusion.1
  145.8 0.0 copy-start
  145.8 0.0 copy-start.1
  145.8 0.1 fusion.15
  145.9 2.0 %collective-permute-start.7 = (bf16[2,64,1024]{2,1,0:T(8,128)(2,1)S(1)}, bf16[2,64,1024]{2,1,0:T(8,128)(2,1)S(1)}, u32[]{:S(2)}, u32[]{:S(2)}) collective-permute-start(bf16[2,64,1024]{2,1,0:T(8,128)(2,1)S(1)} %get-tuple-element.63), channel_id=1, source_target_pairs={{0,4},{1,5},{2,6},{3,7},{4,8},{5,9},{6,10},{7,11},{8,12},{9,13},{1... | collective-permute-start | bytes 786440 | tf_op jit(solution)/shard_map/statistics/ppermute | solution.py:238
  148.0 3.7 %collective-permute-start.8 = (bf16[2,64,1024]{2,1,0:T(8,128)(2,1)S(1)}, bf16[2,64,1024]{2,1,0:T(8,128)(2,1)S(1)}, u32[]{:S(2)}, u32[]{:S(2)}) collective-permute-start(bf16[2,64,1024]{2,1,0:T(8,128)(2,1)S(1)} %get-tuple-element.64), channel_id=1, source_target_pairs={{0,8},{1,9},{2,10},{3,11},{4,12},{5,13},{6,14},{7,15},{8,0},{9,1},... | collective-permute-start | bytes 786440 | tf_op jit(solution)/shard_map/statistics/ppermute | solution.py:238
  151.7 1.9 collective-permute-start.9
  153.6 0.2 select_reduce_fusion.1.index_ref
  153.8 0.0 collective-permute-done.7.refs_1_
  153.8 7.8 %collective-permute-done.8.refs_2_ = bf16[2,64,1024]{2,1,0:T(8,128)(2,1)S(1)} collective-permute-done((bf16[2,64,1024]{2,1,0:T(8,128)(2,1)S(1)}, bf16[2,64,1024]{2,1,0:T(8,128)(2,1)S(1)}, u32[]{:S(2)}, u32[]{:S(2)}) %collective-permute-start.8) | collective-permute-done | bytes 262176 | tf_op jit(solution)/shard_map/statistics/ppermute | solution.py:238
  161.5 0.7 collective-permute-done.9.refs_3_
  162.2 9.4 %all-to-all-done.4 = bf16[32,3,16,128]{3,2,1,0:T(8,128)(2,1)S(1)} async-done(((bf16[32,3,16,128]{3,2,1,0:T(8,128)(2,1)}), bf16[32,3,16,128]{3,2,1,0:T(8,128)(2,1)S(1)}, u32[]{:S(2)}, u32[]{:S(2)}) %all-to-all-start.4) | async-done | bytes 393248 | tf_op jit(solution)/shard_map/step_to_gradient_rows/all_to_all | solution.py:247
  171.7 1.2 statistics.2
  172.9 4.0 %all-to-all-start.5 = ((bf16[32,16,128]{2,1,0:T(8,128)(2,1)}), bf16[32,16,128]{2,1,0:T(8,128)(2,1)S(1)}, u32[]{:S(2)}, u32[]{:S(2)}) async-start(bf16[32,16,128]{2,1,0:T(8,128)(2,1)} %statistics.2), calls=%async_computation.5 | async-start | bytes 262144 | tf_op jit(solution)/shard_map/statistics/all_to_all | solution.py:247
  176.9 1.9 %statistics.3 = (f32[3,64,1024]{2,1,0:T(8,128)}, f32[3,64,1024]{2,1,0:T(8,128)}) custom-call(s32[2]{0:T(128)S(1)} %pad_add_fusion.place_ref, f32[3,64,1024]{2,1,0:T(8,128)S(1)} %copy-done, f32[3,64,1024]{2,1,0:T(8,128)S(1)} %copy-done.1, bf16[2,64,1024]{2,1,0:T(8,128)(2,1)S(1)} %get-tuple-element.48.refs_0_, ...), custom_call_target="tpu_custom_call" | custom-call | bytes 4194304 | tf_op jit(solution)/shard_map/statistics/pallas_call | solution.py:353
  178.9 14.2 %all-to-all-done.5.tiles_ref = bf16[32,16,128]{2,1,0:T(8,128)(2,1)S(1)} async-done(((bf16[32,16,128]{2,1,0:T(8,128)(2,1)}), bf16[32,16,128]{2,1,0:T(8,128)(2,1)S(1)}, u32[]{:S(2)}, u32[]{:S(2)}) %all-to-all-start.5) | async-done | bytes 131104 | tf_op jit(solution)/shard_map/statistics/all_to_all | solution.py:247
  193.1 0.7 update.1
  (25 shorter events, 0.3 us)
Async XLA Ops:
  0.6 28.7 %copy-start.8 = (s32[4,8]{1,0:T(4,128)S(1)}, s32[4,8]{1,0:T(4,128)}, u32[]{:S(2)}) copy-start(s32[4,8]{1,0:T(4,128)} %param.7) | copy-start | bytes 388
  0.7 0.9 copy-start.4
  2.2 32.6 %all-to-all-start = ((bf16[32,16,128]{2,1,0:T(8,128)(2,1)}), bf16[32,16,128]{2,1,0:T(8,128)(2,1)S(1)}, u32[]{:S(2)}, u32[]{:S(2)}) async-start(bf16[32,16,128]{2,1,0:T(8,128)(2,1)} %gradient_spread.1), calls=%async_computation | async-start | bytes 262144 | tf_op jit(solution)/shard_map/gradient_spread/all_to_all | solution.py:247
  20.5 23.4 %collective-permute-start.2 = (bf16[2,64,1024]{2,1,0:T(8,128)(2,1)S(1)}, bf16[2,64,1024]{2,1,0:T(8,128)(2,1)S(1)}, u32[]{:S(2)}, u32[]{:S(2)}) collective-permute-start(bf16[2,64,1024]{2,1,0:T(8,128)(2,1)S(1)} %get-tuple-element.68), channel_id=1, source_target_pairs={{4,0},{5,1},{6,2},{7,3},{8,4},{9,5},{10,6},{11,7},{12,8},{13,9},{1... | collective-permute-start | bytes 786440 | tf_op jit(solution)/shard_map/roots_to_slot_groups/ppermute | solution.py:238
  21.8 22.1 %collective-permute-start.1 = (bf16[2,64,1024]{2,1,0:T(8,128)(2,1)S(1)}, bf16[2,64,1024]{2,1,0:T(8,128)(2,1)S(1)}, u32[]{:S(2)}, u32[]{:S(2)}) collective-permute-start(bf16[2,64,1024]{2,1,0:T(8,128)(2,1)S(1)} %get-tuple-element.67), channel_id=1, source_target_pairs={{0,8},{1,9},{2,10},{3,11},{8,0},{9,1},{10,2},{11,3},{12,4},{13,5},... | collective-permute-start | bytes 786440 | tf_op jit(solution)/shard_map/roots_to_slot_groups/ppermute | solution.py:238
  27.4 16.6 %collective-permute-start = (bf16[2,64,1024]{2,1,0:T(8,128)(2,1)S(1)}, bf16[2,64,1024]{2,1,0:T(8,128)(2,1)S(1)}, u32[]{:S(2)}, u32[]{:S(2)}) collective-permute-start(bf16[2,64,1024]{2,1,0:T(8,128)(2,1)S(1)} %get-tuple-element.66), channel_id=1, source_target_pairs={{0,4},{1,5},{2,6},{3,7},{4,8},{5,9},{6,10},{7,11},{12,0},{13,1},{1... | collective-permute-start | bytes 786440 | tf_op jit(solution)/shard_map/roots_to_slot_groups/ppermute | solution.py:238
  36.2 35.6 %all-to-all-start.1 = ((bf16[32,3,16,128]{3,2,1,0:T(8,128)(2,1)}), bf16[32,3,16,128]{3,2,1,0:T(8,128)(2,1)S(1)}, u32[]{:S(2)}, u32[]{:S(2)}) async-start(bf16[32,3,16,128]{3,2,1,0:T(8,128)(2,1)} %bitcast.3), calls=%async_computation.1 | async-start | bytes 786432 | tf_op jit(solution)/shard_map/gradient_to_owners/all_to_all | solution.py:247
  44.1 16.4 %collective-permute-start.3 = (bf16[4,64,1024]{2,1,0:T(8,128)(2,1)S(1)}, bf16[4,64,1024]{2,1,0:T(8,128)(2,1)S(1)}, u32[]{:S(2)}, u32[]{:S(2)}) collective-permute-start(bf16[4,64,1024]{2,1,0:T(8,128)(2,1)S(1)} %pad_maximum_fusion.1), channel_id=1, source_target_pairs={{0,1},{1,2},{2,3},{3,0},{4,5},{5,6},{6,7},{7,4},{8,9},{9,10},{10,1... | collective-permute-start | bytes 1572872 | tf_op jit(solution)/shard_map/roots_to_slot_groups/ppermute | solution.py:244
  47.2 15.2 %collective-permute-start.4 = (bf16[4,64,1024]{2,1,0:T(8,128)(2,1)S(1)}, bf16[4,64,1024]{2,1,0:T(8,128)(2,1)S(1)}, u32[]{:S(2)}, u32[]{:S(2)}) collective-permute-start(bf16[4,64,1024]{2,1,0:T(8,128)(2,1)S(1)} %pad_maximum_fusion.1), channel_id=1, source_target_pairs={{0,3},{1,0},{2,1},{3,2},{4,7},{5,4},{6,5},{7,6},{8,11},{9,8},{10,9... | collective-permute-start | bytes 1572872 | tf_op jit(solution)/shard_map/roots_to_slot_groups/ppermute | solution.py:244
  60.5 6.6 %copy-start.5 = (bf16[4,64,1024]{2,1,0:T(8,128)(2,1)}, bf16[4,64,1024]{2,1,0:T(8,128)(2,1)S(1)}, u32[]{:S(2)}) copy-start(bf16[4,64,1024]{2,1,0:T(8,128)(2,1)S(1)} %collective-permute-done.3) | copy-start | bytes 1572868
  60.5 9.9 %collective-permute-start.5 = (bf16[2,64,1024]{2,1,0:T(8,128)(2,1)S(1)}, bf16[2,64,1024]{2,1,0:T(8,128)(2,1)S(1)}, u32[]{:S(2)}, u32[]{:S(2)}) collective-permute-start(bf16[2,64,1024]{2,1,0:T(8,128)(2,1)S(1)} %slice.56), channel_id=1, source_target_pairs={{0,1},{1,2},{2,3},{3,0},{4,5},{5,6},{6,7},{7,4},{8,9},{9,10},{10,1... | collective-permute-start | bytes 786440 | tf_op jit(solution)/shard_map/roots_to_slot_groups/ppermute | solution.py:244
  62.4 11.5 %copy-start.6 = (bf16[4,64,1024]{2,1,0:T(8,128)(2,1)}, bf16[4,64,1024]{2,1,0:T(8,128)(2,1)S(1)}, u32[]{:S(2)}) copy-start(bf16[4,64,1024]{2,1,0:T(8,128)(2,1)S(1)} %collective-permute-done.4) | copy-start | bytes 1572868
  62.5 8.8 %collective-permute-start.6 = (bf16[2,64,1024]{2,1,0:T(8,128)(2,1)S(1)}, bf16[2,64,1024]{2,1,0:T(8,128)(2,1)}, u32[]{:S(2)}, u32[]{:S(2)}) collective-permute-start(bf16[2,64,1024]{2,1,0:T(8,128)(2,1)S(1)} %slice.57), channel_id=1, source_target_pairs={{0,3},{1,0},{2,1},{3,2},{4,7},{5,4},{6,5},{7,6},{8,11},{9,8},{10,9... | collective-permute-start | bytes 786440 | tf_op jit(solution)/shard_map/roots_to_slot_groups/ppermute | solution.py:244
  73.9 38.2 %all-to-all-start.2 = ((bf16[16,64,1024]{2,1,0:T(8,128)(2,1)}), bf16[16,64,1024]{2,1,0:T(8,128)(2,1)S(1)}, u32[]{:S(2)}, u32[]{:S(2)}) async-start(bf16[16,64,1024]{2,1,0:T(8,128)(2,1)} %rows_of_held_blocks.1), calls=%async_computation.2 | async-start | bytes 4194304 | tf_op jit(solution)/shard_map/rows_of_held_blocks/all_to_all | solution.py:33
  80.8 1.2 copy-start.7
  83.1 1.3 copy-start.2
  112.1 1.6 copy-start.3
  133.7 38.0 %all-to-all-start.4 = ((bf16[32,3,16,128]{3,2,1,0:T(8,128)(2,1)}), bf16[32,3,16,128]{3,2,1,0:T(8,128)(2,1)S(1)}, u32[]{:S(2)}, u32[]{:S(2)}) async-start(bf16[32,3,16,128]{3,2,1,0:T(8,128)(2,1)} %step_to_gradient_rows.1), calls=%async_computation.4 | async-start | bytes 786432 | tf_op jit(solution)/shard_map/step_to_gradient_rows/all_to_all | solution.py:247
  145.8 31.1 %copy-start = (f32[3,64,1024]{2,1,0:T(8,128)S(1)}, f32[3,64,1024]{2,1,0:T(8,128)}, u32[]{:S(2)}) copy-start(f32[3,64,1024]{2,1,0:T(8,128)} %left_ref.1) | copy-start | bytes 2359300
  145.8 31.1 %copy-start.1 = (f32[3,64,1024]{2,1,0:T(8,128)S(1)}, f32[3,64,1024]{2,1,0:T(8,128)}, u32[]{:S(2)}) copy-start(f32[3,64,1024]{2,1,0:T(8,128)} %right_ref.1) | copy-start | bytes 2359300
  145.9 7.9 %collective-permute-start.7 = (bf16[2,64,1024]{2,1,0:T(8,128)(2,1)S(1)}, bf16[2,64,1024]{2,1,0:T(8,128)(2,1)S(1)}, u32[]{:S(2)}, u32[]{:S(2)}) collective-permute-start(bf16[2,64,1024]{2,1,0:T(8,128)(2,1)S(1)} %get-tuple-element.63), channel_id=1, source_target_pairs={{0,4},{1,5},{2,6},{3,7},{4,8},{5,9},{6,10},{7,11},{8,12},{9,13},{1... | collective-permute-start | bytes 786440 | tf_op jit(solution)/shard_map/statistics/ppermute | solution.py:238
  148.0 13.6 %collective-permute-start.8 = (bf16[2,64,1024]{2,1,0:T(8,128)(2,1)S(1)}, bf16[2,64,1024]{2,1,0:T(8,128)(2,1)S(1)}, u32[]{:S(2)}, u32[]{:S(2)}) collective-permute-start(bf16[2,64,1024]{2,1,0:T(8,128)(2,1)S(1)} %get-tuple-element.64), channel_id=1, source_target_pairs={{0,8},{1,9},{2,10},{3,11},{4,12},{5,13},{6,14},{7,15},{8,0},{9,1},... | collective-permute-start | bytes 786440 | tf_op jit(solution)/shard_map/statistics/ppermute | solution.py:238
  151.7 10.6 %collective-permute-start.9 = (bf16[2,64,1024]{2,1,0:T(8,128)(2,1)S(1)}, bf16[2,64,1024]{2,1,0:T(8,128)(2,1)S(1)}, u32[]{:S(2)}, u32[]{:S(2)}) collective-permute-start(bf16[2,64,1024]{2,1,0:T(8,128)(2,1)S(1)} %get-tuple-element.61), channel_id=1, source_target_pairs={{0,12},{1,13},{2,14},{3,15},{4,0},{5,1},{6,2},{7,3},{8,4},{9,5},{1... | collective-permute-start | bytes 786440 | tf_op jit(solution)/shard_map/statistics/ppermute | solution.py:238
  172.9 20.2 %all-to-all-start.5 = ((bf16[32,16,128]{2,1,0:T(8,128)(2,1)}), bf16[32,16,128]{2,1,0:T(8,128)(2,1)S(1)}, u32[]{:S(2)}, u32[]{:S(2)}) async-start(bf16[32,16,128]{2,1,0:T(8,128)(2,1)} %statistics.2), calls=%async_computation.5 | async-start | bytes 262144 | tf_op jit(solution)/shard_map/statistics/all_to_all | solution.py:247

commit v3 on v2

--- a/solution.py
+++ b/solution.py
@@ -12,6 +12,7 @@
 TAIL = 16
 ROWS = 16
 LANES = 128
+CORES = 2
 VMEM = pl.BlockSpec(memory_space=pltpu.VMEM)
 ANY = pl.BlockSpec(memory_space=pl.ANY)
 SMEM = pl.BlockSpec(memory_space=pltpu.SMEM)
@@ -121,7 +122,9 @@
     left_ref, right_ref, block_ref, out_ref = refs
     y, x = place_ref[0], place_ref[1]
     places, height, block_side = block_ref.shape
-    width = out_ref.shape[2]
+    width = block_side // side
+    cores = out_ref.shape[0] // places
+    narrow = width // side
     block = block_ref[...].reshape(block_side, block_side)
     right = jnp.concatenate([right_ref[around(y, at, side)] for at in range(side)], axis=0)
     power = jnp.zeros((1, width), jnp.float32)
@@ -133,19 +136,28 @@
         )
         power += jnp.sum(product * product, axis=0, keepdims=True)
         product = product.astype(jnp.bfloat16)
-        for at, (row, column) in enumerate(origins[begin : begin + side]):
-            place = around(y, row, side) * side + around(x, column, side)
-            out_ref[place, pl.ds(0, height), :] = product[at * height : (at + 1) * height]
+        for core in range(cores):
+            share = jnp.concatenate(
+                [
+                    product[:, part * narrow : (part + 1) * narrow]
+                    for part in range(core, side, cores)
+                ],
+                axis=1,
+            )
+            for at, (row, column) in enumerate(origins[begin : begin + side]):
+                place = core * places + around(y, row, side) * side + around(x, column, side)
+                out_ref[place, pl.ds(0, height), :] = share[at * height : (at + 1) * height]
     share = places // side
     own = block_ref[pl.ds(x * share, share)].astype(jnp.float32).reshape(width, block_side)
     own = jnp.sum(own * own, axis=0, keepdims=True)
-    grad = sum(own[:, at * width : (at + 1) * width] for at in range(side))
-    number = lax.broadcasted_iota(jnp.int32, (TAIL, width), 0)
-    tail = jnp.zeros((TAIL, width), jnp.float32)
+    grad = sum(own[:, at : at + LANES] for at in range(0, block_side, LANES))
+    power = sum(power[:, at : at + LANES] for at in range(0, width, LANES))
+    number = lax.broadcasted_iota(jnp.int32, (TAIL, LANES), 0)
+    tail = jnp.zeros((TAIL, LANES), jnp.float32)
     for at, line in enumerate(three_parts(power) + three_parts(grad)):
         tail = jnp.where(number == at, line.astype(jnp.float32), tail)
     tail = tail.astype(jnp.bfloat16)
-    for place in range(places):
+    for place in range(places * cores):
         out_ref[place, pl.ds(height, TAIL), :] = tail
 
 
@@ -155,7 +167,7 @@
     width = block_side // side
     return pl.pallas_call(
         functools.partial(precondition_kernel, side, origins),
-        out_shape=jax.ShapeDtypeStruct((places, height + TAIL, width), jnp.bfloat16),
+        out_shape=jax.ShapeDtypeStruct((places * CORES, height + TAIL, LANES), jnp.bfloat16),
         in_specs=[SMEM] + [VMEM] * 3,
         out_specs=VMEM,
         compiler_params=pltpu.CompilerParams(vmem_limit_bytes=32 * 2**20),
@@ -165,11 +177,14 @@
 
 def steps_kernel(side, column_ref, back_ref, out_ref):
     height = back_ref.shape[1] - TAIL
-    piece = back_ref.shape[2] // side
-    tiles = out_ref.shape[0] // side
-    for slot in range(column_ref.shape[0]):
+    tiles = out_ref.shape[0] // CORES
+    narrow = back_ref.shape[2] // CORES
+    slots = column_ref.shape[0]
+    for held in range(slots):
+        core, slot = held // (slots // CORES), held % (slots // CORES)
+        first = core * (back_ref.shape[0] // CORES) + slot * side
         sums = sum(
-            back_ref[slot * side + member, pl.ds(height, TAIL), :].astype(jnp.float32)
+            back_ref[first + member, pl.ds(height, TAIL), :].astype(jnp.float32)
             for member in range(side)
         )
         sums = jnp.sum(sums, axis=1, keepdims=True)
@@ -177,31 +192,30 @@
         grad = jnp.sum(sums[3:6], axis=0, keepdims=True)
         scale = -STEP * jnp.sqrt(grad) * lax.rsqrt(power + EPS)
         rows_of = [
-            (
-                scale * back_ref[slot * side + member, pl.ds(0, height), :].astype(jnp.float32)
-            ).astype(jnp.bfloat16)
+            (scale * back_ref[first + member, pl.ds(0, height), :].astype(jnp.float32)).astype(
+                jnp.bfloat16
+            )
             for member in range(side)
         ]
-        for part in range(side):
-            group = lax.rem(column_ref[slot] + part, side)
+        for half in range(CORES):
+            group = lax.rem(column_ref[held] + half, CORES)
             chunk = jnp.concatenate(
-                [rows[:, part * piece : (part + 1) * piece] for rows in rows_of], axis=1
+                [rows[:, half * narrow : (half + 1) * narrow] for rows in rows_of], axis=1
             )
             for tile in range(tiles):
                 rows, lanes = tile_of(tile)
-                out_ref[group * tiles + tile, slot] = chunk[
+                out_ref[group * tiles + tile, held] = chunk[
                     rows.start : rows.start + ROWS, lanes.start : lanes.start + LANES
                 ]
 
 
-def update_kernel(part_ref, tiles_ref, out_ref):
-    count = out_ref.shape[0]
-    tiles = tiles_ref.shape[0] // count
-    for column in range(count):
-        group = lax.rem(column + part_ref[0], count)
+def update_kernel(half_ref, tiles_ref, out_ref):
+    tiles = tiles_ref.shape[0] // CORES
+    for column in range(out_ref.shape[0]):
+        group = lax.rem(column + half_ref[0], CORES)
         for tile in range(tiles):
             rows, lanes = tile_of(tile)
-            out_ref[column, rows, lanes] = tiles_ref[group * tiles + tile]
+            out_ref[column, rows, lanes] = tiles_ref[group * tiles + tile, column // CORES]
 
 
 def statistics_kernel(side, place_ref, left_ref, right_ref, *refs):
@@ -246,6 +260,26 @@
     def over_rows(value):
         return lax.all_to_all(value, "fsdp", split_axis=0, concat_axis=0, tiled=True)
 
+    chips = fsdp_count // CORES
+
+    def along_z(value):
+        rings = [[chip * CORES + core for chip in range(chips)] for core in range(CORES)]
+        return lax.all_to_all(
+            value, "fsdp", split_axis=0, concat_axis=0, tiled=True, axis_index_groups=rings
+        )
+
+    def over_chip_planes(value):
+        count = CORES * tensor_count
+        planes = [[chip * count + member for member in range(count)] for chip in range(chips)]
+        return lax.all_to_all(
+            value,
+            ("fsdp", "tensor"),
+            split_axis=0,
+            concat_axis=0,
+            tiled=True,
+            axis_index_groups=planes,
+        )
+
     part = (fsdp_index % side).astype(jnp.int32).reshape(1)
     group = fsdp_index // (fsdp_count // col_blocks)
 
@@ -272,11 +306,19 @@
         mine = entries[:, None] == (fsdp_index * capacity + jnp.arange(capacity))[None, :]
         used = jnp.any(mine, axis=0).astype(jnp.int32)
         column_of = jnp.sum(jnp.where(mine, column_flat[:, None], 0), axis=0).astype(jnp.int32)
-        homes = jnp.arange(fsdp_count)
-        wanted = (group - homes % side + side) % side * row_blocks + homes // side
+        chip = fsdp_index // CORES
+        ours = (chip * CORES * capacity + jnp.arange(CORES * capacity))[None, :]
+        columns_here = jnp.sum(
+            jnp.where(entries[:, None] == ours, column_flat[:, None], 0), axis=0
+        ).astype(jnp.int32)
+        homes = jnp.arange(chips)[:, None]
+        turn = (chip // (chips // CORES) - homes % CORES + CORES) % CORES
+        wanted = CORES * jnp.arange(col_blocks // CORES)[None, :] + turn
+        wanted = (wanted * row_blocks + homes // CORES).reshape(-1)
         backward = jnp.sum(
             jnp.where(wanted[:, None] == numbers[None, :], entries[None, :], 0), axis=1
         ).astype(jnp.int32)
+        half_here = (chip % CORES).astype(jnp.int32).reshape(1)
 
     with jax.named_scope("gradient_to_owners"):
         sent = pick(forward, spread).reshape(fsdp_count, capacity, ROWS, LANES)
@@ -316,19 +358,8 @@
         leaving = precondition(place, left, origins, right_rows, block)
 
     with jax.named_scope("step_to_gradient_rows"):
-        back = exchange(leaving)
-        steps = pl.pallas_call(
-            functools.partial(steps_kernel, side),
-            out_shape=jax.ShapeDtypeStruct((fsdp_count, capacity, ROWS, LANES), jnp.bfloat16),
-            in_specs=[SMEM, VMEM],
-            out_specs=VMEM,
-            compiler_params=LIMIT,
-            cost_estimate=cost(0, 2 * 2**20),
-        )(column_of, back)
-        passing = over_rows(steps).reshape(fsdp_count * capacity, ROWS, LANES)
-
-    with jax.named_scope("statistics"):
-        block, steps = lax.optimization_barrier((block, steps))
+        back = over_chip_planes(leaving)
+        block, leaving = lax.optimization_barrier((block, leaving))
         block = block.reshape(block_side, block_side)
         own_rows = lax.dynamic_index_in_dim(
             block.reshape(side, side, local_height, block_side), x, 1, keepdims=False
@@ -344,12 +375,30 @@
         right_term = jnp.einsum("ja,jk->ak", own_columns, block, preferred_element_type=jnp.float32)
         terms = jnp.stack([left_term.astype(jnp.bfloat16), right_term.astype(jnp.bfloat16)])
         terms = terms.reshape(2, side, local_height, block_side)
-        arrived = []
-        for step in range(side):
-            own = lax.dynamic_index_in_dim(terms, (y + step) % side, 1, keepdims=False)
-            arrived.append(along_y(own, step, capacity, side) if step else own)
+        terms = [
+            lax.dynamic_index_in_dim(terms, (y + step) % side, 1, keepdims=False)
+            for step in range(side)
+        ]
+        back, *terms = lax.optimization_barrier((back, *terms))
+        steps = pl.pallas_call(
+            functools.partial(steps_kernel, side),
+            out_shape=jax.ShapeDtypeStruct((chips, CORES * capacity, ROWS, LANES), jnp.bfloat16),
+            in_specs=[SMEM, VMEM],
+            out_specs=VMEM,
+            compiler_params=LIMIT,
+            cost_estimate=cost(0, 2 * 2**20),
+        )(columns_here, back)
+        steps, *terms = lax.optimization_barrier((steps, *terms))
+        passing = along_z(steps).reshape(fsdp_count * capacity, ROWS, LANES)
+
+    with jax.named_scope("statistics"):
+        arrived = terms[:1] + [
+            along_y(terms[step], step, capacity, side) for step in range(1, side)
+        ]
         passing, *arrived = lax.optimization_barrier((passing, *arrived))
-        returned = over_rows(pick(backward, passing))
+        returned = along_z(
+            pick(backward, passing).reshape(chips, col_blocks // CORES, ROWS, LANES)
+        )
         left_updated, right_updated = pl.pallas_call(
             functools.partial(statistics_kernel, side),
             out_shape=(
@@ -373,7 +422,7 @@
             out_specs=VMEM,
             compiler_params=LIMIT,
             cost_estimate=cost(0, 2**20),
-        )(part, returned)
+        )(half_here, returned)
     return (left_updated, right_updated, update)
 
 

time: 195 us -> 191 us (0.979)
  blocking collectives: 14.8 us -> 0 us
  starting transfers between devices: 74.7 us -> 85.9 us
  waiting for transfers between devices: 79.2 us -> 75 us
    all_to_all x0 -> x3, starting transfers between devices: none -> 24.6 us  [the longest x2 19.2 us: along_z(): lax.all_to_all(value, 'fsdp', split_axis=0, concat_axis=0, tiled=True, ax...]
    all_to_all x4 -> x2, waiting for transfers between devices: 29.3 us -> 5.64 us  [over_rows(): lax.all_to_all(value, 'fsdp', split_axis=0, concat_axis=0, tiled=True)]
    all_to_all x0 -> x3, waiting for transfers between devices: none -> 19.8 us  [the longest x2 10.5 us: along_z(): lax.all_to_all(value, 'fsdp', split_axis=0, concat_axis=0, tiled=True, ax...]
    all_to_all x1 -> x0, blocking collectives: 14.8 us -> none  [exchange(): lax.all_to_all(pieces, 'tensor', split_axis=0, concat_axis=0, tiled=True)]
    all_to_all x4 -> x2, starting transfers between devices: 38.4 us -> 24.4 us  [over_rows(): lax.all_to_all(value, 'fsdp', split_axis=0, concat_axis=0, tiled=True)]
  transfers between devices with their start and end apart: 15 -> 16, of which waited for: 10 -> 11; matrix products, arithmetic and copies ran while one was open for 4% -> 4% of each run, Pallas kernels for 2% -> 2%
where the time goes in v3:
time: 191 us; the launch traced here: 188 us
  starting transfers between devices  85.9 us (45%)
  waiting for transfers between devices  75 us (39%)
  Pallas kernels  14 us (7%)
  local copies, waits for them, and re-layouts  6.69 us (4%)
  other arithmetic  3.64 us (2%)
    all_to_all x1, waiting for transfers between devices, exchange(): lax.all_to_all(pieces, 'tensor', split_axis=0, concat_axis=0, tiled=True)  27.5 us
    all_to_all x2, starting transfers between devices, over_rows(): lax.all_to_all(value, 'fsdp', split_axis=0, concat_axis=0, tiled=True)  24.4 us
    all_to_all x2, starting transfers between devices, along_z(): lax.all_to_all(value, 'fsdp', split_axis=0, concat_axis=0, tiled=True, ax...  19.2 us
    ppermute x6, starting transfers between devices, along_y(): return lax.ppermute(value, 'tensor', pairs)  17.1 us
    ppermute x4, waiting for transfers between devices, along_x(): return lax.ppermute(value, 'tensor', pairs)  13.6 us
    ppermute x4, starting transfers between devices, along_x(): return lax.ppermute(value, 'tensor', pairs)  13 us
    all_to_all x2, waiting for transfers between devices, along_z(): lax.all_to_all(value, 'fsdp', split_axis=0, concat_axis=0, tiled=True, ax...  10.5 us
    all_to_all x1, waiting for transfers between devices, over_chip_planes(): lax.all_to_all(value, ('fsdp', 'tensor'), split_axis=0, concat_axis=0, ti...  9.33 us
  transfers between devices with their start and end apart: 16, of which 11 were waited for; matrix products, arithmetic and copies ran while one was open for 4% of the time, Pallas kernels for 2%

profile of v3, /device:TPU:1, one launch (start us, length us, event | category | flops | bytes accessed | tf_op | source)
XLA Modules:
  0.0 188.1 jit_solution(4685606277987527156)
XLA Ops:
  0.7 0.9 copy-done.4
  1.6 0.7 gradient_spread.1
  2.2 16.7 %all-to-all-start = ((bf16[32,16,128]{2,1,0:T(8,128)(2,1)}), bf16[32,16,128]{2,1,0:T(8,128)(2,1)S(1)}, u32[]{:S(2)}, u32[]{:S(2)}) async-start(bf16[32,16,128]{2,1,0:T(8,128)(2,1)} %gradient_spread.1), calls=%async_computation | async-start | bytes 262144 | tf_op jit(solution)/shard_map/gradient_spread/all_to_all | solution.py:261
  19.1 1.4 fusion.9
  20.5 1.3 collective-permute-start.2
  21.8 5.6 %collective-permute-start.1 = (bf16[2,64,1024]{2,1,0:T(8,128)(2,1)S(1)}, bf16[2,64,1024]{2,1,0:T(8,128)(2,1)S(1)}, u32[]{:S(2)}, u32[]{:S(2)}) collective-permute-start(bf16[2,64,1024]{2,1,0:T(8,128)(2,1)S(1)} %get-tuple-element.87), channel_id=1, source_target_pairs={{0,8},{1,9},{2,10},{3,11},{8,0},{9,1},{10,2},{11,3},{12,4},{13,5},... | collective-permute-start | bytes 786440 | tf_op jit(solution)/shard_map/roots_to_slot_groups/ppermute | solution.py:252
  27.4 1.9 %collective-permute-start = (bf16[2,64,1024]{2,1,0:T(8,128)(2,1)S(1)}, bf16[2,64,1024]{2,1,0:T(8,128)(2,1)S(1)}, u32[]{:S(2)}, u32[]{:S(2)}) collective-permute-start(bf16[2,64,1024]{2,1,0:T(8,128)(2,1)S(1)} %get-tuple-element.86), channel_id=1, source_target_pairs={{0,4},{1,5},{2,6},{3,7},{4,8},{5,9},{6,10},{7,11},{12,0},{13,1},{1... | collective-permute-start | bytes 786440 | tf_op jit(solution)/shard_map/roots_to_slot_groups/ppermute | solution.py:252
  29.3 0.1 reshape.211
  29.4 0.2 select_reduce_fusion.2
  29.7 0.1 select_reduce_fusion.index_ref
  29.8 5.1 %all-to-all-done.tiles_ref = bf16[32,16,128]{2,1,0:T(8,128)(2,1)S(1)} async-done(((bf16[32,16,128]{2,1,0:T(8,128)(2,1)}), bf16[32,16,128]{2,1,0:T(8,128)(2,1)S(1)}, u32[]{:S(2)}, u32[]{:S(2)}) %all-to-all-start) | async-done | bytes 131104 | tf_op jit(solution)/shard_map/gradient_spread/all_to_all | solution.py:261
  34.8 1.4 gradient_to_owners.1
  36.2 7.7 %all-to-all-start.1 = ((bf16[32,3,16,128]{3,2,1,0:T(8,128)(2,1)}), bf16[32,3,16,128]{3,2,1,0:T(8,128)(2,1)S(1)}, u32[]{:S(2)}, u32[]{:S(2)}) async-start(bf16[32,3,16,128]{3,2,1,0:T(8,128)(2,1)} %bitcast.3), calls=%async_computation.1 | async-start | bytes 786432 | tf_op jit(solution)/shard_map/gradient_to_owners/all_to_all | solution.py:261
  43.9 0.0 collective-permute-done.2
  43.9 0.0 collective-permute-done.1
  44.0 0.0 collective-permute-done
  44.0 0.1 pad_maximum_fusion.1
  44.1 3.1 %collective-permute-start.3 = (bf16[4,64,1024]{2,1,0:T(8,128)(2,1)S(1)}, bf16[4,64,1024]{2,1,0:T(8,128)(2,1)S(1)}, u32[]{:S(2)}, u32[]{:S(2)}) collective-permute-start(bf16[4,64,1024]{2,1,0:T(8,128)(2,1)S(1)} %pad_maximum_fusion.1), channel_id=1, source_target_pairs={{0,1},{1,2},{2,3},{3,0},{4,5},{5,6},{6,7},{7,4},{8,9},{9,10},{10,1... | collective-permute-start | bytes 1572872 | tf_op jit(solution)/shard_map/roots_to_slot_groups/ppermute | solution.py:258
  47.2 3.4 %collective-permute-start.4 = (bf16[4,64,1024]{2,1,0:T(8,128)(2,1)S(1)}, bf16[4,64,1024]{2,1,0:T(8,128)(2,1)S(1)}, u32[]{:S(2)}, u32[]{:S(2)}) collective-permute-start(bf16[4,64,1024]{2,1,0:T(8,128)(2,1)S(1)} %pad_maximum_fusion.1), channel_id=1, source_target_pairs={{0,3},{1,0},{2,1},{3,2},{4,7},{5,4},{6,5},{7,6},{8,11},{9,8},{10,9... | collective-permute-start | bytes 1572872 | tf_op jit(solution)/shard_map/roots_to_slot_groups/ppermute | solution.py:258
  50.6 0.2 compare_reduce_fusion
  50.8 9.7 %collective-permute-done.3 = bf16[4,64,1024]{2,1,0:T(8,128)(2,1)S(1)} collective-permute-done((bf16[4,64,1024]{2,1,0:T(8,128)(2,1)S(1)}, bf16[4,64,1024]{2,1,0:T(8,128)(2,1)S(1)}, u32[]{:S(2)}, u32[]{:S(2)}) %collective-permute-start.3) | collective-permute-done | bytes 524320 | tf_op jit(solution)/shard_map/roots_to_slot_groups/ppermute | solution.py:258
  60.5 1.9 %collective-permute-start.5 = (bf16[2,64,1024]{2,1,0:T(8,128)(2,1)S(1)}, bf16[2,64,1024]{2,1,0:T(8,128)(2,1)S(1)}, u32[]{:S(2)}, u32[]{:S(2)}) collective-permute-start(bf16[2,64,1024]{2,1,0:T(8,128)(2,1)S(1)} %slice.56), channel_id=1, source_target_pairs={{0,1},{1,2},{2,3},{3,0},{4,5},{5,6},{6,7},{7,4},{8,9},{9,10},{10,1... | collective-permute-start | bytes 786440 | tf_op jit(solution)/shard_map/roots_to_slot_groups/ppermute | solution.py:258
  62.4 0.0 copy-start.6
  62.5 4.6 %collective-permute-start.6 = (bf16[2,64,1024]{2,1,0:T(8,128)(2,1)S(1)}, bf16[2,64,1024]{2,1,0:T(8,128)(2,1)}, u32[]{:S(2)}, u32[]{:S(2)}) collective-permute-start(bf16[2,64,1024]{2,1,0:T(8,128)(2,1)S(1)} %slice.57), channel_id=1, source_target_pairs={{0,3},{1,0},{2,1},{3,2},{4,7},{5,4},{6,5},{7,6},{8,11},{9,8},{10,9... | collective-permute-start | bytes 786440 | tf_op jit(solution)/shard_map/roots_to_slot_groups/ppermute | solution.py:258
  67.1 0.2 fusion.23.column_ref
  67.3 0.1 pad_maximum_fusion.refs_1_
  67.3 3.0 %collective-permute-done.5 = bf16[2,64,1024]{2,1,0:T(8,128)(2,1)S(1)} collective-permute-done((bf16[2,64,1024]{2,1,0:T(8,128)(2,1)S(1)}, bf16[2,64,1024]{2,1,0:T(8,128)(2,1)S(1)}, u32[]{:S(2)}, u32[]{:S(2)}) %collective-permute-start.5) | collective-permute-done | bytes 262176 | tf_op jit(solution)/shard_map/roots_to_slot_groups/ppermute | solution.py:258
  70.3 1.0 collective-permute-done.6
  71.3 0.6 all-to-all-done.1.tiles_ref
  71.9 2.1 %rows_of_held_blocks.1 = bf16[16,64,1024]{2,1,0:T(8,128)(2,1)} custom-call(s32[3]{0:T(128)S(1)} %fusion.23.column_ref, s32[3]{0:T(128)S(1)} %convert_element_type.9.used_ref, bf16[32,3,16,128]{3,2,1,0:T(8,128)(2,1)S(1)} %all-to-all-done.1.tiles_ref), custom_call_target="tpu_custom_call" | custom-call | bytes 4194304 | tf_op jit(solution)/shard_map/rows_of_held_blocks/pallas_call | solution.py:96
  73.9 6.8 %all-to-all-start.2 = ((bf16[16,64,1024]{2,1,0:T(8,128)(2,1)}), bf16[16,64,1024]{2,1,0:T(8,128)(2,1)S(1)}, u32[]{:S(2)}, u32[]{:S(2)}) async-start(bf16[16,64,1024]{2,1,0:T(8,128)(2,1)} %rows_of_held_blocks.1), calls=%async_computation.2 | async-start | bytes 4194304 | tf_op jit(solution)/shard_map/rows_of_held_blocks/all_to_all | solution.py:34
  80.8 0.0 copy-start.7
  80.8 0.1 pad_add_fusion.place_ref
  80.9 0.2 select_reduce_fusion.3.column_ref
  81.2 1.1 constant_dynamic-update-slice_fusion.3
  82.3 1.0 constant_dynamic-update-slice_fusion.refs_0_
  83.3 1.3 copy-done.2
  84.6 27.5 %all-to-all-done.2.refs_2_ = bf16[16,64,1024]{2,1,0:T(8,128)(2,1)S(1)} async-done(((bf16[16,64,1024]{2,1,0:T(8,128)(2,1)}), bf16[16,64,1024]{2,1,0:T(8,128)(2,1)S(1)}, u32[]{:S(2)}, u32[]{:S(2)}) %all-to-all-start.2) | async-done | bytes 2097184 | tf_op jit(solution)/shard_map/rows_of_held_blocks/all_to_all | solution.py:34
  112.1 1.6 copy-done.3
  113.7 4.5 %precondition.1 = bf16[32,80,128]{2,1,0:T(8,128)(2,1)} custom-call(s32[2]{0:T(128)S(1)} %pad_add_fusion.place_ref, bf16[16,64,1024]{2,1,0:T(8,128)(2,1)S(1)} %copy-done.3, bf16[4,64,1024]{2,1,0:T(8,128)(2,1)S(1)} %pad_maximum_fusion.refs_1_, bf16[16,64,1024]{2,1,0:T(8,128)(2,1)S(1)} %all-to-all-done.2.refs_2_), custom_call_target="tpu_custom_call" | custom-call | flops 2684354560 | bytes 6291456 | tf_op jit(solution)/shard_map/precondition/pallas_call | solution.py:168
  118.2 5.4 %all-to-all-start.3 = ((bf16[32,80,128]{2,1,0:T(8,128)(2,1)}), bf16[32,80,128]{2,1,0:T(8,128)(2,1)S(1)}, u32[]{:S(2)}, u32[]{:S(2)}) async-start(bf16[32,80,128]{2,1,0:T(8,128)(2,1)} %precondition.1), calls=%async_computation.3 | async-start | bytes 1310720 | tf_op jit(solution)/shard_map/step_to_gradient_rows/all_to_all | solution.py:274
  123.6 0.4 constant_dynamic-slice_fusion.3
  124.0 0.8 convolution_convert_fusion
  124.9 0.7 convolution_convert_fusion.1
  125.6 0.0 copy-start
  125.6 0.0 copy-start.1
  125.6 0.9 fusion.15
  126.5 9.3 %all-to-all-done.3.back_ref = bf16[32,80,128]{2,1,0:T(8,128)(2,1)S(1)} async-done(((bf16[32,80,128]{2,1,0:T(8,128)(2,1)}), bf16[32,80,128]{2,1,0:T(8,128)(2,1)S(1)}, u32[]{:S(2)}, u32[]{:S(2)}) %all-to-all-start.3) | async-done | bytes 655392 | tf_op jit(solution)/shard_map/step_to_gradient_rows/all_to_all | solution.py:274
  135.9 1.6 step_to_gradient_rows.1
  137.5 7.2 %all-to-all-start.4 = ((bf16[16,6,16,128]{3,2,1,0:T(8,128)(2,1)}), bf16[16,6,16,128]{3,2,1,0:T(8,128)(2,1)S(1)}, u32[]{:S(2)}, u32[]{:S(2)}) async-start(bf16[16,6,16,128]{3,2,1,0:T(8,128)(2,1)} %step_to_gradient_rows.1), calls=%async_computation.4 | async-start | bytes 786432 | tf_op jit(solution)/shard_map/step_to_gradient_rows/all_to_all | solution.py:267
  144.7 2.0 %collective-permute-start.7 = (bf16[2,64,1024]{2,1,0:T(8,128)(2,1)}, bf16[2,64,1024]{2,1,0:T(8,128)(2,1)S(1)}, u32[]{:S(2)}, u32[]{:S(2)}) collective-permute-start(bf16[2,64,1024]{2,1,0:T(8,128)(2,1)} %get-tuple-element.64), channel_id=1, source_target_pairs={{0,4},{1,5},{2,6},{3,7},{4,8},{5,9},{6,10},{7,11},{8,12},{9,13},{1... | collective-permute-start | bytes 786440 | tf_op jit(solution)/shard_map/statistics/ppermute | solution.py:252
  146.7 4.4 %collective-permute-start.8 = (bf16[2,64,1024]{2,1,0:T(8,128)(2,1)}, bf16[2,64,1024]{2,1,0:T(8,128)(2,1)S(1)}, u32[]{:S(2)}, u32[]{:S(2)}) collective-permute-start(bf16[2,64,1024]{2,1,0:T(8,128)(2,1)} %get-tuple-element.65), channel_id=1, source_target_pairs={{0,8},{1,9},{2,10},{3,11},{4,12},{5,13},{6,14},{7,15},{8,0},{9,1},... | collective-permute-start | bytes 786440 | tf_op jit(solution)/shard_map/statistics/ppermute | solution.py:252
  151.1 1.9 %collective-permute-start.9 = (bf16[2,64,1024]{2,1,0:T(8,128)(2,1)}, bf16[2,64,1024]{2,1,0:T(8,128)(2,1)S(1)}, u32[]{:S(2)}, u32[]{:S(2)}) collective-permute-start(bf16[2,64,1024]{2,1,0:T(8,128)(2,1)} %get-tuple-element.66), channel_id=1, source_target_pairs={{0,12},{1,13},{2,14},{3,15},{4,0},{5,1},{6,2},{7,3},{8,4},{9,5},{1... | collective-permute-start | bytes 786440 | tf_op jit(solution)/shard_map/statistics/ppermute | solution.py:252
  153.0 0.1 multiply_add_fusion
  153.1 0.1 add.234
  153.2 0.2 select_reduce_fusion.1.index_ref
  153.3 7.9 %collective-permute-done.8.refs_2_ = bf16[2,64,1024]{2,1,0:T(8,128)(2,1)S(1)} collective-permute-done((bf16[2,64,1024]{2,1,0:T(8,128)(2,1)}, bf16[2,64,1024]{2,1,0:T(8,128)(2,1)S(1)}, u32[]{:S(2)}, u32[]{:S(2)}) %collective-permute-start.8) | collective-permute-done | bytes 262176 | tf_op jit(solution)/shard_map/statistics/ppermute | solution.py:252
  161.2 0.4 collective-permute-done.9.refs_3_
  161.6 0.5 all-to-all-done.4
  162.2 1.2 statistics.2
  163.4 12.0 %all-to-all-start.5 = ((bf16[16,2,16,128]{3,2,1,0:T(8,128)(2,1)}), bf16[16,2,16,128]{3,2,1,0:T(8,128)(2,1)S(1)}, u32[]{:S(2)}, u32[]{:S(2)}) async-start(bf16[16,2,16,128]{3,2,1,0:T(8,128)(2,1)} %bitcast.23), calls=%async_computation.5 | async-start | bytes 262144 | tf_op jit(solution)/shard_map/statistics/all_to_all | solution.py:267
  175.5 1.9 %statistics.3 = (f32[3,64,1024]{2,1,0:T(8,128)}, f32[3,64,1024]{2,1,0:T(8,128)}) custom-call(s32[2]{0:T(128)S(1)} %pad_add_fusion.place_ref, f32[3,64,1024]{2,1,0:T(8,128)S(1)} %copy-done, f32[3,64,1024]{2,1,0:T(8,128)S(1)} %copy-done.1, bf16[2,64,1024]{2,1,0:T(8,128)(2,1)S(1)} %get-tuple-element.68.refs_0_, ...), custom_call_target="tpu_custom_call" | custom-call | bytes 4194304 | tf_op jit(solution)/shard_map/statistics/pallas_call | solution.py:402
  177.4 10.0 %all-to-all-done.5.tiles_ref = bf16[16,2,16,128]{3,2,1,0:T(8,128)(2,1)S(1)} async-done(((bf16[16,2,16,128]{3,2,1,0:T(8,128)(2,1)}), bf16[16,2,16,128]{3,2,1,0:T(8,128)(2,1)S(1)}, u32[]{:S(2)}, u32[]{:S(2)}) %all-to-all-start.5) | async-done | bytes 131104 | tf_op jit(solution)/shard_map/statistics/all_to_all | solution.py:267
  187.4 0.7 update.1
  (31 shorter events, 0.3 us)
Async XLA Ops:
  0.6 28.7 %copy-start.8 = (s32[4,8]{1,0:T(4,128)S(1)}, s32[4,8]{1,0:T(4,128)}, u32[]{:S(2)}) copy-start(s32[4,8]{1,0:T(4,128)} %param.7) | copy-start | bytes 388
  0.7 0.9 copy-start.4
  2.2 32.6 %all-to-all-start = ((bf16[32,16,128]{2,1,0:T(8,128)(2,1)}), bf16[32,16,128]{2,1,0:T(8,128)(2,1)S(1)}, u32[]{:S(2)}, u32[]{:S(2)}) async-start(bf16[32,16,128]{2,1,0:T(8,128)(2,1)} %gradient_spread.1), calls=%async_computation | async-start | bytes 262144 | tf_op jit(solution)/shard_map/gradient_spread/all_to_all | solution.py:261
  20.5 23.4 %collective-permute-start.2 = (bf16[2,64,1024]{2,1,0:T(8,128)(2,1)S(1)}, bf16[2,64,1024]{2,1,0:T(8,128)(2,1)S(1)}, u32[]{:S(2)}, u32[]{:S(2)}) collective-permute-start(bf16[2,64,1024]{2,1,0:T(8,128)(2,1)S(1)} %get-tuple-element.88), channel_id=1, source_target_pairs={{4,0},{5,1},{6,2},{7,3},{8,4},{9,5},{10,6},{11,7},{12,8},{13,9},{1... | collective-permute-start | bytes 786440 | tf_op jit(solution)/shard_map/roots_to_slot_groups/ppermute | solution.py:252
  21.8 22.1 %collective-permute-start.1 = (bf16[2,64,1024]{2,1,0:T(8,128)(2,1)S(1)}, bf16[2,64,1024]{2,1,0:T(8,128)(2,1)S(1)}, u32[]{:S(2)}, u32[]{:S(2)}) collective-permute-start(bf16[2,64,1024]{2,1,0:T(8,128)(2,1)S(1)} %get-tuple-element.87), channel_id=1, source_target_pairs={{0,8},{1,9},{2,10},{3,11},{8,0},{9,1},{10,2},{11,3},{12,4},{13,5},... | collective-permute-start | bytes 786440 | tf_op jit(solution)/shard_map/roots_to_slot_groups/ppermute | solution.py:252
  27.4 16.6 %collective-permute-start = (bf16[2,64,1024]{2,1,0:T(8,128)(2,1)S(1)}, bf16[2,64,1024]{2,1,0:T(8,128)(2,1)S(1)}, u32[]{:S(2)}, u32[]{:S(2)}) collective-permute-start(bf16[2,64,1024]{2,1,0:T(8,128)(2,1)S(1)} %get-tuple-element.86), channel_id=1, source_target_pairs={{0,4},{1,5},{2,6},{3,7},{4,8},{5,9},{6,10},{7,11},{12,0},{13,1},{1... | collective-permute-start | bytes 786440 | tf_op jit(solution)/shard_map/roots_to_slot_groups/ppermute | solution.py:252
  36.2 35.6 %all-to-all-start.1 = ((bf16[32,3,16,128]{3,2,1,0:T(8,128)(2,1)}), bf16[32,3,16,128]{3,2,1,0:T(8,128)(2,1)S(1)}, u32[]{:S(2)}, u32[]{:S(2)}) async-start(bf16[32,3,16,128]{3,2,1,0:T(8,128)(2,1)} %bitcast.3), calls=%async_computation.1 | async-start | bytes 786432 | tf_op jit(solution)/shard_map/gradient_to_owners/all_to_all | solution.py:261
  44.1 16.4 %collective-permute-start.3 = (bf16[4,64,1024]{2,1,0:T(8,128)(2,1)S(1)}, bf16[4,64,1024]{2,1,0:T(8,128)(2,1)S(1)}, u32[]{:S(2)}, u32[]{:S(2)}) collective-permute-start(bf16[4,64,1024]{2,1,0:T(8,128)(2,1)S(1)} %pad_maximum_fusion.1), channel_id=1, source_target_pairs={{0,1},{1,2},{2,3},{3,0},{4,5},{5,6},{6,7},{7,4},{8,9},{9,10},{10,1... | collective-permute-start | bytes 1572872 | tf_op jit(solution)/shard_map/roots_to_slot_groups/ppermute | solution.py:258
  47.2 15.2 %collective-permute-start.4 = (bf16[4,64,1024]{2,1,0:T(8,128)(2,1)S(1)}, bf16[4,64,1024]{2,1,0:T(8,128)(2,1)S(1)}, u32[]{:S(2)}, u32[]{:S(2)}) collective-permute-start(bf16[4,64,1024]{2,1,0:T(8,128)(2,1)S(1)} %pad_maximum_fusion.1), channel_id=1, source_target_pairs={{0,3},{1,0},{2,1},{3,2},{4,7},{5,4},{6,5},{7,6},{8,11},{9,8},{10,9... | collective-permute-start | bytes 1572872 | tf_op jit(solution)/shard_map/roots_to_slot_groups/ppermute | solution.py:258
  60.5 6.6 %copy-start.5 = (bf16[4,64,1024]{2,1,0:T(8,128)(2,1)}, bf16[4,64,1024]{2,1,0:T(8,128)(2,1)S(1)}, u32[]{:S(2)}) copy-start(bf16[4,64,1024]{2,1,0:T(8,128)(2,1)S(1)} %collective-permute-done.3) | copy-start | bytes 1572868
  60.5 9.9 %collective-permute-start.5 = (bf16[2,64,1024]{2,1,0:T(8,128)(2,1)S(1)}, bf16[2,64,1024]{2,1,0:T(8,128)(2,1)S(1)}, u32[]{:S(2)}, u32[]{:S(2)}) collective-permute-start(bf16[2,64,1024]{2,1,0:T(8,128)(2,1)S(1)} %slice.56), channel_id=1, source_target_pairs={{0,1},{1,2},{2,3},{3,0},{4,5},{5,6},{6,7},{7,4},{8,9},{9,10},{10,1... | collective-permute-start | bytes 786440 | tf_op jit(solution)/shard_map/roots_to_slot_groups/ppermute | solution.py:258
  62.4 11.5 %copy-start.6 = (bf16[4,64,1024]{2,1,0:T(8,128)(2,1)}, bf16[4,64,1024]{2,1,0:T(8,128)(2,1)S(1)}, u32[]{:S(2)}) copy-start(bf16[4,64,1024]{2,1,0:T(8,128)(2,1)S(1)} %collective-permute-done.4) | copy-start | bytes 1572868
  62.5 8.8 %collective-permute-start.6 = (bf16[2,64,1024]{2,1,0:T(8,128)(2,1)S(1)}, bf16[2,64,1024]{2,1,0:T(8,128)(2,1)}, u32[]{:S(2)}, u32[]{:S(2)}) collective-permute-start(bf16[2,64,1024]{2,1,0:T(8,128)(2,1)S(1)} %slice.57), channel_id=1, source_target_pairs={{0,3},{1,0},{2,1},{3,2},{4,7},{5,4},{6,5},{7,6},{8,11},{9,8},{10,9... | collective-permute-start | bytes 786440 | tf_op jit(solution)/shard_map/roots_to_slot_groups/ppermute | solution.py:258
  73.9 38.2 %all-to-all-start.2 = ((bf16[16,64,1024]{2,1,0:T(8,128)(2,1)}), bf16[16,64,1024]{2,1,0:T(8,128)(2,1)S(1)}, u32[]{:S(2)}, u32[]{:S(2)}) async-start(bf16[16,64,1024]{2,1,0:T(8,128)(2,1)} %rows_of_held_blocks.1), calls=%async_computation.2 | async-start | bytes 4194304 | tf_op jit(solution)/shard_map/rows_of_held_blocks/all_to_all | solution.py:34
  80.8 1.4 copy-start.7
  83.3 1.3 copy-start.2
  112.1 1.6 copy-start.3
  118.2 17.6 %all-to-all-start.3 = ((bf16[32,80,128]{2,1,0:T(8,128)(2,1)}), bf16[32,80,128]{2,1,0:T(8,128)(2,1)S(1)}, u32[]{:S(2)}, u32[]{:S(2)}) async-start(bf16[32,80,128]{2,1,0:T(8,128)(2,1)} %precondition.1), calls=%async_computation.3 | async-start | bytes 1310720 | tf_op jit(solution)/shard_map/step_to_gradient_rows/all_to_all | solution.py:274
  125.6 49.8 %copy-start = (f32[3,64,1024]{2,1,0:T(8,128)S(1)}, f32[3,64,1024]{2,1,0:T(8,128)}, u32[]{:S(2)}) copy-start(f32[3,64,1024]{2,1,0:T(8,128)} %left_ref.1) | copy-start | bytes 2359300
  125.6 49.8 %copy-start.1 = (f32[3,64,1024]{2,1,0:T(8,128)S(1)}, f32[3,64,1024]{2,1,0:T(8,128)}, u32[]{:S(2)}) copy-start(f32[3,64,1024]{2,1,0:T(8,128)} %right_ref.1) | copy-start | bytes 2359300
  137.5 24.7 %all-to-all-start.4 = ((bf16[16,6,16,128]{3,2,1,0:T(8,128)(2,1)}), bf16[16,6,16,128]{3,2,1,0:T(8,128)(2,1)S(1)}, u32[]{:S(2)}, u32[]{:S(2)}) async-start(bf16[16,6,16,128]{3,2,1,0:T(8,128)(2,1)} %step_to_gradient_rows.1), calls=%async_computation.4 | async-start | bytes 786432 | tf_op jit(solution)/shard_map/step_to_gradient_rows/all_to_all | solution.py:267
  144.7 8.7 %collective-permute-start.7 = (bf16[2,64,1024]{2,1,0:T(8,128)(2,1)}, bf16[2,64,1024]{2,1,0:T(8,128)(2,1)S(1)}, u32[]{:S(2)}, u32[]{:S(2)}) collective-permute-start(bf16[2,64,1024]{2,1,0:T(8,128)(2,1)} %get-tuple-element.64), channel_id=1, source_target_pairs={{0,4},{1,5},{2,6},{3,7},{4,8},{5,9},{6,10},{7,11},{8,12},{9,13},{1... | collective-permute-start | bytes 786440 | tf_op jit(solution)/shard_map/statistics/ppermute | solution.py:252
  146.7 14.6 %collective-permute-start.8 = (bf16[2,64,1024]{2,1,0:T(8,128)(2,1)}, bf16[2,64,1024]{2,1,0:T(8,128)(2,1)S(1)}, u32[]{:S(2)}, u32[]{:S(2)}) collective-permute-start(bf16[2,64,1024]{2,1,0:T(8,128)(2,1)} %get-tuple-element.65), channel_id=1, source_target_pairs={{0,8},{1,9},{2,10},{3,11},{4,12},{5,13},{6,14},{7,15},{8,0},{9,1},... | collective-permute-start | bytes 786440 | tf_op jit(solution)/shard_map/statistics/ppermute | solution.py:252
  151.1 10.6 %collective-permute-start.9 = (bf16[2,64,1024]{2,1,0:T(8,128)(2,1)}, bf16[2,64,1024]{2,1,0:T(8,128)(2,1)S(1)}, u32[]{:S(2)}, u32[]{:S(2)}) collective-permute-start(bf16[2,64,1024]{2,1,0:T(8,128)(2,1)} %get-tuple-element.66), channel_id=1, source_target_pairs={{0,12},{1,13},{2,14},{3,15},{4,0},{5,1},{6,2},{7,3},{8,4},{9,5},{1... | collective-permute-start | bytes 786440 | tf_op jit(solution)/shard_map/statistics/ppermute | solution.py:252
  163.4 24.0 %all-to-all-start.5 = ((bf16[16,2,16,128]{3,2,1,0:T(8,128)(2,1)}), bf16[16,2,16,128]{3,2,1,0:T(8,128)(2,1)S(1)}, u32[]{:S(2)}, u32[]{:S(2)}) async-start(bf16[16,2,16,128]{3,2,1,0:T(8,128)(2,1)} %bitcast.23), calls=%async_computation.5 | async-start | bytes 262144 | tf_op jit(solution)/shard_map/statistics/all_to_all | solution.py:267

commit v4 on v3

--- a/solution.py
+++ b/solution.py
@@ -118,8 +118,59 @@
     return lax.rem(place + count - step, count)
 
 
-def precondition_kernel(side, origins, place_ref, *refs):
-    left_ref, right_ref, block_ref, out_ref = refs
+def turn_kernel(side, place_ref, root_ref, out_ref):
+    x = place_ref[1]
+    block_side = root_ref.shape[2]
+    width, narrow = block_side // side, block_side // side // side
+    for slot in range(root_ref.shape[0]):
+        for column in range(side):
+            chunk = [
+                root_ref[slot, :, pl.ds(row * width + column * narrow, narrow)]
+                for row in range(side)
+            ]
+            lanes = pl.ds(pl.multiple_of(around(column, x, side) * width, width), width)
+            out_ref[slot, :, lanes] = jnp.concatenate(chunk, axis=1)
+
+
+def whole_root_kernel(side, place_ref, own_ref, before_ref, behind_ref, far_ref, out_ref, turned_ref):
+    y, x = place_ref[0], place_ref[1]
+    block_side = own_ref.shape[2]
+    width, narrow = block_side // side, block_side // side // side
+
+    def block(ref, number):
+        return jnp.concatenate(
+            [
+                ref[around(y, at, side), :, pl.ds(number * width, width)]
+                for at in range(side)
+            ],
+            axis=0,
+        )
+
+    given = {(0, 0): block(own_ref, 0)}
+    for number in range(1, side):
+        given[0, number] = block(own_ref, number)
+    given[3, 3], given[3, 1], given[3, 2] = (block(before_ref, number) for number in range(3))
+    given[1, 1], given[1, 2] = (block(behind_ref, number) for number in range(2))
+    given[2, 2] = block(far_ref, 0)
+    for first in range(side):
+        for second in range(side):
+            if (first, second) in given:
+                value = given[first, second]
+            else:
+                value = given[second, first].astype(jnp.float32).T.astype(own_ref.dtype)
+            turned_ref[pl.ds(first * width, width), pl.ds(second * width, width)] = value
+    for first in range(side):
+        rows = pl.ds(first * width, width)
+        for column in range(side):
+            lanes = pl.ds(pl.multiple_of(around(column, x, side) * width, width), width)
+            chunk = turned_ref[rows, lanes]
+            for row in range(side):
+                out_ref[rows, pl.ds(row * width + column * narrow, narrow)] = chunk[
+                    :, row * narrow : (row + 1) * narrow
+                ]
+
+
+def precondition_kernel(side, place_ref, left_ref, right_ref, block_ref, out_ref):
     y, x = place_ref[0], place_ref[1]
     places, height, block_side = block_ref.shape
     width = block_side // side
@@ -144,8 +195,8 @@
                 ],
                 axis=1,
             )
-            for at, (row, column) in enumerate(origins[begin : begin + side]):
-                place = core * places + around(y, row, side) * side + around(x, column, side)
+            for at in range(side):
+                place = core * places + at * side + lax.rem(x + begin // side, side)
                 out_ref[place, pl.ds(0, height), :] = share[at * height : (at + 1) * height]
     share = places // side
     own = block_ref[pl.ds(x * share, share)].astype(jnp.float32).reshape(width, block_side)
@@ -161,12 +212,12 @@
         out_ref[place, pl.ds(height, TAIL), :] = tail
 
 
-def precondition(place, left, origins, right, block):
+def precondition(place, left, right, block):
     places, height, block_side = block.shape
     side = right.shape[0]
     width = block_side // side
     return pl.pallas_call(
-        functools.partial(precondition_kernel, side, origins),
+        functools.partial(precondition_kernel, side),
         out_shape=jax.ShapeDtypeStruct((places * CORES, height + TAIL, LANES), jnp.bfloat16),
         in_specs=[SMEM] + [VMEM] * 3,
         out_specs=VMEM,
@@ -325,7 +376,15 @@
         tiles = over_rows(sent)
 
     with jax.named_scope("roots_to_slot_groups"):
-        roots = jnp.stack([left_root, right_root], axis=1)
+        turned = pl.pallas_call(
+            functools.partial(turn_kernel, side),
+            out_shape=jax.ShapeDtypeStruct(left_root.shape, left_root.dtype),
+            in_specs=[SMEM, VMEM],
+            out_specs=VMEM,
+            compiler_params=LIMIT,
+            cost_estimate=cost(0, 2**20),
+        )(place, left_root)
+        roots = jnp.stack([turned, right_root], axis=1)
         taken = []
         for step in range(side):
             slot = jnp.minimum((y + step) % side, capacity - 1)
@@ -333,18 +392,16 @@
             taken.append(along_y(own, step, side, capacity) if step else own)
         left_rows = jnp.stack([piece[0] for piece in taken])
         right_rows = jnp.stack([piece[1] for piece in taken])
-        half = side // 2
-        before = along_x(left_rows, 1, capacity)
-        behind = along_x(left_rows, side - 1, capacity)
+        width = row_depth
         lefts = [
             left_rows,
-            before,
-            behind,
-            along_x(before[:half], 1, capacity),
-            along_x(behind[half:], side - 1, capacity),
-        ]
-        origins = [
-            (row, column) for column in (0, 1, side - 1, half) for row in range(side)
+            along_x(
+                jnp.concatenate([left_rows[:, :, :width], left_rows[:, :, 2 * width :]], axis=2),
+                1,
+                capacity,
+            ),
+            along_x(left_rows[:, :, : 2 * width], side - 1, capacity),
+            along_x(left_rows[:, :, :width], 2, capacity),
         ]
         tiles, right_rows, *lefts = lax.optimization_barrier((tiles, right_rows, *lefts))
 
@@ -352,10 +409,19 @@
         sent = held_rows(column_of, used, tiles, local_height, block_side, tensor_count)
         sent, *lefts = lax.optimization_barrier((sent, *lefts))
         block = exchange(sent)
-        left = jnp.concatenate(lefts)
+        left = pl.pallas_call(
+            functools.partial(whole_root_kernel, side),
+            out_shape=jax.ShapeDtypeStruct((block_side, block_side), left_root.dtype),
+            in_specs=[SMEM] + [VMEM] * len(lefts),
+            out_specs=VMEM,
+            scratch_shapes=[pltpu.VMEM((block_side, block_side), left_root.dtype)],
+            compiler_params=LIMIT,
+            cost_estimate=cost(0, 8 * 2**20),
+        )(place, *lefts)
+        left = left.reshape(tensor_count, local_height, block_side)
 
     with jax.named_scope("precondition"):
-        leaving = precondition(place, left, origins, right_rows, block)
+        leaving = precondition(place, left, right_rows, block)
 
     with jax.named_scope("step_to_gradient_rows"):
         back = over_chip_planes(leaving)

time: 191 us -> 188 us (0.984)
  starting transfers between devices: 85.9 us -> 78.8 us
  Pallas kernels: 14 us -> 16.5 us
    all_to_all x2, waiting for transfers between devices: 5.64 us -> 15.1 us  [over_rows(): lax.all_to_all(value, 'fsdp', split_axis=0, concat_axis=0, tiled=True)]
    ppermute x4 -> x3, waiting for transfers between devices: 13.6 us -> 6.97 us  [along_x(): return lax.ppermute(value, 'tensor', pairs)]
    all_to_all x2, starting transfers between devices: 19.2 us -> 16.1 us  [along_z(): lax.all_to_all(value, 'fsdp', split_axis=0, concat_axis=0, tiled=True, ax...]
    ppermute x4 -> x3, starting transfers between devices: 13 us -> 9.93 us  [along_x(): return lax.ppermute(value, 'tensor', pairs)]
    pallas_call x1 -> x3, Pallas kernels: 4.51 us -> 6.93 us  [the longest x1 4.49 us: precondition(): pl.pallas_call(functools.partial(precondition_kernel, side), out_shape=ja...]
  transfers between devices with their start and end apart: 16 -> 15, of which waited for: 11 -> 8; matrix products, arithmetic and copies ran while one was open for 4% -> 3% of each run, Pallas kernels for 2% -> 3%
where the time goes in v4:
time: 188 us; the launch traced here: 185 us
  starting transfers between devices  78.8 us (42%)
  waiting for transfers between devices  76 us (40%)
  Pallas kernels  16.5 us (9%)
  local copies, waits for them, and re-layouts  7.42 us (4%)
  other arithmetic  3.49 us (2%)
    all_to_all x1, waiting for transfers between devices, exchange(): lax.all_to_all(pieces, 'tensor', split_axis=0, concat_axis=0, tiled=True)  26.2 us
    all_to_all x2, starting transfers between devices, over_rows(): lax.all_to_all(value, 'fsdp', split_axis=0, concat_axis=0, tiled=True)  24.4 us
    all_to_all x2, starting transfers between devices, along_z(): lax.all_to_all(value, 'fsdp', split_axis=0, concat_axis=0, tiled=True, ax...  16.1 us
    ppermute x6, starting transfers between devices, along_y(): return lax.ppermute(value, 'tensor', pairs)  15.8 us
    all_to_all x2, waiting for transfers between devices, over_rows(): lax.all_to_all(value, 'fsdp', split_axis=0, concat_axis=0, tiled=True)  15.1 us
    all_to_all x2, waiting for transfers between devices, along_z(): lax.all_to_all(value, 'fsdp', split_axis=0, concat_axis=0, tiled=True, ax...  10 us
    ppermute x3, starting transfers between devices, along_x(): return lax.ppermute(value, 'tensor', pairs)  9.93 us
    all_to_all x1, waiting for transfers between devices, over_chip_planes(): lax.all_to_all(value, ('fsdp', 'tensor'), split_axis=0, concat_axis=0, ti...  9.32 us
  transfers between devices with their start and end apart: 15, of which 8 were waited for; matrix products, arithmetic and copies ran while one was open for 3% of the time, Pallas kernels for 3%

profile of v4, /device:TPU:1, one launch (start us, length us, event | category | flops | bytes accessed | tf_op | source)
XLA Modules:
  0.0 185.0 jit_solution(12367702493030245671)
XLA Ops:
  0.7 0.9 copy-done.9
  1.6 0.7 gradient_spread.1
  2.2 16.7 %all-to-all-start = ((bf16[32,16,128]{2,1,0:T(8,128)(2,1)}), bf16[32,16,128]{2,1,0:T(8,128)(2,1)S(1)}, u32[]{:S(2)}, u32[]{:S(2)}) async-start(bf16[32,16,128]{2,1,0:T(8,128)(2,1)} %gradient_spread.1), calls=%async_computation | async-start | bytes 262144 | tf_op jit(solution)/shard_map/gradient_spread/all_to_all | solution.py:312
  19.1 0.1 pad_add_fusion.place_ref
  19.2 1.0 copy-done.4
  20.2 0.7 roots_to_slot_groups.1
  20.9 1.2 fusion.9
  22.1 3.2 %collective-permute-start = (bf16[2,64,1024]{2,1,0:T(8,128)(2,1)S(1)}, bf16[2,64,1024]{2,1,0:T(8,128)(2,1)S(1)}, u32[]{:S(2)}, u32[]{:S(2)}) collective-permute-start(bf16[2,64,1024]{2,1,0:T(8,128)(2,1)S(1)} %get-tuple-element.82), channel_id=1, source_target_pairs={{0,4},{1,5},{2,6},{3,7},{4,8},{5,9},{6,10},{7,11},{12,0},{13,1},{1... | collective-permute-start | bytes 786440 | tf_op jit(solution)/shard_map/roots_to_slot_groups/ppermute | solution.py:303
  25.3 2.9 %collective-permute-start.1 = (bf16[2,64,1024]{2,1,0:T(8,128)(2,1)S(1)}, bf16[2,64,1024]{2,1,0:T(8,128)(2,1)S(1)}, u32[]{:S(2)}, u32[]{:S(2)}) collective-permute-start(bf16[2,64,1024]{2,1,0:T(8,128)(2,1)S(1)} %get-tuple-element.83), channel_id=1, source_target_pairs={{0,8},{1,9},{2,10},{3,11},{8,0},{9,1},{10,2},{11,3},{12,4},{13,5},... | collective-permute-start | bytes 786440 | tf_op jit(solution)/shard_map/roots_to_slot_groups/ppermute | solution.py:303
  28.2 1.3 collective-permute-start.2
  29.5 0.1 reshape.214
  29.6 0.2 select_reduce_fusion.2
  29.9 0.1 select_reduce_fusion.index_ref
  30.0 4.9 %all-to-all-done.tiles_ref = bf16[32,16,128]{2,1,0:T(8,128)(2,1)S(1)} async-done(((bf16[32,16,128]{2,1,0:T(8,128)(2,1)}), bf16[32,16,128]{2,1,0:T(8,128)(2,1)S(1)}, u32[]{:S(2)}, u32[]{:S(2)}) %all-to-all-start) | async-done | bytes 131104 | tf_op jit(solution)/shard_map/gradient_spread/all_to_all | solution.py:312
  34.8 1.4 gradient_to_owners.1
  36.2 7.6 %all-to-all-start.1 = ((bf16[32,3,16,128]{3,2,1,0:T(8,128)(2,1)}), bf16[32,3,16,128]{3,2,1,0:T(8,128)(2,1)S(1)}, u32[]{:S(2)}, u32[]{:S(2)}) async-start(bf16[32,3,16,128]{3,2,1,0:T(8,128)(2,1)} %bitcast.3), calls=%async_computation.1 | async-start | bytes 786432 | tf_op jit(solution)/shard_map/gradient_to_owners/all_to_all | solution.py:312
  43.8 0.0 collective-permute-done
  43.9 0.0 collective-permute-done.1
  43.9 0.0 collective-permute-done.2
  43.9 0.1 pad_maximum_fusion.1.own_ref
  44.1 3.1 %collective-permute-start.3 = (bf16[4,64,768]{2,1,0:T(8,128)(2,1)S(1)}, bf16[4,64,768]{2,1,0:T(8,128)(2,1)S(1)}, u32[]{:S(2)}, u32[]{:S(2)}) collective-permute-start(bf16[4,64,768]{2,1,0:T(8,128)(2,1)S(1)} %pad_maximum_fusion.2), channel_id=1, source_target_pairs={{0,1},{1,2},{2,3},{3,0},{4,5},{5,6},{6,7},{7,4},{8,9},{9,10},{10,1... | collective-permute-start | bytes 1179656 | tf_op jit(solution)/shard_map/roots_to_slot_groups/ppermute | solution.py:309
  47.3 3.4 %collective-permute-start.4 = (bf16[4,64,512]{2,1,0:T(8,128)(2,1)S(1)}, bf16[4,64,512]{2,1,0:T(8,128)(2,1)S(1)}, u32[]{:S(2)}, u32[]{:S(2)}) collective-permute-start(bf16[4,64,512]{2,1,0:T(8,128)(2,1)S(1)} %get-tuple-element.85), channel_id=1, source_target_pairs={{0,3},{1,0},{2,1},{3,2},{4,7},{5,4},{6,5},{7,6},{8,11},{9,8},{10,9... | collective-permute-start | bytes 786440 | tf_op jit(solution)/shard_map/roots_to_slot_groups/ppermute | solution.py:309
  50.6 0.2 fusion.23.column_ref
  50.8 3.4 %collective-permute-start.5 = (bf16[4,64,256]{2,1,0:T(8,128)(2,1)S(1)}, bf16[4,64,256]{2,1,0:T(8,128)(2,1)S(1)}, u32[]{:S(2)}, u32[]{:S(2)}) collective-permute-start(bf16[4,64,256]{2,1,0:T(8,128)(2,1)S(1)} %slice.61), channel_id=1, source_target_pairs={{0,2},{1,3},{2,0},{3,1},{4,6},{5,7},{6,4},{7,5},{8,10},{9,11},{10,... | collective-permute-start | bytes 393224 | tf_op jit(solution)/shard_map/roots_to_slot_groups/ppermute | solution.py:309
  54.3 0.2 compare_reduce_fusion
  54.5 0.1 pad_maximum_fusion.right_ref
  54.5 7.0 %collective-permute-done.5.far_ref = bf16[4,64,256]{2,1,0:T(8,128)(2,1)S(1)} collective-permute-done((bf16[4,64,256]{2,1,0:T(8,128)(2,1)S(1)}, bf16[4,64,256]{2,1,0:T(8,128)(2,1)S(1)}, u32[]{:S(2)}, u32[]{:S(2)}) %collective-permute-start.5) | collective-permute-done | bytes 131104 | tf_op jit(solution)/shard_map/roots_to_slot_groups/ppermute | solution.py:309
  61.5 0.0 collective-permute-done.4.behind_ref
  61.5 0.0 collective-permute-done.3.before_ref
  61.5 10.3 %all-to-all-done.1.tiles_ref = bf16[32,3,16,128]{3,2,1,0:T(8,128)(2,1)S(1)} async-done(((bf16[32,3,16,128]{3,2,1,0:T(8,128)(2,1)}), bf16[32,3,16,128]{3,2,1,0:T(8,128)(2,1)S(1)}, u32[]{:S(2)}, u32[]{:S(2)}) %all-to-all-start.1) | async-done | bytes 393248 | tf_op jit(solution)/shard_map/gradient_to_owners/all_to_all | solution.py:312
  71.8 2.1 %rows_of_held_blocks.2 = bf16[16,64,1024]{2,1,0:T(8,128)(2,1)} custom-call(s32[3]{0:T(128)S(1)} %fusion.23.column_ref, s32[3]{0:T(128)S(1)} %convert_element_type.9.used_ref, bf16[32,3,16,128]{3,2,1,0:T(8,128)(2,1)S(1)} %all-to-all-done.1.tiles_ref), custom_call_target="tpu_custom_call" | custom-call | bytes 4194304 | tf_op jit(solution)/shard_map/rows_of_held_blocks/pallas_call | solution.py:96
  73.9 7.3 %all-to-all-start.2 = ((bf16[16,64,1024]{2,1,0:T(8,128)(2,1)}), bf16[16,64,1024]{2,1,0:T(8,128)(2,1)S(1)}, u32[]{:S(2)}, u32[]{:S(2)}) async-start(bf16[16,64,1024]{2,1,0:T(8,128)(2,1)} %rows_of_held_blocks.2), calls=%async_computation.2 | async-start | bytes 4194304 | tf_op jit(solution)/shard_map/rows_of_held_blocks/all_to_all | solution.py:34
  81.3 0.2 select_reduce_fusion.3.column_ref
  81.5 0.9 copy-done.6
  82.4 0.9 copy-done.8
  83.3 1.7 rows_of_held_blocks.3
  85.1 1.3 copy-done
  86.4 26.2 %all-to-all-done.2.block_ref = bf16[16,64,1024]{2,1,0:T(8,128)(2,1)S(1)} async-done(((bf16[16,64,1024]{2,1,0:T(8,128)(2,1)}), bf16[16,64,1024]{2,1,0:T(8,128)(2,1)S(1)}, u32[]{:S(2)}, u32[]{:S(2)}) %all-to-all-start.2) | async-done | bytes 2097184 | tf_op jit(solution)/shard_map/rows_of_held_blocks/all_to_all | solution.py:34
  112.6 1.6 copy-done.1
  114.2 4.5 %precondition.1 = bf16[32,80,128]{2,1,0:T(8,128)(2,1)} custom-call(s32[2]{0:T(128)S(1)} %pad_add_fusion.place_ref, bf16[16,64,1024]{2,1,0:T(8,128)(2,1)S(1)} %bitcast.44, bf16[4,64,1024]{2,1,0:T(8,128)(2,1)S(1)} %pad_maximum_fusion.right_ref, bf16[16,64,1024]{2,1,0:T(8,128)(2,1)S(1)} %all-to-all-done.2.block_ref), custom_call_target="tpu_custom_call" | custom-call | flops 2684354560 | bytes 6291456 | tf_op jit(solution)/shard_map/precondition/pallas_call | solution.py:219
  118.6 5.4 %all-to-all-start.3 = ((bf16[32,80,128]{2,1,0:T(8,128)(2,1)}), bf16[32,80,128]{2,1,0:T(8,128)(2,1)S(1)}, u32[]{:S(2)}, u32[]{:S(2)}) async-start(bf16[32,80,128]{2,1,0:T(8,128)(2,1)} %precondition.1), calls=%async_computation.3 | async-start | bytes 1310720 | tf_op jit(solution)/shard_map/step_to_gradient_rows/all_to_all | solution.py:325
  124.0 0.4 constant_dynamic-slice_fusion.3
  124.4 0.8 convolution_convert_fusion
  125.3 0.7 convolution_convert_fusion.1
  126.0 0.0 copy-start.2
  126.0 0.0 copy-start.3
  126.1 0.9 fusion.15
  127.0 9.3 %all-to-all-done.3.back_ref = bf16[32,80,128]{2,1,0:T(8,128)(2,1)S(1)} async-done(((bf16[32,80,128]{2,1,0:T(8,128)(2,1)}), bf16[32,80,128]{2,1,0:T(8,128)(2,1)S(1)}, u32[]{:S(2)}, u32[]{:S(2)}) %all-to-all-start.3) | async-done | bytes 655392 | tf_op jit(solution)/shard_map/step_to_gradient_rows/all_to_all | solution.py:325
  136.3 1.6 step_to_gradient_rows.1
  137.9 3.7 %all-to-all-start.4 = ((bf16[16,6,16,128]{3,2,1,0:T(8,128)(2,1)}), bf16[16,6,16,128]{3,2,1,0:T(8,128)(2,1)S(1)}, u32[]{:S(2)}, u32[]{:S(2)}) async-start(bf16[16,6,16,128]{3,2,1,0:T(8,128)(2,1)} %step_to_gradient_rows.1), calls=%async_computation.4 | async-start | bytes 786432 | tf_op jit(solution)/shard_map/step_to_gradient_rows/all_to_all | solution.py:318
  141.6 2.1 %collective-permute-start.6 = (bf16[2,64,1024]{2,1,0:T(8,128)(2,1)}, bf16[2,64,1024]{2,1,0:T(8,128)(2,1)S(1)}, u32[]{:S(2)}, u32[]{:S(2)}) collective-permute-start(bf16[2,64,1024]{2,1,0:T(8,128)(2,1)} %get-tuple-element.60), channel_id=1, source_target_pairs={{0,4},{1,5},{2,6},{3,7},{4,8},{5,9},{6,10},{7,11},{8,12},{9,13},{1... | collective-permute-start | bytes 786440 | tf_op jit(solution)/shard_map/statistics/ppermute | solution.py:303
  143.7 4.4 %collective-permute-start.7 = (bf16[2,64,1024]{2,1,0:T(8,128)(2,1)}, bf16[2,64,1024]{2,1,0:T(8,128)(2,1)S(1)}, u32[]{:S(2)}, u32[]{:S(2)}) collective-permute-start(bf16[2,64,1024]{2,1,0:T(8,128)(2,1)} %get-tuple-element.61), channel_id=1, source_target_pairs={{0,8},{1,9},{2,10},{3,11},{4,12},{5,13},{6,14},{7,15},{8,0},{9,1},... | collective-permute-start | bytes 786440 | tf_op jit(solution)/shard_map/statistics/ppermute | solution.py:303
  148.1 1.9 %collective-permute-start.8 = (bf16[2,64,1024]{2,1,0:T(8,128)(2,1)}, bf16[2,64,1024]{2,1,0:T(8,128)(2,1)S(1)}, u32[]{:S(2)}, u32[]{:S(2)}) collective-permute-start(bf16[2,64,1024]{2,1,0:T(8,128)(2,1)} %get-tuple-element.62), channel_id=1, source_target_pairs={{0,12},{1,13},{2,14},{3,15},{4,0},{5,1},{6,2},{7,3},{8,4},{9,5},{1... | collective-permute-start | bytes 786440 | tf_op jit(solution)/shard_map/statistics/ppermute | solution.py:303
  150.0 0.1 multiply_add_fusion
  150.1 0.1 add.234
  150.2 0.2 select_reduce_fusion.1.index_ref
  150.4 0.0 collective-permute-done.6.refs_1_
  150.4 8.0 %collective-permute-done.7.refs_2_ = bf16[2,64,1024]{2,1,0:T(8,128)(2,1)S(1)} collective-permute-done((bf16[2,64,1024]{2,1,0:T(8,128)(2,1)}, bf16[2,64,1024]{2,1,0:T(8,128)(2,1)S(1)}, u32[]{:S(2)}, u32[]{:S(2)}) %collective-permute-start.7) | collective-permute-done | bytes 262176 | tf_op jit(solution)/shard_map/statistics/ppermute | solution.py:303
  158.4 0.3 collective-permute-done.8.refs_3_
  158.7 1.2 statistics.2
  160.0 12.4 %all-to-all-start.5 = ((bf16[16,2,16,128]{3,2,1,0:T(8,128)(2,1)}), bf16[16,2,16,128]{3,2,1,0:T(8,128)(2,1)S(1)}, u32[]{:S(2)}, u32[]{:S(2)}) async-start(bf16[16,2,16,128]{3,2,1,0:T(8,128)(2,1)} %bitcast.24), calls=%async_computation.5 | async-start | bytes 262144 | tf_op jit(solution)/shard_map/statistics/all_to_all | solution.py:318
  172.4 1.9 %statistics.3 = (f32[3,64,1024]{2,1,0:T(8,128)}, f32[3,64,1024]{2,1,0:T(8,128)}) custom-call(s32[2]{0:T(128)S(1)} %pad_add_fusion.place_ref, f32[3,64,1024]{2,1,0:T(8,128)S(1)} %copy-done.2, f32[3,64,1024]{2,1,0:T(8,128)S(1)} %copy-done.3, bf16[2,64,1024]{2,1,0:T(8,128)(2,1)S(1)} %get-tuple-element.64.refs_0_, ...), custom_call_target="tpu_custom_call" | custom-call | bytes 4194304 | tf_op jit(solution)/shard_map/statistics/pallas_call | solution.py:468
  174.4 10.0 %all-to-all-done.5.tiles_ref = bf16[16,2,16,128]{3,2,1,0:T(8,128)(2,1)S(1)} async-done(((bf16[16,2,16,128]{3,2,1,0:T(8,128)(2,1)}), bf16[16,2,16,128]{3,2,1,0:T(8,128)(2,1)S(1)}, u32[]{:S(2)}, u32[]{:S(2)}) %all-to-all-start.5) | async-done | bytes 131104 | tf_op jit(solution)/shard_map/statistics/all_to_all | solution.py:318
  184.3 0.7 update.1
  (31 shorter events, 0.3 us)
Async XLA Ops:
  0.6 28.9 %copy-start.10 = (s32[4,8]{1,0:T(4,128)S(1)}, s32[4,8]{1,0:T(4,128)}, u32[]{:S(2)}) copy-start(s32[4,8]{1,0:T(4,128)} %param.7) | copy-start | bytes 388
  0.7 0.9 copy-start.9
  2.2 32.6 %all-to-all-start = ((bf16[32,16,128]{2,1,0:T(8,128)(2,1)}), bf16[32,16,128]{2,1,0:T(8,128)(2,1)S(1)}, u32[]{:S(2)}, u32[]{:S(2)}) async-start(bf16[32,16,128]{2,1,0:T(8,128)(2,1)} %gradient_spread.1), calls=%async_computation | async-start | bytes 262144 | tf_op jit(solution)/shard_map/gradient_spread/all_to_all | solution.py:312
  19.2 1.0 copy-start.4
  22.1 21.7 %collective-permute-start = (bf16[2,64,1024]{2,1,0:T(8,128)(2,1)S(1)}, bf16[2,64,1024]{2,1,0:T(8,128)(2,1)S(1)}, u32[]{:S(2)}, u32[]{:S(2)}) collective-permute-start(bf16[2,64,1024]{2,1,0:T(8,128)(2,1)S(1)} %get-tuple-element.82), channel_id=1, source_target_pairs={{0,4},{1,5},{2,6},{3,7},{4,8},{5,9},{6,10},{7,11},{12,0},{13,1},{1... | collective-permute-start | bytes 786440 | tf_op jit(solution)/shard_map/roots_to_slot_groups/ppermute | solution.py:303
  25.3 18.6 %collective-permute-start.1 = (bf16[2,64,1024]{2,1,0:T(8,128)(2,1)S(1)}, bf16[2,64,1024]{2,1,0:T(8,128)(2,1)S(1)}, u32[]{:S(2)}, u32[]{:S(2)}) collective-permute-start(bf16[2,64,1024]{2,1,0:T(8,128)(2,1)S(1)} %get-tuple-element.83), channel_id=1, source_target_pairs={{0,8},{1,9},{2,10},{3,11},{8,0},{9,1},{10,2},{11,3},{12,4},{13,5},... | collective-permute-start | bytes 786440 | tf_op jit(solution)/shard_map/roots_to_slot_groups/ppermute | solution.py:303
  28.2 15.7 %collective-permute-start.2 = (bf16[2,64,1024]{2,1,0:T(8,128)(2,1)S(1)}, bf16[2,64,1024]{2,1,0:T(8,128)(2,1)S(1)}, u32[]{:S(2)}, u32[]{:S(2)}) collective-permute-start(bf16[2,64,1024]{2,1,0:T(8,128)(2,1)S(1)} %get-tuple-element.84), channel_id=1, source_target_pairs={{4,0},{5,1},{6,2},{7,3},{8,4},{9,5},{10,6},{11,7},{12,8},{13,9},{1... | collective-permute-start | bytes 786440 | tf_op jit(solution)/shard_map/roots_to_slot_groups/ppermute | solution.py:303
  36.2 35.6 %all-to-all-start.1 = ((bf16[32,3,16,128]{3,2,1,0:T(8,128)(2,1)}), bf16[32,3,16,128]{3,2,1,0:T(8,128)(2,1)S(1)}, u32[]{:S(2)}, u32[]{:S(2)}) async-start(bf16[32,3,16,128]{3,2,1,0:T(8,128)(2,1)} %bitcast.3), calls=%async_computation.1 | async-start | bytes 786432 | tf_op jit(solution)/shard_map/gradient_to_owners/all_to_all | solution.py:312
  44.1 17.4 %collective-permute-start.3 = (bf16[4,64,768]{2,1,0:T(8,128)(2,1)S(1)}, bf16[4,64,768]{2,1,0:T(8,128)(2,1)S(1)}, u32[]{:S(2)}, u32[]{:S(2)}) collective-permute-start(bf16[4,64,768]{2,1,0:T(8,128)(2,1)S(1)} %pad_maximum_fusion.2), channel_id=1, source_target_pairs={{0,1},{1,2},{2,3},{3,0},{4,5},{5,6},{6,7},{7,4},{8,9},{9,10},{10,1... | collective-permute-start | bytes 1179656 | tf_op jit(solution)/shard_map/roots_to_slot_groups/ppermute | solution.py:309
  47.3 14.2 %collective-permute-start.4 = (bf16[4,64,512]{2,1,0:T(8,128)(2,1)S(1)}, bf16[4,64,512]{2,1,0:T(8,128)(2,1)S(1)}, u32[]{:S(2)}, u32[]{:S(2)}) collective-permute-start(bf16[4,64,512]{2,1,0:T(8,128)(2,1)S(1)} %get-tuple-element.85), channel_id=1, source_target_pairs={{0,3},{1,0},{2,1},{3,2},{4,7},{5,4},{6,5},{7,6},{8,11},{9,8},{10,9... | collective-permute-start | bytes 786440 | tf_op jit(solution)/shard_map/roots_to_slot_groups/ppermute | solution.py:309
  50.8 10.7 %collective-permute-start.5 = (bf16[4,64,256]{2,1,0:T(8,128)(2,1)S(1)}, bf16[4,64,256]{2,1,0:T(8,128)(2,1)S(1)}, u32[]{:S(2)}, u32[]{:S(2)}) collective-permute-start(bf16[4,64,256]{2,1,0:T(8,128)(2,1)S(1)} %slice.61), channel_id=1, source_target_pairs={{0,2},{1,3},{2,0},{3,1},{4,6},{5,7},{6,4},{7,5},{8,10},{9,11},{10,... | collective-permute-start | bytes 393224 | tf_op jit(solution)/shard_map/roots_to_slot_groups/ppermute | solution.py:309
  61.5 12.4 %copy-start.7 = (bf16[4,64,256]{2,1,0:T(8,128)(2,1)}, bf16[4,64,256]{2,1,0:T(8,128)(2,1)S(1)}, u32[]{:S(2)}) copy-start(bf16[4,64,256]{2,1,0:T(8,128)(2,1)S(1)} %collective-permute-done.5.far_ref) | copy-start | bytes 393220
  61.5 12.4 %copy-start.5 = (bf16[4,64,512]{2,1,0:T(8,128)(2,1)}, bf16[4,64,512]{2,1,0:T(8,128)(2,1)S(1)}, u32[]{:S(2)}) copy-start(bf16[4,64,512]{2,1,0:T(8,128)(2,1)S(1)} %collective-permute-done.4.behind_ref) | copy-start | bytes 786436
  73.9 38.7 %all-to-all-start.2 = ((bf16[16,64,1024]{2,1,0:T(8,128)(2,1)}), bf16[16,64,1024]{2,1,0:T(8,128)(2,1)S(1)}, u32[]{:S(2)}, u32[]{:S(2)}) async-start(bf16[16,64,1024]{2,1,0:T(8,128)(2,1)} %rows_of_held_blocks.2), calls=%async_computation.2 | async-start | bytes 4194304 | tf_op jit(solution)/shard_map/rows_of_held_blocks/all_to_all | solution.py:34
  81.5 1.0 copy-start.6
  82.4 0.9 copy-start.8
  85.1 1.3 copy-start
  112.6 1.6 copy-start.1
  118.6 17.7 %all-to-all-start.3 = ((bf16[32,80,128]{2,1,0:T(8,128)(2,1)}), bf16[32,80,128]{2,1,0:T(8,128)(2,1)S(1)}, u32[]{:S(2)}, u32[]{:S(2)}) async-start(bf16[32,80,128]{2,1,0:T(8,128)(2,1)} %precondition.1), calls=%async_computation.3 | async-start | bytes 1310720 | tf_op jit(solution)/shard_map/step_to_gradient_rows/all_to_all | solution.py:325
  126.0 46.4 %copy-start.2 = (f32[3,64,1024]{2,1,0:T(8,128)S(1)}, f32[3,64,1024]{2,1,0:T(8,128)}, u32[]{:S(2)}) copy-start(f32[3,64,1024]{2,1,0:T(8,128)} %left_ref.1) | copy-start | bytes 2359300
  126.0 46.4 %copy-start.3 = (f32[3,64,1024]{2,1,0:T(8,128)S(1)}, f32[3,64,1024]{2,1,0:T(8,128)}, u32[]{:S(2)}) copy-start(f32[3,64,1024]{2,1,0:T(8,128)} %right_ref.1) | copy-start | bytes 2359300
  137.9 20.8 %all-to-all-start.4 = ((bf16[16,6,16,128]{3,2,1,0:T(8,128)(2,1)}), bf16[16,6,16,128]{3,2,1,0:T(8,128)(2,1)S(1)}, u32[]{:S(2)}, u32[]{:S(2)}) async-start(bf16[16,6,16,128]{3,2,1,0:T(8,128)(2,1)} %step_to_gradient_rows.1), calls=%async_computation.4 | async-start | bytes 786432 | tf_op jit(solution)/shard_map/step_to_gradient_rows/all_to_all | solution.py:318
  141.6 8.8 %collective-permute-start.6 = (bf16[2,64,1024]{2,1,0:T(8,128)(2,1)}, bf16[2,64,1024]{2,1,0:T(8,128)(2,1)S(1)}, u32[]{:S(2)}, u32[]{:S(2)}) collective-permute-start(bf16[2,64,1024]{2,1,0:T(8,128)(2,1)} %get-tuple-element.60), channel_id=1, source_target_pairs={{0,4},{1,5},{2,6},{3,7},{4,8},{5,9},{6,10},{7,11},{8,12},{9,13},{1... | collective-permute-start | bytes 786440 | tf_op jit(solution)/shard_map/statistics/ppermute | solution.py:303
  143.7 14.7 %collective-permute-start.7 = (bf16[2,64,1024]{2,1,0:T(8,128)(2,1)}, bf16[2,64,1024]{2,1,0:T(8,128)(2,1)S(1)}, u32[]{:S(2)}, u32[]{:S(2)}) collective-permute-start(bf16[2,64,1024]{2,1,0:T(8,128)(2,1)} %get-tuple-element.61), channel_id=1, source_target_pairs={{0,8},{1,9},{2,10},{3,11},{4,12},{5,13},{6,14},{7,15},{8,0},{9,1},... | collective-permute-start | bytes 786440 | tf_op jit(solution)/shard_map/statistics/ppermute | solution.py:303
  148.1 10.6 %collective-permute-start.8 = (bf16[2,64,1024]{2,1,0:T(8,128)(2,1)}, bf16[2,64,1024]{2,1,0:T(8,128)(2,1)S(1)}, u32[]{:S(2)}, u32[]{:S(2)}) collective-permute-start(bf16[2,64,1024]{2,1,0:T(8,128)(2,1)} %get-tuple-element.62), channel_id=1, source_target_pairs={{0,12},{1,13},{2,14},{3,15},{4,0},{5,1},{6,2},{7,3},{8,4},{9,5},{1... | collective-permute-start | bytes 786440 | tf_op jit(solution)/shard_map/statistics/ppermute | solution.py:303
  160.0 24.4 %all-to-all-start.5 = ((bf16[16,2,16,128]{3,2,1,0:T(8,128)(2,1)}), bf16[16,2,16,128]{3,2,1,0:T(8,128)(2,1)S(1)}, u32[]{:S(2)}, u32[]{:S(2)}) async-start(bf16[16,2,16,128]{3,2,1,0:T(8,128)(2,1)} %bitcast.24), calls=%async_computation.5 | async-start | bytes 262144 | tf_op jit(solution)/shard_map/statistics/all_to_all | solution.py:318

commit v5 on v4

--- a/solution.py
+++ b/solution.py
@@ -30,22 +30,18 @@
     return jnp.sum(jnp.where(same & earlier, 1, 0), axis=1).astype(jnp.int32)
 
 
-def exchange(pieces):
-    return lax.all_to_all(pieces, "tensor", split_axis=0, concat_axis=0, tiled=True)
-
-
 def tile_of(number):
     return pl.ds(number // 2 * ROWS, ROWS), pl.ds(number % 2 * LANES, LANES)
 
 
-def spread_kernel(part_ref, gradient_ref, out_ref):
-    count = gradient_ref.shape[0]
-    tiles = out_ref.shape[0] // count
-    for group in range(count):
-        column = lax.rem(group + count - part_ref[0], count)
-        for tile in range(tiles):
-            rows, lanes = tile_of(tile)
-            out_ref[group * tiles + tile] = gradient_ref[column, rows, lanes]
+def spread_kernel(half_ref, gradient_ref, out_ref):
+    tiles = out_ref.shape[0] // CORES
+    for group in range(CORES):
+        for pair in range(out_ref.shape[1]):
+            column = CORES * pair + lax.rem(group + CORES - half_ref[0], CORES)
+            for tile in range(tiles):
+                rows, lanes = tile_of(tile)
+                out_ref[group * tiles + tile, pair] = gradient_ref[column, rows, lanes]
 
 
 def pick_kernel(index_ref, tiles_ref, out_ref):
@@ -66,43 +62,45 @@
 
 
 def held_rows_kernel(column_ref, used_ref, tiles_ref, sent_ref, rows_ref, sems):
-    capacity, _, block_side = rows_ref.shape
-    places = sent_ref.shape[0]
+    capacity = rows_ref.shape[0] // CORES
+    width = rows_ref.shape[2] // CORES
+    places = sent_ref.shape[0] // CORES
     parts = places // (capacity + 1)
-    width = block_side // parts
-    tiles = tiles_ref.shape[0] // parts
+    tiles = tiles_ref.shape[0] // CORES
     copies = []
-    for slot in range(capacity + 1):
-        if slot < capacity:
-            keep = used_ref[slot] > 0
-            for part in range(parts):
-                group = lax.rem(column_ref[slot] + part, parts)
-                for tile in range(tiles):
-                    rows, lanes = tile_of(tile)
-                    lanes = pl.ds(part * width + lanes.start, LANES)
-                    value = tiles_ref[group * tiles + tile, slot]
-                    rows_ref[slot, rows, lanes] = jnp.where(keep, value, jnp.zeros_like(value))
-        for member in range(parts):
-            place = slot * parts + member
-            source = rows_ref.at[min(slot, capacity - 1)]
-            copies.append(pltpu.make_async_copy(source, sent_ref.at[place], sems.at[place]))
-            copies[-1].start()
+    for core in range(CORES):
+        for slot in range(capacity + 1):
+            held = core * capacity + min(slot, capacity - 1)
+            if slot < capacity:
+                keep = used_ref[held] > 0
+                for half in range(CORES):
+                    group = lax.rem(column_ref[held] + half, CORES)
+                    for tile in range(tiles):
+                        rows, lanes = tile_of(tile)
+                        lanes = pl.ds(half * width + lanes.start, LANES)
+                        value = tiles_ref[group * tiles + tile, held]
+                        rows_ref[held, rows, lanes] = jnp.where(keep, value, jnp.zeros_like(value))
+            for member in range(parts):
+                place = core * places + slot * parts + member
+                copies.append(
+                    pltpu.make_async_copy(rows_ref.at[held], sent_ref.at[place], sems.at[place])
+                )
+                copies[-1].start()
     for copy in copies:
         copy.wait()
 
 
-def held_rows(column_of, used, tiles, height, block_side, places):
-    capacity = tiles.shape[1]
+def held_rows(column_of, used, tiles, height, width, places):
     return pl.pallas_call(
         held_rows_kernel,
-        out_shape=jax.ShapeDtypeStruct((places, height, block_side), tiles.dtype),
+        out_shape=jax.ShapeDtypeStruct((places, height, CORES * width), tiles.dtype),
         in_specs=[SMEM, SMEM, VMEM],
-        out_specs=ANY,
+        out_specs=pl.BlockSpec(memory_space=pltpu.HBM),
         scratch_shapes=[
-            pltpu.VMEM((capacity, height, block_side), tiles.dtype),
+            pltpu.VMEM((tiles.shape[1], height, CORES * width), tiles.dtype),
             pltpu.SemaphoreType.DMA((places,)),
         ],
-        compiler_params=LIMIT,
+        compiler_params=pltpu.CompilerParams(vmem_limit_bytes=56 * 2**20),
         cost_estimate=cost(0, 4 * 2**20),
     )(column_of, used, tiles)
 
@@ -170,13 +168,31 @@
                 ]
 
 
+def join_kernel(block_ref, out_ref):
+    places = block_ref.shape[0] // CORES
+    height, width = block_ref.shape[1], block_ref.shape[2] // CORES
+    for place in range(places):
+        for part in range(out_ref.shape[1] // width):
+            out_ref[pl.ds(place * height, height), pl.ds(part * width, width)] = block_ref[
+                part % CORES * places + place, :, pl.ds(part // CORES * width, width)
+            ]
+
+
 def precondition_kernel(side, place_ref, left_ref, right_ref, block_ref, out_ref):
     y, x = place_ref[0], place_ref[1]
-    places, height, block_side = block_ref.shape
+    places, height, block_side = left_ref.shape
     width = block_side // side
     cores = out_ref.shape[0] // places
     narrow = width // side
-    block = block_ref[...].reshape(block_side, block_side)
+    block = jnp.concatenate(
+        [
+            block_ref[
+                pl.ds(part % cores * places, places), :, pl.ds(part // cores * width, width)
+            ].reshape(block_side, width)
+            for part in range(side)
+        ],
+        axis=1,
+    )
     right = jnp.concatenate([right_ref[around(y, at, side)] for at in range(side)], axis=0)
     power = jnp.zeros((1, width), jnp.float32)
     for begin in range(0, places, side):
@@ -199,9 +215,12 @@
                 place = core * places + at * side + lax.rem(x + begin // side, side)
                 out_ref[place, pl.ds(0, height), :] = share[at * height : (at + 1) * height]
     share = places // side
-    own = block_ref[pl.ds(x * share, share)].astype(jnp.float32).reshape(width, block_side)
-    own = jnp.sum(own * own, axis=0, keepdims=True)
-    grad = sum(own[:, at : at + LANES] for at in range(0, block_side, LANES))
+    grad = jnp.zeros((1, LANES), jnp.float32)
+    for core in range(cores):
+        own = block_ref[pl.ds(core * places + x * share, share)].astype(jnp.float32)
+        own = own.reshape(width, cores * width)
+        own = jnp.sum(own * own, axis=0, keepdims=True)
+        grad += sum(own[:, at : at + LANES] for at in range(0, cores * width, LANES))
     power = sum(power[:, at : at + LANES] for at in range(0, width, LANES))
     number = lax.broadcasted_iota(jnp.int32, (TAIL, LANES), 0)
     tail = jnp.zeros((TAIL, LANES), jnp.float32)
@@ -213,7 +232,7 @@
 
 
 def precondition(place, left, right, block):
-    places, height, block_side = block.shape
+    places, height, block_side = left.shape
     side = right.shape[0]
     width = block_side // side
     return pl.pallas_call(
@@ -221,7 +240,7 @@
         out_shape=jax.ShapeDtypeStruct((places * CORES, height + TAIL, LANES), jnp.bfloat16),
         in_specs=[SMEM] + [VMEM] * 3,
         out_specs=VMEM,
-        compiler_params=pltpu.CompilerParams(vmem_limit_bytes=32 * 2**20),
+        compiler_params=pltpu.CompilerParams(vmem_limit_bytes=20 * 2**20),
         cost_estimate=cost(2 * block_side * block_side * (block_side + width), 6 * 2**20),
     )(place, left, right, block)
 
@@ -308,9 +327,6 @@
         ]
         return lax.ppermute(value, "tensor", pairs)
 
-    def over_rows(value):
-        return lax.all_to_all(value, "fsdp", split_axis=0, concat_axis=0, tiled=True)
-
     chips = fsdp_count // CORES
 
     def along_z(value):
@@ -331,20 +347,23 @@
             axis_index_groups=planes,
         )
 
-    part = (fsdp_index % side).astype(jnp.int32).reshape(1)
-    group = fsdp_index // (fsdp_count // col_blocks)
+    chip = fsdp_index // CORES
+    group = chip // (chips // CORES)
+    half_here = (chip % CORES).astype(jnp.int32).reshape(1)
 
     with jax.named_scope("gradient_spread"):
         spread = pl.pallas_call(
             spread_kernel,
-            out_shape=jax.ShapeDtypeStruct((fsdp_count, ROWS, LANES), gradient.dtype),
+            out_shape=jax.ShapeDtypeStruct(
+                (chips, col_blocks // CORES, ROWS, LANES), gradient.dtype
+            ),
             in_specs=[SMEM, VMEM],
             out_specs=VMEM,
             compiler_params=LIMIT,
             cost_estimate=cost(0, 2**18),
-        )(part, gradient)
+        )(half_here, gradient)
         spread, left_root, right_root = lax.optimization_barrier((spread, left_root, right_root))
-        spread = over_rows(spread)
+        spread = along_z(spread).reshape(-1, ROWS, LANES)
 
     with jax.named_scope("where_blocks_go"):
         owners_flat = block_owner.reshape(-1)
@@ -352,28 +371,24 @@
         column_flat, band_flat = numbers // row_blocks, numbers % row_blocks
         entries = owners_flat * capacity + slot_numbers(owners_flat)
         held_at = entries[:, None] == jnp.arange(fsdp_count * capacity)[None, :]
-        source = band_flat * side + (group - column_flat + side) % side
+        source = band_flat * CORES + (group - column_flat % CORES + CORES) % CORES
+        source = source * (col_blocks // CORES) + column_flat // CORES
         forward = jnp.sum(jnp.where(held_at, source[:, None], 0), axis=0).astype(jnp.int32)
-        mine = entries[:, None] == (fsdp_index * capacity + jnp.arange(capacity))[None, :]
-        used = jnp.any(mine, axis=0).astype(jnp.int32)
-        column_of = jnp.sum(jnp.where(mine, column_flat[:, None], 0), axis=0).astype(jnp.int32)
-        chip = fsdp_index // CORES
         ours = (chip * CORES * capacity + jnp.arange(CORES * capacity))[None, :]
-        columns_here = jnp.sum(
-            jnp.where(entries[:, None] == ours, column_flat[:, None], 0), axis=0
-        ).astype(jnp.int32)
+        ours = entries[:, None] == ours
+        used = jnp.any(ours, axis=0).astype(jnp.int32)
+        columns_here = jnp.sum(jnp.where(ours, column_flat[:, None], 0), axis=0).astype(jnp.int32)
         homes = jnp.arange(chips)[:, None]
-        turn = (chip // (chips // CORES) - homes % CORES + CORES) % CORES
+        turn = (group - homes % CORES + CORES) % CORES
         wanted = CORES * jnp.arange(col_blocks // CORES)[None, :] + turn
         wanted = (wanted * row_blocks + homes // CORES).reshape(-1)
         backward = jnp.sum(
             jnp.where(wanted[:, None] == numbers[None, :], entries[None, :], 0), axis=1
         ).astype(jnp.int32)
-        half_here = (chip % CORES).astype(jnp.int32).reshape(1)
 
     with jax.named_scope("gradient_to_owners"):
-        sent = pick(forward, spread).reshape(fsdp_count, capacity, ROWS, LANES)
-        tiles = over_rows(sent)
+        sent = pick(forward, spread).reshape(chips, CORES * capacity, ROWS, LANES)
+        tiles = along_z(sent)
 
     with jax.named_scope("roots_to_slot_groups"):
         turned = pl.pallas_call(
@@ -406,9 +421,11 @@
         tiles, right_rows, *lefts = lax.optimization_barrier((tiles, right_rows, *lefts))
 
     with jax.named_scope("rows_of_held_blocks"):
-        sent = held_rows(column_of, used, tiles, local_height, block_side, tensor_count)
+        sent = held_rows(
+            columns_here, used, tiles, local_height, row_depth, CORES * tensor_count
+        )
         sent, *lefts = lax.optimization_barrier((sent, *lefts))
-        block = exchange(sent)
+        block = over_chip_planes(sent)
         left = pl.pallas_call(
             functools.partial(whole_root_kernel, side),
             out_shape=jax.ShapeDtypeStruct((block_side, block_side), left_root.dtype),
@@ -426,7 +443,14 @@
     with jax.named_scope("step_to_gradient_rows"):
         back = over_chip_planes(leaving)
         block, leaving = lax.optimization_barrier((block, leaving))
-        block = block.reshape(block_side, block_side)
+        block = pl.pallas_call(
+            join_kernel,
+            out_shape=jax.ShapeDtypeStruct((block_side, block_side), block.dtype),
+            in_specs=[VMEM],
+            out_specs=VMEM,
+            compiler_params=LIMIT,
+            cost_estimate=cost(0, 4 * 2**20),
+        )(block)
         own_rows = lax.dynamic_index_in_dim(
             block.reshape(side, side, local_height, block_side), x, 1, keepdims=False
         ).reshape(row_depth, block_side)

time: 188 us -> 182 us (0.968)
  waiting for transfers between devices: 76 us -> 56.6 us
  starting transfers between devices: 78.8 us -> 88.4 us
  local copies, waits for them, and re-layouts: 7.42 us -> 9.51 us
    all_to_all x3 -> x0, waiting for transfers between devices: 41.3 us -> none  [the longest x1 26.2 us: exchange(): lax.all_to_all(pieces, 'tensor', split_axis=0, concat_axis=0, tiled=True)]
    all_to_all x3 -> x0, starting transfers between devices: 31.7 us -> none  [the longest x2 24.4 us: over_rows(): lax.all_to_all(value, 'fsdp', split_axis=0, concat_axis=0, tiled=True)]
    all_to_all x2 -> x4, starting transfers between devices: 16.1 us -> 44.3 us  [along_z(): lax.all_to_all(value, 'fsdp', split_axis=0, concat_axis=0, tiled=True, ax...]
    all_to_all x1 -> x2, waiting for transfers between devices: 9.32 us -> 32.6 us  [over_chip_planes(): lax.all_to_all(value, ('fsdp', 'tensor'), split_axis=0, concat_axis=0, ti...]
    all_to_all x1 -> x2, starting transfers between devices: 5.36 us -> 18.4 us  [over_chip_planes(): lax.all_to_all(value, ('fsdp', 'tensor'), split_axis=0, concat_axis=0, ti...]
    ppermute x3, waiting for transfers between devices: 6.97 us -> 4.69 us  [along_x(): return lax.ppermute(value, 'tensor', pairs)]
    unnamed x22 -> x26, local copies, waits for them, and re-layouts: 6.66 us -> 8.75 us
    all_to_all x2 -> x4, waiting for transfers between devices: 10 us -> 11 us  [along_z(): lax.all_to_all(value, 'fsdp', split_axis=0, concat_axis=0, tiled=True, ax...]
  transfers between devices with their start and end apart: 15 -> 15, of which waited for: 8 -> 7; matrix products, arithmetic and copies ran while one was open for 3% -> 4% of each run, Pallas kernels for 3% -> 3%
where the time goes in v5:
time: 182 us; the launch traced here: 179 us
  starting transfers between devices  88.4 us (49%)
  waiting for transfers between devices  56.6 us (31%)
  Pallas kernels  17.2 us (9%)
  local copies, waits for them, and re-layouts  9.51 us (5%)
  other arithmetic  4.4 us (2%)
    all_to_all x4, starting transfers between devices, along_z(): lax.all_to_all(value, 'fsdp', split_axis=0, concat_axis=0, tiled=True, ax...  44.3 us
    all_to_all x2, waiting for transfers between devices, over_chip_planes(): lax.all_to_all(value, ('fsdp', 'tensor'), split_axis=0, concat_axis=0, ti...  32.6 us
    all_to_all x2, starting transfers between devices, over_chip_planes(): lax.all_to_all(value, ('fsdp', 'tensor'), split_axis=0, concat_axis=0, ti...  18.4 us
    ppermute x6, starting transfers between devices, along_y(): return lax.ppermute(value, 'tensor', pairs)  15.8 us
    all_to_all x4, waiting for transfers between devices, along_z(): lax.all_to_all(value, 'fsdp', split_axis=0, concat_axis=0, tiled=True, ax...  11 us
    ppermute x3, starting transfers between devices, along_x(): return lax.ppermute(value, 'tensor', pairs)  9.92 us
    unnamed x26, local copies, waits for them, and re-layouts  8.75 us
    ppermute x6, waiting for transfers between devices, along_y(): return lax.ppermute(value, 'tensor', pairs)  8.33 us
  transfers between devices with their start and end apart: 15, of which 7 were waited for; matrix products, arithmetic and copies ran while one was open for 4% of the time, Pallas kernels for 3%

profile of v5, /device:TPU:1, one launch (start us, length us, event | category | flops | bytes accessed | tf_op | source)
XLA Modules:
  0.0 179.0 jit_solution(1818729754474272498)
XLA Ops:
  0.7 0.9 copy-done.9
  1.6 0.7 gradient_spread.1
  2.3 15.7 %all-to-all-start = ((bf16[16,2,16,128]{3,2,1,0:T(8,128)(2,1)}), bf16[16,2,16,128]{3,2,1,0:T(8,128)(2,1)S(1)}, u32[]{:S(2)}, u32[]{:S(2)}) async-start(bf16[16,2,16,128]{3,2,1,0:T(8,128)(2,1)} %gradient_spread.1), calls=%async_computation | async-start | bytes 262144 | tf_op jit(solution)/shard_map/gradient_spread/all_to_all | solution.py:334
  18.1 0.1 pad_add_fusion.place_ref
  18.2 1.0 copy-done.4
  19.2 0.7 roots_to_slot_groups.1
  19.9 1.2 fusion.9
  21.1 3.2 %collective-permute-start = (bf16[2,64,1024]{2,1,0:T(8,128)(2,1)S(1)}, bf16[2,64,1024]{2,1,0:T(8,128)(2,1)S(1)}, u32[]{:S(2)}, u32[]{:S(2)}) collective-permute-start(bf16[2,64,1024]{2,1,0:T(8,128)(2,1)S(1)} %get-tuple-element.82), channel_id=1, source_target_pairs={{0,4},{1,5},{2,6},{3,7},{4,8},{5,9},{6,10},{7,11},{12,0},{13,1},{1... | collective-permute-start | bytes 786440 | tf_op jit(solution)/shard_map/roots_to_slot_groups/ppermute | solution.py:322
  24.3 2.9 %collective-permute-start.1 = (bf16[2,64,1024]{2,1,0:T(8,128)(2,1)S(1)}, bf16[2,64,1024]{2,1,0:T(8,128)(2,1)S(1)}, u32[]{:S(2)}, u32[]{:S(2)}) collective-permute-start(bf16[2,64,1024]{2,1,0:T(8,128)(2,1)S(1)} %get-tuple-element.83), channel_id=1, source_target_pairs={{0,8},{1,9},{2,10},{3,11},{8,0},{9,1},{10,2},{11,3},{12,4},{13,5},... | collective-permute-start | bytes 786440 | tf_op jit(solution)/shard_map/roots_to_slot_groups/ppermute | solution.py:322
  27.2 1.3 collective-permute-start.2
  28.6 0.1 reshape.235
  28.7 0.2 select_reduce_fusion.2
  28.9 0.1 select_reduce_fusion.index_ref
  29.0 1.0 all-to-all-done
  30.0 1.4 gradient_to_owners.1
  31.4 10.4 %all-to-all-start.1 = ((bf16[16,6,16,128]{3,2,1,0:T(8,128)(2,1)}), bf16[16,6,16,128]{3,2,1,0:T(8,128)(2,1)S(1)}, u32[]{:S(2)}, u32[]{:S(2)}) async-start(bf16[16,6,16,128]{3,2,1,0:T(8,128)(2,1)} %bitcast.4), calls=%async_computation.1 | async-start | bytes 786432 | tf_op jit(solution)/shard_map/gradient_to_owners/all_to_all | solution.py:334
  41.8 0.0 collective-permute-done.2
  41.9 0.1 pad_maximum_fusion.1.own_ref
  42.0 3.1 %collective-permute-start.3 = (bf16[4,64,768]{2,1,0:T(8,128)(2,1)S(1)}, bf16[4,64,768]{2,1,0:T(8,128)(2,1)S(1)}, u32[]{:S(2)}, u32[]{:S(2)}) collective-permute-start(bf16[4,64,768]{2,1,0:T(8,128)(2,1)S(1)} %pad_maximum_fusion.2), channel_id=1, source_target_pairs={{0,1},{1,2},{2,3},{3,0},{4,5},{5,6},{6,7},{7,4},{8,9},{9,10},{10,1... | collective-permute-start | bytes 1179656 | tf_op jit(solution)/shard_map/roots_to_slot_groups/ppermute | solution.py:328
  45.2 3.4 %collective-permute-start.4 = (bf16[4,64,512]{2,1,0:T(8,128)(2,1)S(1)}, bf16[4,64,512]{2,1,0:T(8,128)(2,1)S(1)}, u32[]{:S(2)}, u32[]{:S(2)}) collective-permute-start(bf16[4,64,512]{2,1,0:T(8,128)(2,1)S(1)} %get-tuple-element.85), channel_id=1, source_target_pairs={{0,3},{1,0},{2,1},{3,2},{4,7},{5,4},{6,5},{7,6},{8,11},{9,8},{10,9... | collective-permute-start | bytes 786440 | tf_op jit(solution)/shard_map/roots_to_slot_groups/ppermute | solution.py:328
  48.6 0.7 fusion.23.column_ref
  49.3 3.4 %collective-permute-start.5 = (bf16[4,64,256]{2,1,0:T(8,128)(2,1)S(1)}, bf16[4,64,256]{2,1,0:T(8,128)(2,1)S(1)}, u32[]{:S(2)}, u32[]{:S(2)}) collective-permute-start(bf16[4,64,256]{2,1,0:T(8,128)(2,1)S(1)} %slice.61), channel_id=1, source_target_pairs={{0,2},{1,3},{2,0},{3,1},{4,6},{5,7},{6,4},{7,5},{8,10},{9,11},{10,... | collective-permute-start | bytes 393224 | tf_op jit(solution)/shard_map/roots_to_slot_groups/ppermute | solution.py:328
  52.7 0.2 compare_reduce_fusion
  52.9 0.6 convert_element_type.9.used_ref
  53.5 0.1 pad_maximum_fusion.right_ref
  53.5 4.7 %collective-permute-done.5.far_ref = bf16[4,64,256]{2,1,0:T(8,128)(2,1)S(1)} collective-permute-done((bf16[4,64,256]{2,1,0:T(8,128)(2,1)S(1)}, bf16[4,64,256]{2,1,0:T(8,128)(2,1)S(1)}, u32[]{:S(2)}, u32[]{:S(2)}) %collective-permute-start.5) | collective-permute-done | bytes 131104 | tf_op jit(solution)/shard_map/roots_to_slot_groups/ppermute | solution.py:328
  58.2 0.7 copy-done.7
  58.9 0.0 collective-permute-done.4.behind_ref
  58.9 0.7 copy-done.5
  59.6 0.7 copy-done.11
  60.3 2.7 %rows_of_held_blocks.2 = bf16[32,64,512]{2,1,0:T(8,128)(2,1)} custom-call(s32[6]{0:T(128)} %fusion.23.column_ref, s32[6]{0:T(128)} %convert_element_type.9.used_ref, bf16[16,6,16,128]{3,2,1,0:T(8,128)(2,1)} %copy-done.11), custom_call_target="tpu_custom_call" | custom-call | bytes 4194304 | tf_op jit(solution)/shard_map/rows_of_held_blocks/pallas_call | solution.py:94
  63.0 13.9 %all-to-all-start.2 = ((bf16[32,64,512]{2,1,0:T(8,128)(2,1)}), bf16[32,64,512]{2,1,0:T(8,128)(2,1)S(1)}, u32[]{:S(2)}, u32[]{:S(2)}) async-start(bf16[32,64,512]{2,1,0:T(8,128)(2,1)} %rows_of_held_blocks.2), calls=%async_computation.2 | async-start | bytes 4194304 | tf_op jit(solution)/shard_map/rows_of_held_blocks/all_to_all | solution.py:341
  77.0 0.0 copy-start.6
  77.0 0.9 copy-done.6
  78.0 0.9 copy-done.8
  78.9 1.7 rows_of_held_blocks.3
  80.6 1.3 copy-done
  81.9 23.4 %all-to-all-done.2.block_ref = bf16[32,64,512]{2,1,0:T(8,128)(2,1)S(1)} async-done(((bf16[32,64,512]{2,1,0:T(8,128)(2,1)}), bf16[32,64,512]{2,1,0:T(8,128)(2,1)S(1)}, u32[]{:S(2)}, u32[]{:S(2)}) %all-to-all-start.2) | async-done | bytes 2097184 | tf_op jit(solution)/shard_map/rows_of_held_blocks/all_to_all | solution.py:341
  105.3 1.6 copy-done.1
  106.9 4.5 %precondition.1 = bf16[32,80,128]{2,1,0:T(8,128)(2,1)} custom-call(s32[2]{0:T(128)S(1)} %pad_add_fusion.place_ref, bf16[16,64,1024]{2,1,0:T(8,128)(2,1)S(1)} %bitcast.40, bf16[4,64,1024]{2,1,0:T(8,128)(2,1)S(1)} %pad_maximum_fusion.right_ref, bf16[32,64,512]{2,1,0:T(8,128)(2,1)S(1)} %all-to-all-done.2.block_ref), custom_call_target="tpu_custom_call" | custom-call | flops 2684354560 | bytes 6291456 | tf_op jit(solution)/shard_map/precondition/pallas_call | solution.py:238
  111.4 4.5 %all-to-all-start.3 = ((bf16[32,80,128]{2,1,0:T(8,128)(2,1)}), bf16[32,80,128]{2,1,0:T(8,128)(2,1)S(1)}, u32[]{:S(2)}, u32[]{:S(2)}) async-start(bf16[32,80,128]{2,1,0:T(8,128)(2,1)} %precondition.1), calls=%async_computation.3 | async-start | bytes 1310720 | tf_op jit(solution)/shard_map/step_to_gradient_rows/all_to_all | solution.py:341
  115.9 0.1 step_to_gradient_rows.2
  116.0 0.4 constant_dynamic-slice_fusion.3
  116.4 0.8 convolution_convert_fusion
  117.3 0.7 convolution_convert_fusion.1
  118.1 0.0 copy-start.2
  118.1 0.0 copy-start.3
  118.1 0.9 fusion.15
  119.0 9.2 %all-to-all-done.3.back_ref = bf16[32,80,128]{2,1,0:T(8,128)(2,1)S(1)} async-done(((bf16[32,80,128]{2,1,0:T(8,128)(2,1)}), bf16[32,80,128]{2,1,0:T(8,128)(2,1)S(1)}, u32[]{:S(2)}, u32[]{:S(2)}) %all-to-all-start.3) | async-done | bytes 655392 | tf_op jit(solution)/shard_map/step_to_gradient_rows/all_to_all | solution.py:341
  128.2 1.6 step_to_gradient_rows.3
  129.8 5.7 %all-to-all-start.4 = ((bf16[16,6,16,128]{3,2,1,0:T(8,128)(2,1)}), bf16[16,6,16,128]{3,2,1,0:T(8,128)(2,1)S(1)}, u32[]{:S(2)}, u32[]{:S(2)}) async-start(bf16[16,6,16,128]{3,2,1,0:T(8,128)(2,1)} %step_to_gradient_rows.3), calls=%async_computation.4 | async-start | bytes 786432 | tf_op jit(solution)/shard_map/step_to_gradient_rows/all_to_all | solution.py:334
  135.5 2.0 %collective-permute-start.6 = (bf16[2,64,1024]{2,1,0:T(8,128)(2,1)}, bf16[2,64,1024]{2,1,0:T(8,128)(2,1)S(1)}, u32[]{:S(2)}, u32[]{:S(2)}) collective-permute-start(bf16[2,64,1024]{2,1,0:T(8,128)(2,1)} %get-tuple-element.60), channel_id=1, source_target_pairs={{0,4},{1,5},{2,6},{3,7},{4,8},{5,9},{6,10},{7,11},{8,12},{9,13},{1... | collective-permute-start | bytes 786440 | tf_op jit(solution)/shard_map/statistics/ppermute | solution.py:322
  137.6 4.4 %collective-permute-start.7 = (bf16[2,64,1024]{2,1,0:T(8,128)(2,1)}, bf16[2,64,1024]{2,1,0:T(8,128)(2,1)S(1)}, u32[]{:S(2)}, u32[]{:S(2)}) collective-permute-start(bf16[2,64,1024]{2,1,0:T(8,128)(2,1)} %get-tuple-element.61), channel_id=1, source_target_pairs={{0,8},{1,9},{2,10},{3,11},{4,12},{5,13},{6,14},{7,15},{8,0},{9,1},... | collective-permute-start | bytes 786440 | tf_op jit(solution)/shard_map/statistics/ppermute | solution.py:322
  142.0 1.9 %collective-permute-start.8 = (bf16[2,64,1024]{2,1,0:T(8,128)(2,1)}, bf16[2,64,1024]{2,1,0:T(8,128)(2,1)S(1)}, u32[]{:S(2)}, u32[]{:S(2)}) collective-permute-start(bf16[2,64,1024]{2,1,0:T(8,128)(2,1)} %get-tuple-element.62), channel_id=1, source_target_pairs={{0,12},{1,13},{2,14},{3,15},{4,0},{5,1},{6,2},{7,3},{8,4},{9,5},{1... | collective-permute-start | bytes 786440 | tf_op jit(solution)/shard_map/statistics/ppermute | solution.py:322
  143.9 0.1 multiply_add_fusion
  144.0 0.1 add.240
  144.1 0.2 select_reduce_fusion.1.index_ref
  144.3 8.0 %collective-permute-done.7.refs_2_ = bf16[2,64,1024]{2,1,0:T(8,128)(2,1)S(1)} collective-permute-done((bf16[2,64,1024]{2,1,0:T(8,128)(2,1)}, bf16[2,64,1024]{2,1,0:T(8,128)(2,1)S(1)}, u32[]{:S(2)}, u32[]{:S(2)}) %collective-permute-start.7) | collective-permute-done | bytes 262176 | tf_op jit(solution)/shard_map/statistics/ppermute | solution.py:322
  152.3 0.3 collective-permute-done.8.refs_3_
  152.6 1.2 statistics.2
  153.8 12.5 %all-to-all-start.5 = ((bf16[16,2,16,128]{3,2,1,0:T(8,128)(2,1)}), bf16[16,2,16,128]{3,2,1,0:T(8,128)(2,1)S(1)}, u32[]{:S(2)}, u32[]{:S(2)}) async-start(bf16[16,2,16,128]{3,2,1,0:T(8,128)(2,1)} %bitcast.24), calls=%async_computation.5 | async-start | bytes 262144 | tf_op jit(solution)/shard_map/statistics/all_to_all | solution.py:334
  166.3 1.9 %statistics.3 = (f32[3,64,1024]{2,1,0:T(8,128)}, f32[3,64,1024]{2,1,0:T(8,128)}) custom-call(s32[2]{0:T(128)S(1)} %pad_add_fusion.place_ref, f32[3,64,1024]{2,1,0:T(8,128)S(1)} %copy-done.2, f32[3,64,1024]{2,1,0:T(8,128)S(1)} %copy-done.3, bf16[2,64,1024]{2,1,0:T(8,128)(2,1)S(1)} %get-tuple-element.64.refs_0_, ...), custom_call_target="tpu_custom_call" | custom-call | bytes 4194304 | tf_op jit(solution)/shard_map/statistics/pallas_call | solution.py:492
  168.3 10.0 %all-to-all-done.5.tiles_ref = bf16[16,2,16,128]{3,2,1,0:T(8,128)(2,1)S(1)} async-done(((bf16[16,2,16,128]{3,2,1,0:T(8,128)(2,1)}), bf16[16,2,16,128]{3,2,1,0:T(8,128)(2,1)S(1)}, u32[]{:S(2)}, u32[]{:S(2)}) %all-to-all-start.5) | async-done | bytes 131104 | tf_op jit(solution)/shard_map/statistics/all_to_all | solution.py:334
  178.3 0.7 update.1
  (34 shorter events, 0.3 us)
Async XLA Ops:
  0.6 27.9 %copy-start.12 = (s32[4,8]{1,0:T(4,128)S(1)}, s32[4,8]{1,0:T(4,128)}, u32[]{:S(2)}) copy-start(s32[4,8]{1,0:T(4,128)} %param.7) | copy-start | bytes 388
  0.7 0.9 copy-start.9
  2.3 27.8 %all-to-all-start = ((bf16[16,2,16,128]{3,2,1,0:T(8,128)(2,1)}), bf16[16,2,16,128]{3,2,1,0:T(8,128)(2,1)S(1)}, u32[]{:S(2)}, u32[]{:S(2)}) async-start(bf16[16,2,16,128]{3,2,1,0:T(8,128)(2,1)} %gradient_spread.1), calls=%async_computation | async-start | bytes 262144 | tf_op jit(solution)/shard_map/gradient_spread/all_to_all | solution.py:334
  18.2 1.0 copy-start.4
  21.1 20.6 %collective-permute-start = (bf16[2,64,1024]{2,1,0:T(8,128)(2,1)S(1)}, bf16[2,64,1024]{2,1,0:T(8,128)(2,1)S(1)}, u32[]{:S(2)}, u32[]{:S(2)}) collective-permute-start(bf16[2,64,1024]{2,1,0:T(8,128)(2,1)S(1)} %get-tuple-element.82), channel_id=1, source_target_pairs={{0,4},{1,5},{2,6},{3,7},{4,8},{5,9},{6,10},{7,11},{12,0},{13,1},{1... | collective-permute-start | bytes 786440 | tf_op jit(solution)/shard_map/roots_to_slot_groups/ppermute | solution.py:322
  24.3 17.5 %collective-permute-start.1 = (bf16[2,64,1024]{2,1,0:T(8,128)(2,1)S(1)}, bf16[2,64,1024]{2,1,0:T(8,128)(2,1)S(1)}, u32[]{:S(2)}, u32[]{:S(2)}) collective-permute-start(bf16[2,64,1024]{2,1,0:T(8,128)(2,1)S(1)} %get-tuple-element.83), channel_id=1, source_target_pairs={{0,8},{1,9},{2,10},{3,11},{8,0},{9,1},{10,2},{11,3},{12,4},{13,5},... | collective-permute-start | bytes 786440 | tf_op jit(solution)/shard_map/roots_to_slot_groups/ppermute | solution.py:322
  27.2 14.6 %collective-permute-start.2 = (bf16[2,64,1024]{2,1,0:T(8,128)(2,1)S(1)}, bf16[2,64,1024]{2,1,0:T(8,128)(2,1)S(1)}, u32[]{:S(2)}, u32[]{:S(2)}) collective-permute-start(bf16[2,64,1024]{2,1,0:T(8,128)(2,1)S(1)} %get-tuple-element.84), channel_id=1, source_target_pairs={{4,0},{5,1},{6,2},{7,3},{8,4},{9,5},{10,6},{11,7},{12,8},{13,9},{1... | collective-permute-start | bytes 786440 | tf_op jit(solution)/shard_map/roots_to_slot_groups/ppermute | solution.py:322
  31.4 28.2 %all-to-all-start.1 = ((bf16[16,6,16,128]{3,2,1,0:T(8,128)(2,1)}), bf16[16,6,16,128]{3,2,1,0:T(8,128)(2,1)S(1)}, u32[]{:S(2)}, u32[]{:S(2)}) async-start(bf16[16,6,16,128]{3,2,1,0:T(8,128)(2,1)} %bitcast.4), calls=%async_computation.1 | async-start | bytes 786432 | tf_op jit(solution)/shard_map/gradient_to_owners/all_to_all | solution.py:334
  42.0 17.5 %collective-permute-start.3 = (bf16[4,64,768]{2,1,0:T(8,128)(2,1)S(1)}, bf16[4,64,768]{2,1,0:T(8,128)(2,1)S(1)}, u32[]{:S(2)}, u32[]{:S(2)}) collective-permute-start(bf16[4,64,768]{2,1,0:T(8,128)(2,1)S(1)} %pad_maximum_fusion.2), channel_id=1, source_target_pairs={{0,1},{1,2},{2,3},{3,0},{4,5},{5,6},{6,7},{7,4},{8,9},{9,10},{10,1... | collective-permute-start | bytes 1179656 | tf_op jit(solution)/shard_map/roots_to_slot_groups/ppermute | solution.py:328
  45.2 13.7 %collective-permute-start.4 = (bf16[4,64,512]{2,1,0:T(8,128)(2,1)S(1)}, bf16[4,64,512]{2,1,0:T(8,128)(2,1)S(1)}, u32[]{:S(2)}, u32[]{:S(2)}) collective-permute-start(bf16[4,64,512]{2,1,0:T(8,128)(2,1)S(1)} %get-tuple-element.85), channel_id=1, source_target_pairs={{0,3},{1,0},{2,1},{3,2},{4,7},{5,4},{6,5},{7,6},{8,11},{9,8},{10,9... | collective-permute-start | bytes 786440 | tf_op jit(solution)/shard_map/roots_to_slot_groups/ppermute | solution.py:328
  49.3 9.0 %collective-permute-start.5 = (bf16[4,64,256]{2,1,0:T(8,128)(2,1)S(1)}, bf16[4,64,256]{2,1,0:T(8,128)(2,1)S(1)}, u32[]{:S(2)}, u32[]{:S(2)}) collective-permute-start(bf16[4,64,256]{2,1,0:T(8,128)(2,1)S(1)} %slice.61), channel_id=1, source_target_pairs={{0,2},{1,3},{2,0},{3,1},{4,6},{5,7},{6,4},{7,5},{8,10},{9,11},{10,... | collective-permute-start | bytes 393224 | tf_op jit(solution)/shard_map/roots_to_slot_groups/ppermute | solution.py:328
  58.2 0.7 copy-start.7
  58.9 0.7 copy-start.5
  59.6 0.7 copy-start.11
  63.0 42.3 %all-to-all-start.2 = ((bf16[32,64,512]{2,1,0:T(8,128)(2,1)}), bf16[32,64,512]{2,1,0:T(8,128)(2,1)S(1)}, u32[]{:S(2)}, u32[]{:S(2)}) async-start(bf16[32,64,512]{2,1,0:T(8,128)(2,1)} %rows_of_held_blocks.2), calls=%async_computation.2 | async-start | bytes 4194304 | tf_op jit(solution)/shard_map/rows_of_held_blocks/all_to_all | solution.py:341
  77.0 1.0 copy-start.6
  78.0 0.9 copy-start.8
  80.6 1.3 copy-start
  105.3 1.6 copy-start.1
  111.4 16.8 %all-to-all-start.3 = ((bf16[32,80,128]{2,1,0:T(8,128)(2,1)}), bf16[32,80,128]{2,1,0:T(8,128)(2,1)S(1)}, u32[]{:S(2)}, u32[]{:S(2)}) async-start(bf16[32,80,128]{2,1,0:T(8,128)(2,1)} %precondition.1), calls=%async_computation.3 | async-start | bytes 1310720 | tf_op jit(solution)/shard_map/step_to_gradient_rows/all_to_all | solution.py:341
  117.3 10.9 %copy-start.10 = (s32[6]{0:T(128)S(1)}, s32[6]{0:T(128)}, u32[]{:S(2)}) copy-start(s32[6]{0:T(128)} %fusion.23.column_ref) | copy-start | bytes 76
  118.1 48.2 %copy-start.2 = (f32[3,64,1024]{2,1,0:T(8,128)S(1)}, f32[3,64,1024]{2,1,0:T(8,128)}, u32[]{:S(2)}) copy-start(f32[3,64,1024]{2,1,0:T(8,128)} %left_ref.1) | copy-start | bytes 2359300
  118.1 48.2 %copy-start.3 = (f32[3,64,1024]{2,1,0:T(8,128)S(1)}, f32[3,64,1024]{2,1,0:T(8,128)}, u32[]{:S(2)}) copy-start(f32[3,64,1024]{2,1,0:T(8,128)} %right_ref.1) | copy-start | bytes 2359300
  129.8 22.8 %all-to-all-start.4 = ((bf16[16,6,16,128]{3,2,1,0:T(8,128)(2,1)}), bf16[16,6,16,128]{3,2,1,0:T(8,128)(2,1)S(1)}, u32[]{:S(2)}, u32[]{:S(2)}) async-start(bf16[16,6,16,128]{3,2,1,0:T(8,128)(2,1)} %step_to_gradient_rows.3), calls=%async_computation.4 | async-start | bytes 786432 | tf_op jit(solution)/shard_map/step_to_gradient_rows/all_to_all | solution.py:334
  135.5 8.7 %collective-permute-start.6 = (bf16[2,64,1024]{2,1,0:T(8,128)(2,1)}, bf16[2,64,1024]{2,1,0:T(8,128)(2,1)S(1)}, u32[]{:S(2)}, u32[]{:S(2)}) collective-permute-start(bf16[2,64,1024]{2,1,0:T(8,128)(2,1)} %get-tuple-element.60), channel_id=1, source_target_pairs={{0,4},{1,5},{2,6},{3,7},{4,8},{5,9},{6,10},{7,11},{8,12},{9,13},{1... | collective-permute-start | bytes 786440 | tf_op jit(solution)/shard_map/statistics/ppermute | solution.py:322
  137.6 14.7 %collective-permute-start.7 = (bf16[2,64,1024]{2,1,0:T(8,128)(2,1)}, bf16[2,64,1024]{2,1,0:T(8,128)(2,1)S(1)}, u32[]{:S(2)}, u32[]{:S(2)}) collective-permute-start(bf16[2,64,1024]{2,1,0:T(8,128)(2,1)} %get-tuple-element.61), channel_id=1, source_target_pairs={{0,8},{1,9},{2,10},{3,11},{4,12},{5,13},{6,14},{7,15},{8,0},{9,1},... | collective-permute-start | bytes 786440 | tf_op jit(solution)/shard_map/statistics/ppermute | solution.py:322
  142.0 10.6 %collective-permute-start.8 = (bf16[2,64,1024]{2,1,0:T(8,128)(2,1)}, bf16[2,64,1024]{2,1,0:T(8,128)(2,1)S(1)}, u32[]{:S(2)}, u32[]{:S(2)}) collective-permute-start(bf16[2,64,1024]{2,1,0:T(8,128)(2,1)} %get-tuple-element.62), channel_id=1, source_target_pairs={{0,12},{1,13},{2,14},{3,15},{4,0},{5,1},{6,2},{7,3},{8,4},{9,5},{1... | collective-permute-start | bytes 786440 | tf_op jit(solution)/shard_map/statistics/ppermute | solution.py:322
  153.8 24.5 %all-to-all-start.5 = ((bf16[16,2,16,128]{3,2,1,0:T(8,128)(2,1)}), bf16[16,2,16,128]{3,2,1,0:T(8,128)(2,1)S(1)}, u32[]{:S(2)}, u32[]{:S(2)}) async-start(bf16[16,2,16,128]{3,2,1,0:T(8,128)(2,1)} %bitcast.24), calls=%async_computation.5 | async-start | bytes 262144 | tf_op jit(solution)/shard_map/statistics/all_to_all | solution.py:334

commit v6 on v5

--- a/solution.py
+++ b/solution.py
@@ -194,13 +194,13 @@
         axis=1,
     )
     right = jnp.concatenate([right_ref[around(y, at, side)] for at in range(side)], axis=0)
+    mixed = lax.dot_general(
+        block, right, (((1,), (1,)), ((), ())), preferred_element_type=jnp.float32
+    ).astype(jnp.bfloat16)
     power = jnp.zeros((1, width), jnp.float32)
     for begin in range(0, places, side):
         left = left_ref[pl.ds(begin, side)].reshape(side * height, block_side)
-        mixed = jnp.dot(left, block, preferred_element_type=jnp.float32).astype(jnp.bfloat16)
-        product = lax.dot_general(
-            mixed, right, (((1,), (1,)), ((), ())), preferred_element_type=jnp.float32
-        )
+        product = jnp.dot(left, mixed, preferred_element_type=jnp.float32)
         power += jnp.sum(product * product, axis=0, keepdims=True)
         product = product.astype(jnp.bfloat16)
         for core in range(cores):

time: 182 us -> 181 us (level)
  no operation moved by 1% of the time
where the time goes in v6:
time: 181 us; the launch traced here: 178 us
  starting transfers between devices  88.4 us (49%)
  waiting for transfers between devices  56.6 us (31%)
  Pallas kernels  16.4 us (9%)
  local copies, waits for them, and re-layouts  9.51 us (5%)
  other arithmetic  4.4 us (2%)
    all_to_all x4, starting transfers between devices, along_z(): lax.all_to_all(value, 'fsdp', split_axis=0, concat_axis=0, tiled=True, ax...  44.3 us
    all_to_all x2, waiting for transfers between devices, over_chip_planes(): lax.all_to_all(value, ('fsdp', 'tensor'), split_axis=0, concat_axis=0, ti...  32.6 us
    all_to_all x2, starting transfers between devices, over_chip_planes(): lax.all_to_all(value, ('fsdp', 'tensor'), split_axis=0, concat_axis=0, ti...  18.4 us
    ppermute x6, starting transfers between devices, along_y(): return lax.ppermute(value, 'tensor', pairs)  15.8 us
    all_to_all x4, waiting for transfers between devices, along_z(): lax.all_to_all(value, 'fsdp', split_axis=0, concat_axis=0, tiled=True, ax...  11 us
    ppermute x3, starting transfers between devices, along_x(): return lax.ppermute(value, 'tensor', pairs)  9.92 us
    unnamed x26, local copies, waits for them, and re-layouts  8.75 us
    ppermute x6, waiting for transfers between devices, along_y(): return lax.ppermute(value, 'tensor', pairs)  8.33 us
  transfers between devices with their start and end apart: 15, of which 7 were waited for; matrix products, arithmetic and copies ran while one was open for 4% of the time, Pallas kernels for 3%

profile of v6, /device:TPU:1, one launch (start us, length us, event | category | flops | bytes accessed | tf_op | source)
XLA Modules:
  0.0 178.2 jit_solution(17466934109890524704)
XLA Ops:
  0.7 0.9 copy-done.9
  1.6 0.7 gradient_spread.1
  2.3 15.7 %all-to-all-start = ((bf16[16,2,16,128]{3,2,1,0:T(8,128)(2,1)}), bf16[16,2,16,128]{3,2,1,0:T(8,128)(2,1)S(1)}, u32[]{:S(2)}, u32[]{:S(2)}) async-start(bf16[16,2,16,128]{3,2,1,0:T(8,128)(2,1)} %gradient_spread.1), calls=%async_computation | async-start | bytes 262144 | tf_op jit(solution)/shard_map/gradient_spread/all_to_all | solution.py:334
  18.1 0.1 pad_add_fusion.place_ref
  18.2 1.0 copy-done.4
  19.2 0.7 roots_to_slot_groups.1
  19.9 1.2 fusion.9
  21.1 3.2 %collective-permute-start = (bf16[2,64,1024]{2,1,0:T(8,128)(2,1)S(1)}, bf16[2,64,1024]{2,1,0:T(8,128)(2,1)S(1)}, u32[]{:S(2)}, u32[]{:S(2)}) collective-permute-start(bf16[2,64,1024]{2,1,0:T(8,128)(2,1)S(1)} %get-tuple-element.82), channel_id=1, source_target_pairs={{0,4},{1,5},{2,6},{3,7},{4,8},{5,9},{6,10},{7,11},{12,0},{13,1},{1... | collective-permute-start | bytes 786440 | tf_op jit(solution)/shard_map/roots_to_slot_groups/ppermute | solution.py:322
  24.3 2.9 %collective-permute-start.1 = (bf16[2,64,1024]{2,1,0:T(8,128)(2,1)S(1)}, bf16[2,64,1024]{2,1,0:T(8,128)(2,1)S(1)}, u32[]{:S(2)}, u32[]{:S(2)}) collective-permute-start(bf16[2,64,1024]{2,1,0:T(8,128)(2,1)S(1)} %get-tuple-element.83), channel_id=1, source_target_pairs={{0,8},{1,9},{2,10},{3,11},{8,0},{9,1},{10,2},{11,3},{12,4},{13,5},... | collective-permute-start | bytes 786440 | tf_op jit(solution)/shard_map/roots_to_slot_groups/ppermute | solution.py:322
  27.2 1.3 collective-permute-start.2
  28.6 0.1 reshape.235
  28.7 0.2 select_reduce_fusion.2
  28.9 0.1 select_reduce_fusion.index_ref
  29.0 1.0 all-to-all-done
  30.0 1.4 gradient_to_owners.1
  31.4 10.4 %all-to-all-start.1 = ((bf16[16,6,16,128]{3,2,1,0:T(8,128)(2,1)}), bf16[16,6,16,128]{3,2,1,0:T(8,128)(2,1)S(1)}, u32[]{:S(2)}, u32[]{:S(2)}) async-start(bf16[16,6,16,128]{3,2,1,0:T(8,128)(2,1)} %bitcast.4), calls=%async_computation.1 | async-start | bytes 786432 | tf_op jit(solution)/shard_map/gradient_to_owners/all_to_all | solution.py:334
  41.8 0.0 collective-permute-done.1
  41.8 0.0 collective-permute-done.2
  41.9 0.1 pad_maximum_fusion.1.own_ref
  42.0 3.1 %collective-permute-start.3 = (bf16[4,64,768]{2,1,0:T(8,128)(2,1)S(1)}, bf16[4,64,768]{2,1,0:T(8,128)(2,1)S(1)}, u32[]{:S(2)}, u32[]{:S(2)}) collective-permute-start(bf16[4,64,768]{2,1,0:T(8,128)(2,1)S(1)} %pad_maximum_fusion.2), channel_id=1, source_target_pairs={{0,1},{1,2},{2,3},{3,0},{4,5},{5,6},{6,7},{7,4},{8,9},{9,10},{10,1... | collective-permute-start | bytes 1179656 | tf_op jit(solution)/shard_map/roots_to_slot_groups/ppermute | solution.py:328
  45.2 3.4 %collective-permute-start.4 = (bf16[4,64,512]{2,1,0:T(8,128)(2,1)S(1)}, bf16[4,64,512]{2,1,0:T(8,128)(2,1)S(1)}, u32[]{:S(2)}, u32[]{:S(2)}) collective-permute-start(bf16[4,64,512]{2,1,0:T(8,128)(2,1)S(1)} %get-tuple-element.85), channel_id=1, source_target_pairs={{0,3},{1,0},{2,1},{3,2},{4,7},{5,4},{6,5},{7,6},{8,11},{9,8},{10,9... | collective-permute-start | bytes 786440 | tf_op jit(solution)/shard_map/roots_to_slot_groups/ppermute | solution.py:328
  48.6 0.7 fusion.23.column_ref
  49.3 3.4 %collective-permute-start.5 = (bf16[4,64,256]{2,1,0:T(8,128)(2,1)S(1)}, bf16[4,64,256]{2,1,0:T(8,128)(2,1)S(1)}, u32[]{:S(2)}, u32[]{:S(2)}) collective-permute-start(bf16[4,64,256]{2,1,0:T(8,128)(2,1)S(1)} %slice.61), channel_id=1, source_target_pairs={{0,2},{1,3},{2,0},{3,1},{4,6},{5,7},{6,4},{7,5},{8,10},{9,11},{10,... | collective-permute-start | bytes 393224 | tf_op jit(solution)/shard_map/roots_to_slot_groups/ppermute | solution.py:328
  52.7 0.2 compare_reduce_fusion
  52.9 0.6 convert_element_type.9.used_ref
  53.5 0.1 pad_maximum_fusion.right_ref
  53.5 4.7 %collective-permute-done.5.far_ref = bf16[4,64,256]{2,1,0:T(8,128)(2,1)S(1)} collective-permute-done((bf16[4,64,256]{2,1,0:T(8,128)(2,1)S(1)}, bf16[4,64,256]{2,1,0:T(8,128)(2,1)S(1)}, u32[]{:S(2)}, u32[]{:S(2)}) %collective-permute-start.5) | collective-permute-done | bytes 131104 | tf_op jit(solution)/shard_map/roots_to_slot_groups/ppermute | solution.py:328
  58.2 0.7 copy-done.7
  58.9 0.7 copy-done.5
  59.6 0.7 copy-done.11
  60.3 2.7 %rows_of_held_blocks.2 = bf16[32,64,512]{2,1,0:T(8,128)(2,1)} custom-call(s32[6]{0:T(128)} %fusion.23.column_ref, s32[6]{0:T(128)} %convert_element_type.9.used_ref, bf16[16,6,16,128]{3,2,1,0:T(8,128)(2,1)} %copy-done.11), custom_call_target="tpu_custom_call" | custom-call | bytes 4194304 | tf_op jit(solution)/shard_map/rows_of_held_blocks/pallas_call | solution.py:94
  63.0 13.9 %all-to-all-start.2 = ((bf16[32,64,512]{2,1,0:T(8,128)(2,1)}), bf16[32,64,512]{2,1,0:T(8,128)(2,1)S(1)}, u32[]{:S(2)}, u32[]{:S(2)}) async-start(bf16[32,64,512]{2,1,0:T(8,128)(2,1)} %rows_of_held_blocks.2), calls=%async_computation.2 | async-start | bytes 4194304 | tf_op jit(solution)/shard_map/rows_of_held_blocks/all_to_all | solution.py:341
  77.0 0.0 copy-start.6
  77.0 0.9 copy-done.6
  78.0 0.9 copy-done.8
  78.9 1.7 rows_of_held_blocks.3
  80.6 1.3 copy-done
  81.9 23.4 %all-to-all-done.2.block_ref = bf16[32,64,512]{2,1,0:T(8,128)(2,1)S(1)} async-done(((bf16[32,64,512]{2,1,0:T(8,128)(2,1)}), bf16[32,64,512]{2,1,0:T(8,128)(2,1)S(1)}, u32[]{:S(2)}, u32[]{:S(2)}) %all-to-all-start.2) | async-done | bytes 2097184 | tf_op jit(solution)/shard_map/rows_of_held_blocks/all_to_all | solution.py:341
  105.3 1.6 copy-done.1
  106.9 3.7 %precondition.1 = bf16[32,80,128]{2,1,0:T(8,128)(2,1)} custom-call(s32[2]{0:T(128)S(1)} %pad_add_fusion.place_ref, bf16[16,64,1024]{2,1,0:T(8,128)(2,1)S(1)} %bitcast.40, bf16[4,64,1024]{2,1,0:T(8,128)(2,1)S(1)} %pad_maximum_fusion.right_ref, bf16[32,64,512]{2,1,0:T(8,128)(2,1)S(1)} %all-to-all-done.2.block_ref), custom_call_target="tpu_custom_call" | custom-call | flops 2684354560 | bytes 6291456 | tf_op jit(solution)/shard_map/precondition/pallas_call | solution.py:238
  110.7 4.5 %all-to-all-start.3 = ((bf16[32,80,128]{2,1,0:T(8,128)(2,1)}), bf16[32,80,128]{2,1,0:T(8,128)(2,1)S(1)}, u32[]{:S(2)}, u32[]{:S(2)}) async-start(bf16[32,80,128]{2,1,0:T(8,128)(2,1)} %precondition.1), calls=%async_computation.3 | async-start | bytes 1310720 | tf_op jit(solution)/shard_map/step_to_gradient_rows/all_to_all | solution.py:341
  115.2 0.1 step_to_gradient_rows.2
  115.3 0.4 constant_dynamic-slice_fusion.3
  115.7 0.8 convolution_convert_fusion
  116.6 0.7 convolution_convert_fusion.1
  117.3 0.0 copy-start.2
  117.3 0.0 copy-start.3
  117.4 0.9 fusion.15
  118.3 9.2 %all-to-all-done.3.back_ref = bf16[32,80,128]{2,1,0:T(8,128)(2,1)S(1)} async-done(((bf16[32,80,128]{2,1,0:T(8,128)(2,1)}), bf16[32,80,128]{2,1,0:T(8,128)(2,1)S(1)}, u32[]{:S(2)}, u32[]{:S(2)}) %all-to-all-start.3) | async-done | bytes 655392 | tf_op jit(solution)/shard_map/step_to_gradient_rows/all_to_all | solution.py:341
  127.5 1.6 step_to_gradient_rows.3
  129.1 5.7 %all-to-all-start.4 = ((bf16[16,6,16,128]{3,2,1,0:T(8,128)(2,1)}), bf16[16,6,16,128]{3,2,1,0:T(8,128)(2,1)S(1)}, u32[]{:S(2)}, u32[]{:S(2)}) async-start(bf16[16,6,16,128]{3,2,1,0:T(8,128)(2,1)} %step_to_gradient_rows.3), calls=%async_computation.4 | async-start | bytes 786432 | tf_op jit(solution)/shard_map/step_to_gradient_rows/all_to_all | solution.py:334
  134.8 2.0 %collective-permute-start.6 = (bf16[2,64,1024]{2,1,0:T(8,128)(2,1)}, bf16[2,64,1024]{2,1,0:T(8,128)(2,1)S(1)}, u32[]{:S(2)}, u32[]{:S(2)}) collective-permute-start(bf16[2,64,1024]{2,1,0:T(8,128)(2,1)} %get-tuple-element.60), channel_id=1, source_target_pairs={{0,4},{1,5},{2,6},{3,7},{4,8},{5,9},{6,10},{7,11},{8,12},{9,13},{1... | collective-permute-start | bytes 786440 | tf_op jit(solution)/shard_map/statistics/ppermute | solution.py:322
  136.9 4.4 %collective-permute-start.7 = (bf16[2,64,1024]{2,1,0:T(8,128)(2,1)}, bf16[2,64,1024]{2,1,0:T(8,128)(2,1)S(1)}, u32[]{:S(2)}, u32[]{:S(2)}) collective-permute-start(bf16[2,64,1024]{2,1,0:T(8,128)(2,1)} %get-tuple-element.61), channel_id=1, source_target_pairs={{0,8},{1,9},{2,10},{3,11},{4,12},{5,13},{6,14},{7,15},{8,0},{9,1},... | collective-permute-start | bytes 786440 | tf_op jit(solution)/shard_map/statistics/ppermute | solution.py:322
  141.3 1.9 %collective-permute-start.8 = (bf16[2,64,1024]{2,1,0:T(8,128)(2,1)}, bf16[2,64,1024]{2,1,0:T(8,128)(2,1)S(1)}, u32[]{:S(2)}, u32[]{:S(2)}) collective-permute-start(bf16[2,64,1024]{2,1,0:T(8,128)(2,1)} %get-tuple-element.62), channel_id=1, source_target_pairs={{0,12},{1,13},{2,14},{3,15},{4,0},{5,1},{6,2},{7,3},{8,4},{9,5},{1... | collective-permute-start | bytes 786440 | tf_op jit(solution)/shard_map/statistics/ppermute | solution.py:322
  143.2 0.1 multiply_add_fusion
  143.3 0.1 add.240
  143.4 0.2 select_reduce_fusion.1.index_ref
  143.5 8.0 %collective-permute-done.7.refs_2_ = bf16[2,64,1024]{2,1,0:T(8,128)(2,1)S(1)} collective-permute-done((bf16[2,64,1024]{2,1,0:T(8,128)(2,1)}, bf16[2,64,1024]{2,1,0:T(8,128)(2,1)S(1)}, u32[]{:S(2)}, u32[]{:S(2)}) %collective-permute-start.7) | collective-permute-done | bytes 262176 | tf_op jit(solution)/shard_map/statistics/ppermute | solution.py:322
  151.5 0.3 collective-permute-done.8.refs_3_
  151.9 1.2 statistics.2
  153.1 12.5 %all-to-all-start.5 = ((bf16[16,2,16,128]{3,2,1,0:T(8,128)(2,1)}), bf16[16,2,16,128]{3,2,1,0:T(8,128)(2,1)S(1)}, u32[]{:S(2)}, u32[]{:S(2)}) async-start(bf16[16,2,16,128]{3,2,1,0:T(8,128)(2,1)} %bitcast.24), calls=%async_computation.5 | async-start | bytes 262144 | tf_op jit(solution)/shard_map/statistics/all_to_all | solution.py:334
  165.6 1.9 %statistics.3 = (f32[3,64,1024]{2,1,0:T(8,128)}, f32[3,64,1024]{2,1,0:T(8,128)}) custom-call(s32[2]{0:T(128)S(1)} %pad_add_fusion.place_ref, f32[3,64,1024]{2,1,0:T(8,128)S(1)} %copy-done.2, f32[3,64,1024]{2,1,0:T(8,128)S(1)} %copy-done.3, bf16[2,64,1024]{2,1,0:T(8,128)(2,1)S(1)} %get-tuple-element.64.refs_0_, ...), custom_call_target="tpu_custom_call" | custom-call | bytes 4194304 | tf_op jit(solution)/shard_map/statistics/pallas_call | solution.py:492
  167.5 10.0 %all-to-all-done.5.tiles_ref = bf16[16,2,16,128]{3,2,1,0:T(8,128)(2,1)S(1)} async-done(((bf16[16,2,16,128]{3,2,1,0:T(8,128)(2,1)}), bf16[16,2,16,128]{3,2,1,0:T(8,128)(2,1)S(1)}, u32[]{:S(2)}, u32[]{:S(2)}) %all-to-all-start.5) | async-done | bytes 131104 | tf_op jit(solution)/shard_map/statistics/all_to_all | solution.py:334
  177.6 0.7 update.1
  (34 shorter events, 0.3 us)
Async XLA Ops:
  0.6 27.9 %copy-start.12 = (s32[4,8]{1,0:T(4,128)S(1)}, s32[4,8]{1,0:T(4,128)}, u32[]{:S(2)}) copy-start(s32[4,8]{1,0:T(4,128)} %param.7) | copy-start | bytes 388
  0.7 0.9 copy-start.9
  2.3 27.8 %all-to-all-start = ((bf16[16,2,16,128]{3,2,1,0:T(8,128)(2,1)}), bf16[16,2,16,128]{3,2,1,0:T(8,128)(2,1)S(1)}, u32[]{:S(2)}, u32[]{:S(2)}) async-start(bf16[16,2,16,128]{3,2,1,0:T(8,128)(2,1)} %gradient_spread.1), calls=%async_computation | async-start | bytes 262144 | tf_op jit(solution)/shard_map/gradient_spread/all_to_all | solution.py:334
  18.2 1.0 copy-start.4
  21.1 20.6 %collective-permute-start = (bf16[2,64,1024]{2,1,0:T(8,128)(2,1)S(1)}, bf16[2,64,1024]{2,1,0:T(8,128)(2,1)S(1)}, u32[]{:S(2)}, u32[]{:S(2)}) collective-permute-start(bf16[2,64,1024]{2,1,0:T(8,128)(2,1)S(1)} %get-tuple-element.82), channel_id=1, source_target_pairs={{0,4},{1,5},{2,6},{3,7},{4,8},{5,9},{6,10},{7,11},{12,0},{13,1},{1... | collective-permute-start | bytes 786440 | tf_op jit(solution)/shard_map/roots_to_slot_groups/ppermute | solution.py:322
  24.3 17.5 %collective-permute-start.1 = (bf16[2,64,1024]{2,1,0:T(8,128)(2,1)S(1)}, bf16[2,64,1024]{2,1,0:T(8,128)(2,1)S(1)}, u32[]{:S(2)}, u32[]{:S(2)}) collective-permute-start(bf16[2,64,1024]{2,1,0:T(8,128)(2,1)S(1)} %get-tuple-element.83), channel_id=1, source_target_pairs={{0,8},{1,9},{2,10},{3,11},{8,0},{9,1},{10,2},{11,3},{12,4},{13,5},... | collective-permute-start | bytes 786440 | tf_op jit(solution)/shard_map/roots_to_slot_groups/ppermute | solution.py:322
  27.2 14.6 %collective-permute-start.2 = (bf16[2,64,1024]{2,1,0:T(8,128)(2,1)S(1)}, bf16[2,64,1024]{2,1,0:T(8,128)(2,1)S(1)}, u32[]{:S(2)}, u32[]{:S(2)}) collective-permute-start(bf16[2,64,1024]{2,1,0:T(8,128)(2,1)S(1)} %get-tuple-element.84), channel_id=1, source_target_pairs={{4,0},{5,1},{6,2},{7,3},{8,4},{9,5},{10,6},{11,7},{12,8},{13,9},{1... | collective-permute-start | bytes 786440 | tf_op jit(solution)/shard_map/roots_to_slot_groups/ppermute | solution.py:322
  31.4 28.2 %all-to-all-start.1 = ((bf16[16,6,16,128]{3,2,1,0:T(8,128)(2,1)}), bf16[16,6,16,128]{3,2,1,0:T(8,128)(2,1)S(1)}, u32[]{:S(2)}, u32[]{:S(2)}) async-start(bf16[16,6,16,128]{3,2,1,0:T(8,128)(2,1)} %bitcast.4), calls=%async_computation.1 | async-start | bytes 786432 | tf_op jit(solution)/shard_map/gradient_to_owners/all_to_all | solution.py:334
  42.0 17.5 %collective-permute-start.3 = (bf16[4,64,768]{2,1,0:T(8,128)(2,1)S(1)}, bf16[4,64,768]{2,1,0:T(8,128)(2,1)S(1)}, u32[]{:S(2)}, u32[]{:S(2)}) collective-permute-start(bf16[4,64,768]{2,1,0:T(8,128)(2,1)S(1)} %pad_maximum_fusion.2), channel_id=1, source_target_pairs={{0,1},{1,2},{2,3},{3,0},{4,5},{5,6},{6,7},{7,4},{8,9},{9,10},{10,1... | collective-permute-start | bytes 1179656 | tf_op jit(solution)/shard_map/roots_to_slot_groups/ppermute | solution.py:328
  45.2 13.7 %collective-permute-start.4 = (bf16[4,64,512]{2,1,0:T(8,128)(2,1)S(1)}, bf16[4,64,512]{2,1,0:T(8,128)(2,1)S(1)}, u32[]{:S(2)}, u32[]{:S(2)}) collective-permute-start(bf16[4,64,512]{2,1,0:T(8,128)(2,1)S(1)} %get-tuple-element.85), channel_id=1, source_target_pairs={{0,3},{1,0},{2,1},{3,2},{4,7},{5,4},{6,5},{7,6},{8,11},{9,8},{10,9... | collective-permute-start | bytes 786440 | tf_op jit(solution)/shard_map/roots_to_slot_groups/ppermute | solution.py:328
  49.3 9.0 %collective-permute-start.5 = (bf16[4,64,256]{2,1,0:T(8,128)(2,1)S(1)}, bf16[4,64,256]{2,1,0:T(8,128)(2,1)S(1)}, u32[]{:S(2)}, u32[]{:S(2)}) collective-permute-start(bf16[4,64,256]{2,1,0:T(8,128)(2,1)S(1)} %slice.61), channel_id=1, source_target_pairs={{0,2},{1,3},{2,0},{3,1},{4,6},{5,7},{6,4},{7,5},{8,10},{9,11},{10,... | collective-permute-start | bytes 393224 | tf_op jit(solution)/shard_map/roots_to_slot_groups/ppermute | solution.py:328
  58.2 0.7 copy-start.7
  58.9 0.7 copy-start.5
  59.6 0.7 copy-start.11
  63.0 42.3 %all-to-all-start.2 = ((bf16[32,64,512]{2,1,0:T(8,128)(2,1)}), bf16[32,64,512]{2,1,0:T(8,128)(2,1)S(1)}, u32[]{:S(2)}, u32[]{:S(2)}) async-start(bf16[32,64,512]{2,1,0:T(8,128)(2,1)} %rows_of_held_blocks.2), calls=%async_computation.2 | async-start | bytes 4194304 | tf_op jit(solution)/shard_map/rows_of_held_blocks/all_to_all | solution.py:341
  77.0 1.0 copy-start.6
  78.0 0.9 copy-start.8
  80.6 1.3 copy-start
  105.3 1.6 copy-start.1
  110.7 16.8 %all-to-all-start.3 = ((bf16[32,80,128]{2,1,0:T(8,128)(2,1)}), bf16[32,80,128]{2,1,0:T(8,128)(2,1)S(1)}, u32[]{:S(2)}, u32[]{:S(2)}) async-start(bf16[32,80,128]{2,1,0:T(8,128)(2,1)} %precondition.1), calls=%async_computation.3 | async-start | bytes 1310720 | tf_op jit(solution)/shard_map/step_to_gradient_rows/all_to_all | solution.py:341
  116.6 10.9 %copy-start.10 = (s32[6]{0:T(128)S(1)}, s32[6]{0:T(128)}, u32[]{:S(2)}) copy-start(s32[6]{0:T(128)} %fusion.23.column_ref) | copy-start | bytes 76
  117.3 48.2 %copy-start.2 = (f32[3,64,1024]{2,1,0:T(8,128)S(1)}, f32[3,64,1024]{2,1,0:T(8,128)}, u32[]{:S(2)}) copy-start(f32[3,64,1024]{2,1,0:T(8,128)} %left_ref.1) | copy-start | bytes 2359300
  117.3 48.2 %copy-start.3 = (f32[3,64,1024]{2,1,0:T(8,128)S(1)}, f32[3,64,1024]{2,1,0:T(8,128)}, u32[]{:S(2)}) copy-start(f32[3,64,1024]{2,1,0:T(8,128)} %right_ref.1) | copy-start | bytes 2359300
  129.1 22.8 %all-to-all-start.4 = ((bf16[16,6,16,128]{3,2,1,0:T(8,128)(2,1)}), bf16[16,6,16,128]{3,2,1,0:T(8,128)(2,1)S(1)}, u32[]{:S(2)}, u32[]{:S(2)}) async-start(bf16[16,6,16,128]{3,2,1,0:T(8,128)(2,1)} %step_to_gradient_rows.3), calls=%async_computation.4 | async-start | bytes 786432 | tf_op jit(solution)/shard_map/step_to_gradient_rows/all_to_all | solution.py:334
  134.8 8.7 %collective-permute-start.6 = (bf16[2,64,1024]{2,1,0:T(8,128)(2,1)}, bf16[2,64,1024]{2,1,0:T(8,128)(2,1)S(1)}, u32[]{:S(2)}, u32[]{:S(2)}) collective-permute-start(bf16[2,64,1024]{2,1,0:T(8,128)(2,1)} %get-tuple-element.60), channel_id=1, source_target_pairs={{0,4},{1,5},{2,6},{3,7},{4,8},{5,9},{6,10},{7,11},{8,12},{9,13},{1... | collective-permute-start | bytes 786440 | tf_op jit(solution)/shard_map/statistics/ppermute | solution.py:322
  136.9 14.7 %collective-permute-start.7 = (bf16[2,64,1024]{2,1,0:T(8,128)(2,1)}, bf16[2,64,1024]{2,1,0:T(8,128)(2,1)S(1)}, u32[]{:S(2)}, u32[]{:S(2)}) collective-permute-start(bf16[2,64,1024]{2,1,0:T(8,128)(2,1)} %get-tuple-element.61), channel_id=1, source_target_pairs={{0,8},{1,9},{2,10},{3,11},{4,12},{5,13},{6,14},{7,15},{8,0},{9,1},... | collective-permute-start | bytes 786440 | tf_op jit(solution)/shard_map/statistics/ppermute | solution.py:322
  141.3 10.6 %collective-permute-start.8 = (bf16[2,64,1024]{2,1,0:T(8,128)(2,1)}, bf16[2,64,1024]{2,1,0:T(8,128)(2,1)S(1)}, u32[]{:S(2)}, u32[]{:S(2)}) collective-permute-start(bf16[2,64,1024]{2,1,0:T(8,128)(2,1)} %get-tuple-element.62), channel_id=1, source_target_pairs={{0,12},{1,13},{2,14},{3,15},{4,0},{5,1},{6,2},{7,3},{8,4},{9,5},{1... | collective-permute-start | bytes 786440 | tf_op jit(solution)/shard_map/statistics/ppermute | solution.py:322
  153.1 24.5 %all-to-all-start.5 = ((bf16[16,2,16,128]{3,2,1,0:T(8,128)(2,1)}), bf16[16,2,16,128]{3,2,1,0:T(8,128)(2,1)S(1)}, u32[]{:S(2)}, u32[]{:S(2)}) async-start(bf16[16,2,16,128]{3,2,1,0:T(8,128)(2,1)} %bitcast.24), calls=%async_computation.5 | async-start | bytes 262144 | tf_op jit(solution)/shard_map/statistics/all_to_all | solution.py:334
